TPU v7x, 32 devices: a whole 2x2x4 slice. The times are simulated.
32 devices in a mesh: row: 16 (over z, y, core), col: 2 (over x).
Axes of the slice: x: 2, y: 2, z: 4, core: 2. Of those that a mesh axis runs over, the one named last changes fastest.
Arguments:
- left_slots: float32 [16, 1024, 512], P('row', 'col'), may hold values from -0.15625 to 0.15625
- right: float32 [2048, 4096], P('col', 'row'), may hold values from -6 to 6
- previous: float32 [1024, 4096], P('col', 'row'), may hold values from -4 to 4
- offsets: int32 [3], replicated, may hold values from 0 to 3, as said below
- owners: int32 [2, 3], P('col'), may hold values from 0 to 15, as said below
Outputs:
- next_density: float32 [1024, 4096], P('col', 'row')
Inputs may be any that keep to these rules, and one draw needn't show every extreme that they name: `offsets`: distinct, in any order; they include 0 and 3. `owners`: distinct within each grid row.
All inputs are finite; a program needn't handle non-finite values.
Results may differ from a plain program's by a relative error of at most 0.0001.
Values sent between devices are 32-bit elements; how exact they have to be, the bound alone decides.
No kernel may reach another device: no remote copies, remote signals or barrier semaphores. Data moves between devices by JAX's collectives and lax.ppermute only.
A program may use at most 64 MiB of HBM per device.

v0:
```python
import functools

import jax
import jax.numpy as jnp
from jax import lax
from jax.experimental import pallas as pl
from jax.experimental.pallas import tpu as pltpu
from jax.sharding import PartitionSpec as P

PARTS = 2
VMEM = pl.BlockSpec(memory_space=pltpu.VMEM)
SMEM = pl.BlockSpec(memory_space=pltpu.SMEM)
ANY = pl.BlockSpec(memory_space=pl.ANY)


def call(kernel, out_shape, in_specs, operands, flops=0):
    outs = out_shape if isinstance(out_shape, tuple) else (out_shape,)
    moved = sum(x.size * x.dtype.itemsize for x in (*operands, *outs))
    return pl.pallas_call(
        kernel,
        out_shape=out_shape,
        in_specs=in_specs,
        out_specs=jax.tree.map(lambda _: VMEM, out_shape),
        cost_estimate=pl.CostEstimate(flops=flops, bytes_accessed=moved, transcendentals=0),
        compiler_params=pltpu.CompilerParams(vmem_limit_bytes=32 * 1024 * 1024),
    )(*operands)


def split(value):
    high = value.astype(jnp.bfloat16)
    low = (value - high.astype(jnp.float32)).astype(jnp.bfloat16)
    return high, low


def dot(left, right):
    return jnp.dot(left, right, preferred_element_type=jnp.float32)


def gather_kernel(part, chips, own, got, *refs):
    outs = refs[-(chips - 1):]
    chunk = outs[0].shape[1]
    for step, out in enumerate(outs, 1):
        place = part * chips + step
        out[0] = own[2 * place * chunk:(2 * place + 1) * chunk, :]
        out[1] = got[place * chunk:(place + 1) * chunk, :]


def pick_kernel(part, chips, owners, own, got, *refs):
    pieces, out = refs[:-1], refs[-1]
    chunk = out.shape[1]
    member = lax.axis_index("row") % (2 * chips)
    first = part * chips
    near = [own[2 * first * chunk:(2 * first + 1) * chunk, :], got[first * chunk:(first + 1) * chunk, :]]
    for number in range(out.shape[0]):
        mask = (owners[0, number] % (2 * chips)) ^ member
        for core in range(2):

            @pl.when(mask == core)
            def _():
                out[number] = near[core]

            for step, piece in enumerate(pieces, 1):

                @pl.when(mask == 2 * step + core)
                def _():
                    out[number] = piece[core]


def merge_kernel(group, owners, mine, other, out):
    half = lax.axis_index("row") // group
    for number in range(out.shape[0]):
        here = owners[0, number] // group == half

        @pl.when(here)
        def _():
            out[number] = mine[number]

        @pl.when(jnp.logical_not(here))
        def _():
            out[number] = other[number]


def right_kernel(offsets, *refs):
    rights, (right_high, right_low) = refs[:-2], refs[-2:]
    count = offsets.shape[0]
    width = right_high.shape[0] // count
    blocks = rights[0].shape[0] // width
    for number in range(count):
        lanes = slice(number * width, (number + 1) * width)
        for step, ref in enumerate(rights):
            for block in range(blocks):

                @pl.when(offsets[number] == step * blocks + block)
                def _():
                    high, low = split(ref[block * width:(block + 1) * width, :])
                    right_high[lanes, :] = high
                    right_low[lanes, :] = low


def multiply_kernel(part, owners, right_high, right_low, previous, *refs):
    group = len(refs) - part - 3
    pieces, early = refs[:group], refs[group:group + part]
    out, left_high, left_low = refs[group + part:]
    count, chunk, width = pieces[0].shape
    member = lax.axis_index("row") % group
    size = group * chunk
    for number in range(count):
        mask = (owners[0, number] % group) ^ member
        lanes = slice(number * width, (number + 1) * width)
        for step in range(group):
            place = pl.multiple_of((mask ^ step) * chunk, chunk)
            high, low = split(pieces[step][number])
            left_high[pl.ds(place, chunk), lanes] = high
            left_low[pl.ds(place, chunk), lanes] = low
    total = 2.0 * previous[part * size:(part + 1) * size, :] - (
        dot(left_high[...], right_low[...])
        + dot(left_low[...], right_high[...])
        + dot(left_high[...], right_high[...])
    )
    if out.shape[0] > size:
        for number, ref in enumerate(early):
            out[number * size:(number + 1) * size, :] = ref[...]
        out[part * size:, :] = total
    else:
        out[...] = total


def shards(left_slots, right, previous, offsets, owners):
    own = left_slots[0]
    rows, width = own.shape
    count = offsets.shape[0]
    devices = lax.axis_size("row")
    columns = lax.axis_size("col")
    group = devices // 2
    chips = group // 2
    size = rows // PARTS
    chunk = size // group
    piece = jax.ShapeDtypeStruct((count, chunk, width), own.dtype)
    pair = jax.ShapeDtypeStruct((2, chunk, width), own.dtype)

    def swap(array, mask):
        return lax.ppermute(array, "row", [(i, i ^ mask) for i in range(devices)])

    def shift(array, distance):
        pairs = [((i + distance) % columns, i) for i in range(columns)]
        return lax.ppermute(array, "col", pairs)

    got = swap(own.reshape(rows // (2 * chunk), 2 * chunk, width)[:, chunk:].reshape(rows // 2, width), 1)
    mine = []
    wait = []
    for part in range(PARTS):
        sent = call(
            functools.partial(gather_kernel, part, chips),
            (pair,) * (chips - 1),
            [VMEM, VMEM] + [ANY] * len(wait),
            (own, got, *wait),
        )
        pieces = [swap(array, 2 * step) for step, array in enumerate(sent, 1)]
        wait = pieces[-1:]
        mine.append(call(
            functools.partial(pick_kernel, part, chips),
            piece,
            [SMEM] + [VMEM] * (2 + len(pieces)),
            (owners, own, got, *pieces),
        ))

    rights = [right] + [shift(right, distance) for distance in range(1, columns)]
    terms = jax.ShapeDtypeStruct((count * width, right.shape[1]), jnp.bfloat16)
    right_terms = call(
        right_kernel, (terms, terms), [SMEM] + [VMEM] * columns, (offsets, *rights), flops=4 * terms.size
    )

    results = []
    for part in range(PARTS):
        merged = call(
            functools.partial(merge_kernel, group),
            piece,
            [SMEM, VMEM, VMEM],
            (owners, mine[part], swap(mine[part], group)),
        )
        pieces = {0: merged}
        step = chips
        while step > 1:
            for s in list(pieces):
                pieces[s + step] = swap(pieces[s], step)
            step //= 2
        for s in list(pieces):
            pieces[s + 1] = swap(pieces[s], 1)
        last = part == PARTS - 1
        operands = (owners, *right_terms, previous, *[pieces[s] for s in range(group)], *results)
        out_shape = jax.ShapeDtypeStruct((rows if last else size, right.shape[1]), previous.dtype)
        moved = sum(x.size * x.dtype.itemsize for x in operands)
        results.append(pl.pallas_call(
            functools.partial(multiply_kernel, part),
            out_shape=out_shape,
            in_specs=[SMEM] + [VMEM] * (len(operands) - 1),
            out_specs=VMEM,
            scratch_shapes=[pltpu.VMEM((size, count * width), jnp.bfloat16)] * 2,
            cost_estimate=pl.CostEstimate(
                flops=6 * size * count * width * right.shape[1], bytes_accessed=moved, transcendentals=0
            ),
            compiler_params=pltpu.CompilerParams(vmem_limit_bytes=32 * 1024 * 1024),
        )(*operands))
    return results[-1]


def solution(mesh):
    return jax.shard_map(
        shards,
        mesh=mesh,
        in_specs=(P("row", "col", None), P("col", "row"), P("col", "row"), P(), P("col", None)),
        out_specs=P("col", "row"),
        check_vma=False,
    )
```

profile of v0, /device:TPU:0, one launch (start us, length us, event | category | flops | bytes accessed | tf_op | source)
XLA Modules:
  0.0 60.2 jit_solution(5190656303463803885)
XLA Ops:
  0.0 1.2 %slice.4 = f32[8,32,512]{2,1,0:T(8,128)S(1)} slice(f32[8,64,512]{2,1,0:T(8,128)} %bitcast.3), slice={[0:8], [32:64], [0:512]} | slice | bytes 1048576 | tf_op jit(solution)/shard_map/slice | solution.py:148
  1.2 0.5 collective-permute-start.1
  1.7 2.6 %collective-permute-start = (f32[1024,256]{1,0:T(8,128)}, f32[1024,256]{1,0:T(8,128)S(1)}, u32[]{:S(2)}, u32[]{:S(2)}) collective-permute-start(f32[1024,256]{1,0:T(8,128)} %refs_0_.1), channel_id=1, source_target_pairs={{1,0},{0,1},{3,2},{2,3},{5,4},{4,5},{7,6},{6,7},{9,8},{8,9},{11,10... | collective-permute-start | bytes 3145736 | tf_op jit(solution)/shard_map/ppermute | solution.py:146
  4.3 0.0 collective-permute-done.1.got
  4.3 0.0 copy-done
  4.3 2.9 %collective-permute-start.2 = (f32[2,32,512]{2,1,0:T(8,128)S(1)}, f32[2,32,512]{2,1,0:T(8,128)S(1)}, u32[]{:S(2)}, u32[]{:S(2)}) collective-permute-start(f32[2,32,512]{2,1,0:T(8,128)S(1)} %get-tuple-element.15), channel_id=1, source_target_pairs={{0,12},{2,14},{4,8},{6,10},{8,4},{10,6},{12,0},{14,2},{16,28},{18,... | collective-permute-start | bytes 393224 | tf_op jit(solution)/shard_map/ppermute | solution.py:142
  7.2 0.5 collective-permute-start.14
  7.7 0.1 collective-permute-start.15
  7.9 3.3 %collective-permute-done.2.refs_0_.refs_2_ = f32[2,32,512]{2,1,0:T(8,128)S(1)} collective-permute-done((f32[2,32,512]{2,1,0:T(8,128)S(1)}, f32[2,32,512]{2,1,0:T(8,128)S(1)}, u32[]{:S(2)}, u32[]{:S(2)}) %collective-permute-start.2) | collective-permute-done | bytes 131104 | tf_op jit(solution)/shard_map/ppermute | solution.py:142
  11.2 2.4 %collective-permute-start.3 = (f32[2,32,512]{2,1,0:T(8,128)S(1)}, f32[2,32,512]{2,1,0:T(8,128)S(1)}, u32[]{:S(2)}, u32[]{:S(2)}) collective-permute-start(f32[2,32,512]{2,1,0:T(8,128)S(1)} %get-tuple-element.16), channel_id=1, source_target_pairs={{0,4},{2,6},{4,0},{6,2},{8,12},{10,14},{12,8},{14,10},{16,20},{18,... | collective-permute-start | bytes 393224 | tf_op jit(solution)/shard_map/ppermute | solution.py:142
  13.6 1.6 %collective-permute-start.4 = (f32[2,32,512]{2,1,0:T(8,128)S(1)}, f32[2,32,512]{2,1,0:T(8,128)S(1)}, u32[]{:S(2)}, u32[]{:S(2)}) collective-permute-start(f32[2,32,512]{2,1,0:T(8,128)S(1)} %get-tuple-element.17), channel_id=1, source_target_pairs={{0,8},{2,10},{4,12},{6,14},{8,0},{10,2},{12,4},{14,6},{16,24},{18,... | collective-permute-start | bytes 393224 | tf_op jit(solution)/shard_map/ppermute | solution.py:142
  15.2 0.0 collective-permute-done.14.refs_0_
  15.2 0.5 collective-permute-start.5
  15.7 0.0 collective-permute-done.15.refs_1_
  15.7 0.0 copy-done.3
  15.7 0.7 %shard_map.60.mine = f32[3,32,512]{2,1,0:T(8,128)S(1)} custom-call(s32[1,3]{1,0:T(1,128)S(1)} %copy-done.3, f32[512,512]{1,0:T(8,128)S(1)} %bitcast.6, f32[256,512]{1,0:T(8,128)S(1)} %collective-permute-done.1.got, f32[2,32,512]{2,1,0:T(8,128)S(1)} %collective-permute-done.14.refs_0_, f32[2,32,512]{2,1,0:T(8,128)S(1)} %collective-permute-done.15.refs_1_, ...), custom_call_target="tpu_custom_call" | custom-call | bytes 2162700 | tf_op jit(solution)/shard_map/pallas_call | solution.py:19
  16.4 2.7 %collective-permute-start.16 = (f32[3,32,512]{2,1,0:T(8,128)S(1)}, f32[3,32,512]{2,1,0:T(8,128)S(1)}, u32[]{:S(2)}, u32[]{:S(2)}) collective-permute-start(f32[3,32,512]{2,1,0:T(8,128)S(1)} %shard_map.60.mine), channel_id=1, source_target_pairs={{0,16},{2,18},{4,20},{6,22},{8,24},{10,26},{12,28},{14,30},{16,0},... | collective-permute-start | bytes 589832 | tf_op jit(solution)/shard_map/ppermute | solution.py:142
  19.0 0.0 collective-permute-done.3.refs_0_
  19.0 4.5 %collective-permute-done.4.refs_1_ = f32[2,32,512]{2,1,0:T(8,128)S(1)} collective-permute-done((f32[2,32,512]{2,1,0:T(8,128)S(1)}, f32[2,32,512]{2,1,0:T(8,128)S(1)}, u32[]{:S(2)}, u32[]{:S(2)}) %collective-permute-start.4) | collective-permute-done | bytes 131104 | tf_op jit(solution)/shard_map/ppermute | solution.py:142
  23.6 0.0 collective-permute-done.5.refs_2_
  23.6 0.7 %shard_map.58.mine = f32[3,32,512]{2,1,0:T(8,128)S(1)} custom-call(s32[1,3]{1,0:T(1,128)S(1)} %copy-done.3, f32[512,512]{1,0:T(8,128)S(1)} %bitcast.7, f32[256,512]{1,0:T(8,128)S(1)} %collective-permute-done.1.got, f32[2,32,512]{2,1,0:T(8,128)S(1)} %collective-permute-done.3.refs_0_, f32[2,32,512]{2,1,0:T(8,128)S(1)} %collective-permute-done.4.refs_1_, ...), custom_call_target="tpu_custom_call" | custom-call | bytes 2162700 | tf_op jit(solution)/shard_map/pallas_call | solution.py:19
  24.3 0.0 copy-start.2
  24.3 1.6 %collective-permute-start.6 = (f32[3,32,512]{2,1,0:T(8,128)S(1)}, f32[3,32,512]{2,1,0:T(8,128)S(1)}, u32[]{:S(2)}, u32[]{:S(2)}) collective-permute-start(f32[3,32,512]{2,1,0:T(8,128)S(1)} %shard_map.58.mine), channel_id=1, source_target_pairs={{0,16},{2,18},{4,20},{6,22},{8,24},{10,26},{12,28},{14,30},{16,0},... | collective-permute-start | bytes 589832 | tf_op jit(solution)/shard_map/ppermute | solution.py:142
  25.9 0.0 collective-permute-done.16.other
  25.9 0.6 %shard_map.61.refs_0_ = f32[3,32,512]{2,1,0:T(8,128)S(1)} custom-call(s32[1,3]{1,0:T(1,128)S(1)} %copy-done.3, f32[3,32,512]{2,1,0:T(8,128)S(1)} %shard_map.60.mine, f32[3,32,512]{2,1,0:T(8,128)S(1)} %collective-permute-done.16.other), custom_call_target="tpu_custom_call" | custom-call | bytes 589836 | tf_op jit(solution)/shard_map/pallas_call | solution.py:19
  26.5 0.0 copy-start.4
  26.5 7.5 %collective-permute-start.20 = (f32[3,32,512]{2,1,0:T(8,128)S(1)}, f32[3,32,512]{2,1,0:T(8,128)S(1)}, u32[]{:S(2)}, u32[]{:S(2)}) collective-permute-start(f32[3,32,512]{2,1,0:T(8,128)S(1)} %shard_map.61.refs_0_), channel_id=1, source_target_pairs={{0,8},{2,10},{4,12},{6,14},{8,0},{10,2},{12,4},{14,6},{16,24},{18,... | collective-permute-start | bytes 589832 | tf_op jit(solution)/shard_map/ppermute | solution.py:142
  34.0 1.9 %collective-permute-start.18 = (f32[3,32,512]{2,1,0:T(8,128)S(1)}, f32[3,32,512]{2,1,0:T(8,128)S(1)}, u32[]{:S(2)}, u32[]{:S(2)}) collective-permute-start(f32[3,32,512]{2,1,0:T(8,128)S(1)} %shard_map.61.refs_0_), channel_id=1, source_target_pairs={{0,4},{2,6},{4,0},{6,2},{8,12},{10,14},{12,8},{14,10},{16,20},{18,... | collective-permute-start | bytes 589832 | tf_op jit(solution)/shard_map/ppermute | solution.py:142
  35.8 0.0 collective-permute-start.17
  35.9 0.1 collective-permute-done.6.other
  36.0 0.6 %shard_map.59.refs_0_ = f32[3,32,512]{2,1,0:T(8,128)S(1)} custom-call(s32[1,3]{1,0:T(1,128)S(1)} %copy-done.3, f32[3,32,512]{2,1,0:T(8,128)S(1)} %shard_map.58.mine, f32[3,32,512]{2,1,0:T(8,128)S(1)} %collective-permute-done.6.other), custom_call_target="tpu_custom_call" | custom-call | bytes 589836 | tf_op jit(solution)/shard_map/pallas_call | solution.py:19
  36.6 0.0 copy-start.1
  36.6 1.7 %collective-permute-start.10 = (f32[3,32,512]{2,1,0:T(8,128)S(1)}, f32[3,32,512]{2,1,0:T(8,128)S(1)}, u32[]{:S(2)}, u32[]{:S(2)}) collective-permute-start(f32[3,32,512]{2,1,0:T(8,128)S(1)} %shard_map.59.refs_0_), channel_id=1, source_target_pairs={{0,8},{2,10},{4,12},{6,14},{8,0},{10,2},{12,4},{14,6},{16,24},{18,... | collective-permute-start | bytes 589832 | tf_op jit(solution)/shard_map/ppermute | solution.py:142
  38.3 1.9 %collective-permute-done.20.refs_4_ = f32[3,32,512]{2,1,0:T(8,128)S(1)} collective-permute-done((f32[3,32,512]{2,1,0:T(8,128)S(1)}, f32[3,32,512]{2,1,0:T(8,128)S(1)}, u32[]{:S(2)}, u32[]{:S(2)}) %collective-permute-start.20) | collective-permute-done | bytes 196640 | tf_op jit(solution)/shard_map/ppermute | solution.py:142
  40.2 3.2 %collective-permute-start.22 = (f32[3,32,512]{2,1,0:T(8,128)S(1)}, f32[3,32,512]{2,1,0:T(8,128)S(1)}, u32[]{:S(2)}, u32[]{:S(2)}) collective-permute-start(f32[3,32,512]{2,1,0:T(8,128)S(1)} %collective-permute-done.20.refs_4_), channel_id=1, source_target_pairs={{0,4},{2,6},{4,0},{6,2},{8,12},{10,14},{12,8},{14,10},{16,20},{18,... | collective-permute-start | bytes 589832 | tf_op jit(solution)/shard_map/ppermute | solution.py:142
  43.4 0.0 collective-permute-done.18.refs_2_
  43.4 0.0 collective-permute-start.8
  43.4 0.0 collective-permute-done.17.refs_1_
  43.4 0.0 collective-permute-start.21
  43.5 0.0 collective-permute-done.refs_1_
  43.5 0.5 collective-permute-start.19
  44.0 0.3 collective-permute-done.10.refs_4_
  44.3 2.0 %collective-permute-start.12 = (f32[3,32,512]{2,1,0:T(8,128)S(1)}, f32[3,32,512]{2,1,0:T(8,128)S(1)}, u32[]{:S(2)}, u32[]{:S(2)}) collective-permute-start(f32[3,32,512]{2,1,0:T(8,128)S(1)} %collective-permute-done.10.refs_4_), channel_id=1, source_target_pairs={{0,4},{2,6},{4,0},{6,2},{8,12},{10,14},{12,8},{14,10},{16,20},{18,... | collective-permute-start | bytes 589832 | tf_op jit(solution)/shard_map/ppermute | solution.py:142
  46.3 2.9 %collective-permute-done.22.refs_6_ = f32[3,32,512]{2,1,0:T(8,128)S(1)} collective-permute-done((f32[3,32,512]{2,1,0:T(8,128)S(1)}, f32[3,32,512]{2,1,0:T(8,128)S(1)}, u32[]{:S(2)}, u32[]{:S(2)}) %collective-permute-start.22) | collective-permute-done | bytes 196640 | tf_op jit(solution)/shard_map/ppermute | solution.py:142
  49.2 0.0 collective-permute-start.23
  49.2 4.0 %collective-permute-done.8.refs_2_ = f32[3,32,512]{2,1,0:T(8,128)S(1)} collective-permute-done((f32[3,32,512]{2,1,0:T(8,128)S(1)}, f32[3,32,512]{2,1,0:T(8,128)S(1)}, u32[]{:S(2)}, u32[]{:S(2)}) %collective-permute-start.8) | collective-permute-done | bytes 196640 | tf_op jit(solution)/shard_map/ppermute | solution.py:142
  53.2 0.0 collective-permute-start.7
  53.2 0.0 collective-permute-done.21.refs_5_
  53.2 0.5 collective-permute-start.11
  53.7 0.0 collective-permute-done.19.refs_3_
  53.7 0.1 collective-permute-start.9
  53.8 1.5 %collective-permute-done.12.refs_6_ = f32[3,32,512]{2,1,0:T(8,128)S(1)} collective-permute-done((f32[3,32,512]{2,1,0:T(8,128)S(1)}, f32[3,32,512]{2,1,0:T(8,128)S(1)}, u32[]{:S(2)}, u32[]{:S(2)}) %collective-permute-start.12) | collective-permute-done | bytes 196640 | tf_op jit(solution)/shard_map/ppermute | solution.py:142
  55.3 0.0 collective-permute-start.13
  55.3 0.0 copy-done.2
  55.3 0.0 copy-done.4
  55.3 0.9 %shard_map.55 = (bf16[1536,256]{1,0:T(8,128)(2,1)S(1)}, bf16[1536,256]{1,0:T(8,128)(2,1)S(1)}) custom-call(s32[3]{0:T(128)S(1)} %copy-done.4, f32[1024,256]{1,0:T(8,128)S(1)} %copy-done.2, f32[1024,256]{1,0:T(8,128)S(1)} %collective-permute-done.refs_1_), custom_call_target="tpu_custom_call" | custom-call | flops 1572864 | bytes 3670028 | tf_op jit(solution)/shard_map/pallas_call | solution.py:19
  56.2 0.0 collective-permute-done.23.refs_7_
  56.2 0.0 copy-done.1
  56.2 1.5 %shard_map.62.refs_8_ = f32[256,256]{1,0:T(8,128)S(1)} custom-call(s32[1,3]{1,0:T(1,128)S(1)} %copy-done.3, bf16[1536,256]{1,0:T(8,128)(2,1)S(1)} %get-tuple-element.13.right_high, bf16[1536,256]{1,0:T(8,128)(2,1)S(1)} %get-tuple-element.14.right_low, f32[512,256]{1,0:T(8,128)S(1)} %copy-done.1, f32[3,32,512]{2,1,0:T(8,128)S(1)} %shard_map.61.refs_0_, ...), custom_call_target="tpu_custom_call" | custom-call | flops 603979776 | bytes 3670028 | tf_op jit(solution)/shard_map/pallas_call | solution.py:193
  57.8 0.0 collective-permute-done.7.refs_1_
  57.8 0.0 collective-permute-done.11.refs_5_
  57.8 0.0 collective-permute-done.9.refs_3_
  57.8 0.0 collective-permute-done.13.refs_7_
  57.8 2.3 %shard_map.63 = f32[512,256]{1,0:T(8,128)} custom-call(s32[1,3]{1,0:T(1,128)S(1)} %copy-done.3, bf16[1536,256]{1,0:T(8,128)(2,1)S(1)} %get-tuple-element.13.right_high, bf16[1536,256]{1,0:T(8,128)(2,1)S(1)} %get-tuple-element.14.right_low, f32[512,256]{1,0:T(8,128)S(1)} %copy-done.1, f32[3,32,512]{2,1,0:T(8,128)S(1)} %shard_map.59.refs_0_, ...), custom_call_target="tpu_custom_call" | custom-call | flops 603979776 | bytes 3932172 | tf_op jit(solution)/shard_map/pallas_call | solution.py:193
  (4 shorter events, 0.1 us)
Async XLA Ops:
  0.0 4.3 %copy-start = (f32[1,512,512]{2,1,0:T(8,128)S(1)}, f32[1,512,512]{2,1,0:T(8,128)}, u32[]{:S(2)}) copy-start(f32[1,512,512]{2,1,0:T(8,128)} %param.5) | copy-start | bytes 3145732
  1.2 3.1 %collective-permute-start.1 = (f32[256,512]{1,0:T(8,128)S(1)}, f32[256,512]{1,0:T(8,128)S(1)}, u32[]{:S(2)}, u32[]{:S(2)}) collective-permute-start(f32[256,512]{1,0:T(8,128)S(1)} %bitcast.8), channel_id=1, source_target_pairs={{0,2},{2,0},{4,6},{6,4},{8,10},{10,8},{12,14},{14,12},{16,18},{18,... | collective-permute-start | bytes 1572872 | tf_op jit(solution)/shard_map/ppermute | solution.py:142
  1.7 41.8 %collective-permute-start = (f32[1024,256]{1,0:T(8,128)}, f32[1024,256]{1,0:T(8,128)S(1)}, u32[]{:S(2)}, u32[]{:S(2)}) collective-permute-start(f32[1024,256]{1,0:T(8,128)} %refs_0_.1), channel_id=1, source_target_pairs={{1,0},{0,1},{3,2},{2,3},{5,4},{4,5},{7,6},{6,7},{9,8},{8,9},{11,10... | collective-permute-start | bytes 3145736 | tf_op jit(solution)/shard_map/ppermute | solution.py:146
  4.3 6.8 %collective-permute-start.2 = (f32[2,32,512]{2,1,0:T(8,128)S(1)}, f32[2,32,512]{2,1,0:T(8,128)S(1)}, u32[]{:S(2)}, u32[]{:S(2)}) collective-permute-start(f32[2,32,512]{2,1,0:T(8,128)S(1)} %get-tuple-element.15), channel_id=1, source_target_pairs={{0,12},{2,14},{4,8},{6,10},{8,4},{10,6},{12,0},{14,2},{16,28},{18,... | collective-permute-start | bytes 393224 | tf_op jit(solution)/shard_map/ppermute | solution.py:142
  7.2 8.0 %collective-permute-start.14 = (f32[2,32,512]{2,1,0:T(8,128)S(1)}, f32[2,32,512]{2,1,0:T(8,128)S(1)}, u32[]{:S(2)}, u32[]{:S(2)}) collective-permute-start(f32[2,32,512]{2,1,0:T(8,128)S(1)} %get-tuple-element.19), channel_id=1, source_target_pairs={{0,4},{2,6},{4,0},{6,2},{8,12},{10,14},{12,8},{14,10},{16,20},{18,... | collective-permute-start | bytes 393224 | tf_op jit(solution)/shard_map/ppermute | solution.py:142
  7.7 7.9 %collective-permute-start.15 = (f32[2,32,512]{2,1,0:T(8,128)S(1)}, f32[2,32,512]{2,1,0:T(8,128)S(1)}, u32[]{:S(2)}, u32[]{:S(2)}) collective-permute-start(f32[2,32,512]{2,1,0:T(8,128)S(1)} %get-tuple-element.20), channel_id=1, source_target_pairs={{0,8},{2,10},{4,12},{6,14},{8,0},{10,2},{12,4},{14,6},{16,24},{18,... | collective-permute-start | bytes 393224 | tf_op jit(solution)/shard_map/ppermute | solution.py:142
  11.2 7.9 %collective-permute-start.3 = (f32[2,32,512]{2,1,0:T(8,128)S(1)}, f32[2,32,512]{2,1,0:T(8,128)S(1)}, u32[]{:S(2)}, u32[]{:S(2)}) collective-permute-start(f32[2,32,512]{2,1,0:T(8,128)S(1)} %get-tuple-element.16), channel_id=1, source_target_pairs={{0,4},{2,6},{4,0},{6,2},{8,12},{10,14},{12,8},{14,10},{16,20},{18,... | collective-permute-start | bytes 393224 | tf_op jit(solution)/shard_map/ppermute | solution.py:142
  13.6 2.1 %copy-start.3 = (s32[1,3]{1,0:T(1,128)S(1)}, s32[1,3]{1,0:T(1,128)}, u32[]{:S(2)}) copy-start(s32[1,3]{1,0:T(1,128)} %owners.11) | copy-start | bytes 40
  13.6 10.0 %collective-permute-start.4 = (f32[2,32,512]{2,1,0:T(8,128)S(1)}, f32[2,32,512]{2,1,0:T(8,128)S(1)}, u32[]{:S(2)}, u32[]{:S(2)}) collective-permute-start(f32[2,32,512]{2,1,0:T(8,128)S(1)} %get-tuple-element.17), channel_id=1, source_target_pairs={{0,8},{2,10},{4,12},{6,14},{8,0},{10,2},{12,4},{14,6},{16,24},{18,... | collective-permute-start | bytes 393224 | tf_op jit(solution)/shard_map/ppermute | solution.py:142
  15.2 8.4 %collective-permute-start.5 = (f32[2,32,512]{2,1,0:T(8,128)S(1)}, f32[2,32,512]{2,1,0:T(8,128)S(1)}, u32[]{:S(2)}, u32[]{:S(2)}) collective-permute-start(f32[2,32,512]{2,1,0:T(8,128)S(1)} %get-tuple-element.18), channel_id=1, source_target_pairs={{0,12},{2,14},{4,8},{6,10},{8,4},{10,6},{12,0},{14,2},{16,28},{18,... | collective-permute-start | bytes 393224 | tf_op jit(solution)/shard_map/ppermute | solution.py:142
  16.4 9.5 %collective-permute-start.16 = (f32[3,32,512]{2,1,0:T(8,128)S(1)}, f32[3,32,512]{2,1,0:T(8,128)S(1)}, u32[]{:S(2)}, u32[]{:S(2)}) collective-permute-start(f32[3,32,512]{2,1,0:T(8,128)S(1)} %shard_map.60.mine), channel_id=1, source_target_pairs={{0,16},{2,18},{4,20},{6,22},{8,24},{10,26},{12,28},{14,30},{16,0},... | collective-permute-start | bytes 589832 | tf_op jit(solution)/shard_map/ppermute | solution.py:142
  24.3 31.0 %copy-start.2 = (f32[1024,256]{1,0:T(8,128)S(1)}, f32[1024,256]{1,0:T(8,128)}, u32[]{:S(2)}) copy-start(f32[1024,256]{1,0:T(8,128)} %refs_0_.1) | copy-start | bytes 3145732
  24.3 11.7 %collective-permute-start.6 = (f32[3,32,512]{2,1,0:T(8,128)S(1)}, f32[3,32,512]{2,1,0:T(8,128)S(1)}, u32[]{:S(2)}, u32[]{:S(2)}) collective-permute-start(f32[3,32,512]{2,1,0:T(8,128)S(1)} %shard_map.58.mine), channel_id=1, source_target_pairs={{0,16},{2,18},{4,20},{6,22},{8,24},{10,26},{12,28},{14,30},{16,0},... | collective-permute-start | bytes 589832 | tf_op jit(solution)/shard_map/ppermute | solution.py:142
  26.5 28.8 %copy-start.4 = (s32[3]{0:T(128)S(1)}, s32[3]{0:T(128)}, u32[]{:S(2)}) copy-start(s32[3]{0:T(128)} %offsets.1) | copy-start | bytes 40
  26.5 13.7 %collective-permute-start.20 = (f32[3,32,512]{2,1,0:T(8,128)S(1)}, f32[3,32,512]{2,1,0:T(8,128)S(1)}, u32[]{:S(2)}, u32[]{:S(2)}) collective-permute-start(f32[3,32,512]{2,1,0:T(8,128)S(1)} %shard_map.61.refs_0_), channel_id=1, source_target_pairs={{0,8},{2,10},{4,12},{6,14},{8,0},{10,2},{12,4},{14,6},{16,24},{18,... | collective-permute-start | bytes 589832 | tf_op jit(solution)/shard_map/ppermute | solution.py:142
  34.0 9.4 %collective-permute-start.18 = (f32[3,32,512]{2,1,0:T(8,128)S(1)}, f32[3,32,512]{2,1,0:T(8,128)S(1)}, u32[]{:S(2)}, u32[]{:S(2)}) collective-permute-start(f32[3,32,512]{2,1,0:T(8,128)S(1)} %shard_map.61.refs_0_), channel_id=1, source_target_pairs={{0,4},{2,6},{4,0},{6,2},{8,12},{10,14},{12,8},{14,10},{16,20},{18,... | collective-permute-start | bytes 589832 | tf_op jit(solution)/shard_map/ppermute | solution.py:142
  35.8 7.6 %collective-permute-start.17 = (f32[3,32,512]{2,1,0:T(8,128)S(1)}, f32[3,32,512]{2,1,0:T(8,128)S(1)}, u32[]{:S(2)}, u32[]{:S(2)}) collective-permute-start(f32[3,32,512]{2,1,0:T(8,128)S(1)} %shard_map.61.refs_0_), channel_id=1, source_target_pairs={{0,2},{2,0},{4,6},{6,4},{8,10},{10,8},{12,14},{14,12},{16,18},{18,... | collective-permute-start | bytes 589832 | tf_op jit(solution)/shard_map/ppermute | solution.py:142
  36.6 19.7 %copy-start.1 = (f32[512,256]{1,0:T(8,128)S(1)}, f32[512,256]{1,0:T(8,128)}, u32[]{:S(2)}) copy-start(f32[512,256]{1,0:T(8,128)} %previous.3) | copy-start | bytes 1572868
  36.6 7.7 %collective-permute-start.10 = (f32[3,32,512]{2,1,0:T(8,128)S(1)}, f32[3,32,512]{2,1,0:T(8,128)S(1)}, u32[]{:S(2)}, u32[]{:S(2)}) collective-permute-start(f32[3,32,512]{2,1,0:T(8,128)S(1)} %shard_map.59.refs_0_), channel_id=1, source_target_pairs={{0,8},{2,10},{4,12},{6,14},{8,0},{10,2},{12,4},{14,6},{16,24},{18,... | collective-permute-start | bytes 589832 | tf_op jit(solution)/shard_map/ppermute | solution.py:142
  40.2 9.0 %collective-permute-start.22 = (f32[3,32,512]{2,1,0:T(8,128)S(1)}, f32[3,32,512]{2,1,0:T(8,128)S(1)}, u32[]{:S(2)}, u32[]{:S(2)}) collective-permute-start(f32[3,32,512]{2,1,0:T(8,128)S(1)} %collective-permute-done.20.refs_4_), channel_id=1, source_target_pairs={{0,4},{2,6},{4,0},{6,2},{8,12},{10,14},{12,8},{14,10},{16,20},{18,... | collective-permute-start | bytes 589832 | tf_op jit(solution)/shard_map/ppermute | solution.py:142
  43.4 9.8 %collective-permute-start.8 = (f32[3,32,512]{2,1,0:T(8,128)S(1)}, f32[3,32,512]{2,1,0:T(8,128)S(1)}, u32[]{:S(2)}, u32[]{:S(2)}) collective-permute-start(f32[3,32,512]{2,1,0:T(8,128)S(1)} %shard_map.59.refs_0_), channel_id=1, source_target_pairs={{0,4},{2,6},{4,0},{6,2},{8,12},{10,14},{12,8},{14,10},{16,20},{18,... | collective-permute-start | bytes 589832 | tf_op jit(solution)/shard_map/ppermute | solution.py:142
  43.4 9.8 %collective-permute-start.21 = (f32[3,32,512]{2,1,0:T(8,128)S(1)}, f32[3,32,512]{2,1,0:T(8,128)S(1)}, u32[]{:S(2)}, u32[]{:S(2)}) collective-permute-start(f32[3,32,512]{2,1,0:T(8,128)S(1)} %collective-permute-done.20.refs_4_), channel_id=1, source_target_pairs={{0,2},{2,0},{4,6},{6,4},{8,10},{10,8},{12,14},{14,12},{16,18},{18,... | collective-permute-start | bytes 589832 | tf_op jit(solution)/shard_map/ppermute | solution.py:142
  43.5 10.2 %collective-permute-start.19 = (f32[3,32,512]{2,1,0:T(8,128)S(1)}, f32[3,32,512]{2,1,0:T(8,128)S(1)}, u32[]{:S(2)}, u32[]{:S(2)}) collective-permute-start(f32[3,32,512]{2,1,0:T(8,128)S(1)} %collective-permute-done.18.refs_2_), channel_id=1, source_target_pairs={{0,2},{2,0},{4,6},{6,4},{8,10},{10,8},{12,14},{14,12},{16,18},{18,... | collective-permute-start | bytes 589832 | tf_op jit(solution)/shard_map/ppermute | solution.py:142
  44.3 11.0 %collective-permute-start.12 = (f32[3,32,512]{2,1,0:T(8,128)S(1)}, f32[3,32,512]{2,1,0:T(8,128)S(1)}, u32[]{:S(2)}, u32[]{:S(2)}) collective-permute-start(f32[3,32,512]{2,1,0:T(8,128)S(1)} %collective-permute-done.10.refs_4_), channel_id=1, source_target_pairs={{0,4},{2,6},{4,0},{6,2},{8,12},{10,14},{12,8},{14,10},{16,20},{18,... | collective-permute-start | bytes 589832 | tf_op jit(solution)/shard_map/ppermute | solution.py:142
  49.2 7.0 %collective-permute-start.23 = (f32[3,32,512]{2,1,0:T(8,128)S(1)}, f32[3,32,512]{2,1,0:T(8,128)S(1)}, u32[]{:S(2)}, u32[]{:S(2)}) collective-permute-start(f32[3,32,512]{2,1,0:T(8,128)S(1)} %collective-permute-done.22.refs_6_), channel_id=1, source_target_pairs={{0,2},{2,0},{4,6},{6,4},{8,10},{10,8},{12,14},{14,12},{16,18},{18,... | collective-permute-start | bytes 589832 | tf_op jit(solution)/shard_map/ppermute | solution.py:142
  53.2 4.6 %collective-permute-start.7 = (f32[3,32,512]{2,1,0:T(8,128)S(1)}, f32[3,32,512]{2,1,0:T(8,128)S(1)}, u32[]{:S(2)}, u32[]{:S(2)}) collective-permute-start(f32[3,32,512]{2,1,0:T(8,128)S(1)} %shard_map.59.refs_0_), channel_id=1, source_target_pairs={{0,2},{2,0},{4,6},{6,4},{8,10},{10,8},{12,14},{14,12},{16,18},{18,... | collective-permute-start | bytes 589832 | tf_op jit(solution)/shard_map/ppermute | solution.py:142
  53.2 4.6 %collective-permute-start.11 = (f32[3,32,512]{2,1,0:T(8,128)S(1)}, f32[3,32,512]{2,1,0:T(8,128)S(1)}, u32[]{:S(2)}, u32[]{:S(2)}) collective-permute-start(f32[3,32,512]{2,1,0:T(8,128)S(1)} %collective-permute-done.10.refs_4_), channel_id=1, source_target_pairs={{0,2},{2,0},{4,6},{6,4},{8,10},{10,8},{12,14},{14,12},{16,18},{18,... | collective-permute-start | bytes 589832 | tf_op jit(solution)/shard_map/ppermute | solution.py:142
  53.7 4.1 %collective-permute-start.9 = (f32[3,32,512]{2,1,0:T(8,128)S(1)}, f32[3,32,512]{2,1,0:T(8,128)S(1)}, u32[]{:S(2)}, u32[]{:S(2)}) collective-permute-start(f32[3,32,512]{2,1,0:T(8,128)S(1)} %collective-permute-done.8.refs_2_), channel_id=1, source_target_pairs={{0,2},{2,0},{4,6},{6,4},{8,10},{10,8},{12,14},{14,12},{16,18},{18,... | collective-permute-start | bytes 589832 | tf_op jit(solution)/shard_map/ppermute | solution.py:142
  55.3 2.5 %collective-permute-start.13 = (f32[3,32,512]{2,1,0:T(8,128)S(1)}, f32[3,32,512]{2,1,0:T(8,128)S(1)}, u32[]{:S(2)}, u32[]{:S(2)}) collective-permute-start(f32[3,32,512]{2,1,0:T(8,128)S(1)} %collective-permute-done.12.refs_6_), channel_id=1, source_target_pairs={{0,2},{2,0},{4,6},{6,4},{8,10},{10,8},{12,14},{14,12},{16,18},{18,... | collective-permute-start | bytes 589832 | tf_op jit(solution)/shard_map/ppermute | solution.py:142
where the time goes:
time: 60.4 us; the launch traced here: 60.2 us
  starting transfers between devices  32.8 us (54%)
  waiting for transfers between devices  18.6 us (31%)
  Pallas kernels  7.42 us (12%)
  local copies, waits for them, and re-layouts  1.19 us (2%)
    ppermute x23, starting transfers between devices, swap(): return lax.ppermute(array, 'row', [(i, i ^ mask) for i in range(devices)])  30.3 us
    ppermute x23, waiting for transfers between devices, swap(): return lax.ppermute(array, 'row', [(i, i ^ mask) for i in range(devices)])  18.6 us
    pallas_call x2, Pallas kernels, shards(): pl.pallas_call(functools.partial(multiply_kernel, part), out_shape=out_sh...  3.89 us
    pallas_call x7, Pallas kernels, call(): pl.pallas_call(kernel, out_shape=out_shape, in_specs=in_specs, out_specs=...  3.53 us
    ppermute x1, starting transfers between devices, shift(): return lax.ppermute(array, 'col', pairs)  2.56 us
  transfers between devices with their start and end apart: 24, of which 8 were waited for; matrix products, arithmetic and copies ran while one was open for 0% of the time, Pallas kernels for 8%

commit v1 on v0

--- a/solution.py
+++ b/solution.py
@@ -45,8 +45,7 @@
         out[1] = got[place * chunk:(place + 1) * chunk, :]
 
 
-def pick_kernel(part, chips, owners, own, got, *refs):
-    pieces, out = refs[:-1], refs[-1]
+def pick(part, chips, owners, own, got, pieces, out):
     chunk = out.shape[1]
     member = lax.axis_index("row") % (2 * chips)
     first = part * chips
@@ -66,7 +65,7 @@
                     out[number] = piece[core]
 
 
-def merge_kernel(group, owners, mine, other, out):
+def merge(group, owners, mine, other, out):
     half = lax.axis_index("row") // group
     for number in range(out.shape[0]):
         here = owners[0, number] // group == half
@@ -78,6 +77,19 @@
         @pl.when(jnp.logical_not(here))
         def _():
             out[number] = other[number]
+
+
+def pick_kernel(chips, owners, own, got, *refs):
+    pick(0, chips, owners, own, got, refs[:chips - 1], refs[-1])
+
+
+def step_kernel(part, chips, owners, mine, other, own, got, *refs):
+    pick(part, chips, owners, own, got, refs[:chips - 1], refs[-1])
+    merge(2 * chips, owners, mine, other, refs[-2])
+
+
+def merge_kernel(group, owners, mine, other, *refs):
+    merge(group, owners, mine, other, refs[-1])
 
 
 def right_kernel(offsets, *refs):
@@ -146,23 +158,16 @@
         return lax.ppermute(array, "col", pairs)
 
     got = swap(own.reshape(rows // (2 * chunk), 2 * chunk, width)[:, chunk:].reshape(rows // 2, width), 1)
-    mine = []
-    wait = []
+    arrived = []
     for part in range(PARTS):
+        wait = [arrived[-1][-1]] if arrived else []
         sent = call(
             functools.partial(gather_kernel, part, chips),
             (pair,) * (chips - 1),
             [VMEM, VMEM] + [ANY] * len(wait),
             (own, got, *wait),
         )
-        pieces = [swap(array, 2 * step) for step, array in enumerate(sent, 1)]
-        wait = pieces[-1:]
-        mine.append(call(
-            functools.partial(pick_kernel, part, chips),
-            piece,
-            [SMEM] + [VMEM] * (2 + len(pieces)),
-            (owners, own, got, *pieces),
-        ))
+        arrived.append([swap(array, 2 * step) for step, array in enumerate(sent, 1)])
 
     rights = [right] + [shift(right, distance) for distance in range(1, columns)]
     terms = jax.ShapeDtypeStruct((count * width, right.shape[1]), jnp.bfloat16)
@@ -170,20 +175,38 @@
         right_kernel, (terms, terms), [SMEM] + [VMEM] * columns, (offsets, *rights), flops=4 * terms.size
     )
 
-    results = []
-    for part in range(PARTS):
-        merged = call(
-            functools.partial(merge_kernel, group),
-            piece,
-            [SMEM, VMEM, VMEM],
-            (owners, mine[part], swap(mine[part], group)),
-        )
+    mine = call(
+        functools.partial(pick_kernel, chips), piece, [SMEM] + [VMEM] * (chips + 1), (owners, own, got, *arrived[0])
+    )
+    def spread(merged):
         pieces = {0: merged}
         step = chips
         while step > 1:
             for s in list(pieces):
                 pieces[s + step] = swap(pieces[s], step)
             step //= 2
+        return pieces
+
+    gathered = []
+    for part in range(1, PARTS):
+        merged, mine = call(
+            functools.partial(step_kernel, part, chips),
+            (piece, piece),
+            [SMEM] + [VMEM] * (chips + 3),
+            (owners, mine, swap(mine, group), own, got, *arrived[part]),
+        )
+        gathered.append(spread(merged))
+    wait = [right_terms[0]] + [array for pieces in gathered for s, array in pieces.items() if s]
+    merged = call(
+        functools.partial(merge_kernel, group),
+        piece,
+        [SMEM, VMEM, VMEM] + [ANY] * len(wait),
+        (owners, mine, swap(mine, group), *wait),
+    )
+    gathered.append(spread(merged))
+
+    results = []
+    for part, pieces in enumerate(gathered):
         for s in list(pieces):
             pieces[s + 1] = swap(pieces[s], 1)
         last = part == PARTS - 1

time: 60.4 us -> 61.9 us (1.025)
  waiting for transfers between devices: 18.6 us -> 36.2 us
  starting transfers between devices: 32.8 us -> 17.3 us
    ppermute x23, waiting for transfers between devices: 18.6 us -> 36.2 us  [swap(): return lax.ppermute(array, 'row', [(i, i ^ mask) for i in range(devices)])]
    ppermute x23, starting transfers between devices: 30.3 us -> 14.8 us  [swap(): return lax.ppermute(array, 'row', [(i, i ^ mask) for i in range(devices)])]
    pallas_call x7 -> x6, Pallas kernels: 3.53 us -> 2.99 us  [call(): pl.pallas_call(kernel, out_shape=out_shape, in_specs=in_specs, out_specs=...]
  transfers between devices with their start and end apart: 24 -> 24, of which waited for: 8 -> 12; matrix products, arithmetic and copies ran while one was open for 0% -> 0% of each run, Pallas kernels for 8% -> 6%
where the time goes in v1:
time: 61.9 us; the launch traced here: 61.8 us
  waiting for transfers between devices  36.2 us (58%)
  starting transfers between devices  17.3 us (28%)
  Pallas kernels  6.89 us (11%)
  local copies, waits for them, and re-layouts  1.19 us (2%)
    ppermute x23, waiting for transfers between devices, swap(): return lax.ppermute(array, 'row', [(i, i ^ mask) for i in range(devices)])  36.2 us
    ppermute x23, starting transfers between devices, swap(): return lax.ppermute(array, 'row', [(i, i ^ mask) for i in range(devices)])  14.8 us
    pallas_call x2, Pallas kernels, shards(): pl.pallas_call(functools.partial(multiply_kernel, part), out_shape=out_sh...  3.9 us
    pallas_call x6, Pallas kernels, call(): pl.pallas_call(kernel, out_shape=out_shape, in_specs=in_specs, out_specs=...  2.99 us
    ppermute x1, starting transfers between devices, shift(): return lax.ppermute(array, 'col', pairs)  2.56 us
  transfers between devices with their start and end apart: 24, of which 12 were waited for; matrix products, arithmetic and copies ran while one was open for 0% of the time, Pallas kernels for 6%

profile of v1, /device:TPU:0, one launch (start us, length us, event | category | flops | bytes accessed | tf_op | source)
XLA Modules:
  0.0 61.8 jit_solution(11149804643240792367)
XLA Ops:
  0.0 0.0 copy-start
  0.0 1.2 %slice.4 = f32[8,32,512]{2,1,0:T(8,128)S(1)} slice(f32[8,64,512]{2,1,0:T(8,128)} %bitcast.3), slice={[0:8], [32:64], [0:512]} | slice | bytes 1048576 | tf_op jit(solution)/shard_map/slice | solution.py:160
  1.2 0.5 collective-permute-start.1
  1.7 2.6 %collective-permute-start = (f32[1024,256]{1,0:T(8,128)}, f32[1024,256]{1,0:T(8,128)S(1)}, u32[]{:S(2)}, u32[]{:S(2)}) collective-permute-start(f32[1024,256]{1,0:T(8,128)} %refs_0_.1), channel_id=1, source_target_pairs={{1,0},{0,1},{3,2},{2,3},{5,4},{4,5},{7,6},{6,7},{9,8},{8,9},{11,10... | collective-permute-start | bytes 3145736 | tf_op jit(solution)/shard_map/ppermute | solution.py:158
  4.3 0.0 collective-permute-done.1.got
  4.3 0.0 copy-done
  4.3 2.9 %collective-permute-start.4 = (f32[2,32,512]{2,1,0:T(8,128)S(1)}, f32[2,32,512]{2,1,0:T(8,128)S(1)}, u32[]{:S(2)}, u32[]{:S(2)}) collective-permute-start(f32[2,32,512]{2,1,0:T(8,128)S(1)} %get-tuple-element.19), channel_id=1, source_target_pairs={{0,12},{2,14},{4,8},{6,10},{8,4},{10,6},{12,0},{14,2},{16,28},{18,... | collective-permute-start | bytes 393224 | tf_op jit(solution)/shard_map/ppermute | solution.py:154
  7.2 0.0 copy-start.3
  7.2 0.5 collective-permute-start.2
  7.7 0.1 collective-permute-start.3
  7.9 3.3 %collective-permute-done.4.refs_2_.refs_0_ = f32[2,32,512]{2,1,0:T(8,128)S(1)} collective-permute-done((f32[2,32,512]{2,1,0:T(8,128)S(1)}, f32[2,32,512]{2,1,0:T(8,128)S(1)}, u32[]{:S(2)}, u32[]{:S(2)}) %collective-permute-start.4) | collective-permute-done | bytes 131104 | tf_op jit(solution)/shard_map/ppermute | solution.py:154
  11.1 2.7 %collective-permute-done.2.refs_0_ = f32[2,32,512]{2,1,0:T(8,128)S(1)} collective-permute-done((f32[2,32,512]{2,1,0:T(8,128)S(1)}, f32[2,32,512]{2,1,0:T(8,128)S(1)}, u32[]{:S(2)}, u32[]{:S(2)}) %collective-permute-start.2) | collective-permute-done | bytes 131104 | tf_op jit(solution)/shard_map/ppermute | solution.py:154
  13.8 0.2 collective-permute-done.3.refs_1_
  14.0 0.0 copy-done.3
  14.0 0.7 %shard_map.57.mine = f32[3,32,512]{2,1,0:T(8,128)S(1)} custom-call(s32[1,3]{1,0:T(1,128)S(1)} %copy-done.3, f32[512,512]{1,0:T(8,128)S(1)} %bitcast.5, f32[256,512]{1,0:T(8,128)S(1)} %collective-permute-done.1.got, f32[2,32,512]{2,1,0:T(8,128)S(1)} %collective-permute-done.2.refs_0_, f32[2,32,512]{2,1,0:T(8,128)S(1)} %collective-permute-done.3.refs_1_, ...), custom_call_target="tpu_custom_call" | custom-call | bytes 2162700 | tf_op jit(solution)/shard_map/pallas_call | solution.py:19
  14.7 2.7 %collective-permute-start.5 = (f32[3,32,512]{2,1,0:T(8,128)S(1)}, f32[3,32,512]{2,1,0:T(8,128)S(1)}, u32[]{:S(2)}, u32[]{:S(2)}) collective-permute-start(f32[3,32,512]{2,1,0:T(8,128)S(1)} %shard_map.57.mine), channel_id=1, source_target_pairs={{0,16},{2,18},{4,20},{6,22},{8,24},{10,26},{12,28},{14,30},{16,0},... | collective-permute-start | bytes 589832 | tf_op jit(solution)/shard_map/ppermute | solution.py:154
  17.4 1.5 %collective-permute-start.6 = (f32[2,32,512]{2,1,0:T(8,128)S(1)}, f32[2,32,512]{2,1,0:T(8,128)S(1)}, u32[]{:S(2)}, u32[]{:S(2)}) collective-permute-start(f32[2,32,512]{2,1,0:T(8,128)S(1)} %get-tuple-element.20), channel_id=1, source_target_pairs={{0,4},{2,6},{4,0},{6,2},{8,12},{10,14},{12,8},{14,10},{16,20},{18,... | collective-permute-start | bytes 393224 | tf_op jit(solution)/shard_map/ppermute | solution.py:154
  18.9 0.8 %collective-permute-start.7 = (f32[2,32,512]{2,1,0:T(8,128)S(1)}, f32[2,32,512]{2,1,0:T(8,128)S(1)}, u32[]{:S(2)}, u32[]{:S(2)}) collective-permute-start(f32[2,32,512]{2,1,0:T(8,128)S(1)} %get-tuple-element.21), channel_id=1, source_target_pairs={{0,8},{2,10},{4,12},{6,14},{8,0},{10,2},{12,4},{14,6},{16,24},{18,... | collective-permute-start | bytes 393224 | tf_op jit(solution)/shard_map/ppermute | solution.py:154
  19.7 0.0 copy-start.2
  19.7 1.2 %collective-permute-start.8 = (f32[2,32,512]{2,1,0:T(8,128)S(1)}, f32[2,32,512]{2,1,0:T(8,128)S(1)}, u32[]{:S(2)}, u32[]{:S(2)}) collective-permute-start(f32[2,32,512]{2,1,0:T(8,128)S(1)} %get-tuple-element.22), channel_id=1, source_target_pairs={{0,12},{2,14},{4,8},{6,10},{8,4},{10,6},{12,0},{14,2},{16,28},{18,... | collective-permute-start | bytes 393224 | tf_op jit(solution)/shard_map/ppermute | solution.py:154
  21.0 1.6 %collective-permute-done.6.refs_0_ = f32[2,32,512]{2,1,0:T(8,128)S(1)} collective-permute-done((f32[2,32,512]{2,1,0:T(8,128)S(1)}, f32[2,32,512]{2,1,0:T(8,128)S(1)}, u32[]{:S(2)}, u32[]{:S(2)}) %collective-permute-start.6) | collective-permute-done | bytes 131104 | tf_op jit(solution)/shard_map/ppermute | solution.py:154
  22.5 5.7 %collective-permute-done.7.refs_1_ = f32[2,32,512]{2,1,0:T(8,128)S(1)} collective-permute-done((f32[2,32,512]{2,1,0:T(8,128)S(1)}, f32[2,32,512]{2,1,0:T(8,128)S(1)}, u32[]{:S(2)}, u32[]{:S(2)}) %collective-permute-start.7) | collective-permute-done | bytes 131104 | tf_op jit(solution)/shard_map/ppermute | solution.py:154
  28.2 2.4 %collective-permute-done.8.refs_2_ = f32[2,32,512]{2,1,0:T(8,128)S(1)} collective-permute-done((f32[2,32,512]{2,1,0:T(8,128)S(1)}, f32[2,32,512]{2,1,0:T(8,128)S(1)}, u32[]{:S(2)}, u32[]{:S(2)}) %collective-permute-start.8) | collective-permute-done | bytes 131104 | tf_op jit(solution)/shard_map/ppermute | solution.py:154
  30.6 0.0 collective-permute-done.5.other
  30.6 0.7 %shard_map.59 = (f32[3,32,512]{2,1,0:T(8,128)S(1)}, f32[3,32,512]{2,1,0:T(8,128)S(1)}) custom-call(s32[1,3]{1,0:T(1,128)S(1)} %copy-done.3, f32[3,32,512]{2,1,0:T(8,128)S(1)} %shard_map.57.mine, f32[3,32,512]{2,1,0:T(8,128)S(1)} %collective-permute-done.5.other, f32[512,512]{1,0:T(8,128)S(1)} %bitcast.7, f32[256,512]{1,0:T(8,128)S(1)} %collective-permute-done.1.got, ...), custom_call_target="tpu_custom_call" | custom-call | bytes 2752524 | tf_op jit(solution)/shard_map/pallas_call | solution.py:19
  31.4 0.0 copy-start.4
  31.4 0.2 collective-permute-start.10
  31.6 0.5 collective-permute-start.11
  32.1 1.8 %collective-permute-start.9 = (f32[3,32,512]{2,1,0:T(8,128)S(1)}, f32[3,32,512]{2,1,0:T(8,128)S(1)}, u32[]{:S(2)}, u32[]{:S(2)}) collective-permute-start(f32[3,32,512]{2,1,0:T(8,128)S(1)} %get-tuple-element.23.mine), channel_id=1, source_target_pairs={{0,16},{2,18},{4,20},{6,22},{8,24},{10,26},{12,28},{14,30},{16,0},... | collective-permute-start | bytes 589832 | tf_op jit(solution)/shard_map/ppermute | solution.py:154
  33.8 5.5 %collective-permute-done.10.refs_1_.refs_4_ = f32[3,32,512]{2,1,0:T(8,128)S(1)} collective-permute-done((f32[3,32,512]{2,1,0:T(8,128)S(1)}, f32[3,32,512]{2,1,0:T(8,128)S(1)}, u32[]{:S(2)}, u32[]{:S(2)}) %collective-permute-start.10) | collective-permute-done | bytes 196640 | tf_op jit(solution)/shard_map/ppermute | solution.py:154
  39.3 0.0 collective-permute-start.12
  39.3 0.0 collective-permute-done.refs_1_
  39.3 0.0 copy-done.2
  39.3 0.0 copy-done.4
  39.3 0.9 %shard_map.55 = (bf16[1536,256]{1,0:T(8,128)(2,1)S(1)}, bf16[1536,256]{1,0:T(8,128)(2,1)S(1)}) custom-call(s32[3]{0:T(128)S(1)} %copy-done.4, f32[1024,256]{1,0:T(8,128)S(1)} %copy-done.2, f32[1024,256]{1,0:T(8,128)S(1)} %collective-permute-done.refs_1_), custom_call_target="tpu_custom_call" | custom-call | flops 1572864 | bytes 3670028 | tf_op jit(solution)/shard_map/pallas_call | solution.py:19
  40.2 0.0 collective-permute-done.11.refs_2_
  40.2 2.4 %collective-permute-done.9.other = f32[3,32,512]{2,1,0:T(8,128)S(1)} collective-permute-done((f32[3,32,512]{2,1,0:T(8,128)S(1)}, f32[3,32,512]{2,1,0:T(8,128)S(1)}, u32[]{:S(2)}, u32[]{:S(2)}) %collective-permute-start.9) | collective-permute-done | bytes 196640 | tf_op jit(solution)/shard_map/ppermute | solution.py:154
  42.6 2.4 %collective-permute-done.12.refs_3_.refs_6_ = f32[3,32,512]{2,1,0:T(8,128)S(1)} collective-permute-done((f32[3,32,512]{2,1,0:T(8,128)S(1)}, f32[3,32,512]{2,1,0:T(8,128)S(1)}, u32[]{:S(2)}, u32[]{:S(2)}) %collective-permute-start.12) | collective-permute-done | bytes 196640 | tf_op jit(solution)/shard_map/ppermute | solution.py:154
  45.0 0.6 shard_map.60.refs_0_
  45.6 0.1 collective-permute-start.16
  45.8 0.0 collective-permute-start.20
  45.8 0.5 collective-permute-start.21
  46.3 0.1 collective-permute-start.22
  46.3 0.4 collective-permute-start.14
  46.8 4.6 %collective-permute-done.16.refs_4_ = f32[3,32,512]{2,1,0:T(8,128)S(1)} collective-permute-done((f32[3,32,512]{2,1,0:T(8,128)S(1)}, f32[3,32,512]{2,1,0:T(8,128)S(1)}, u32[]{:S(2)}, u32[]{:S(2)}) %collective-permute-start.16) | collective-permute-done | bytes 196640 | tf_op jit(solution)/shard_map/ppermute | solution.py:154
  51.3 0.3 collective-permute-start.18
  51.6 0.0 collective-permute-done.20.refs_1_
  51.6 0.0 collective-permute-start.23
  51.6 0.0 collective-permute-done.21.refs_3_
  51.6 0.5 collective-permute-start.13
  52.1 0.0 collective-permute-done.22.refs_5_
  52.2 0.1 collective-permute-start.17
  52.2 1.8 %collective-permute-done.14.refs_2_ = f32[3,32,512]{2,1,0:T(8,128)S(1)} collective-permute-done((f32[3,32,512]{2,1,0:T(8,128)S(1)}, f32[3,32,512]{2,1,0:T(8,128)S(1)}, u32[]{:S(2)}, u32[]{:S(2)}) %collective-permute-start.14) | collective-permute-done | bytes 196640 | tf_op jit(solution)/shard_map/ppermute | solution.py:154
  54.1 0.0 collective-permute-start.15
  54.1 3.7 %collective-permute-done.18.refs_6_ = f32[3,32,512]{2,1,0:T(8,128)S(1)} collective-permute-done((f32[3,32,512]{2,1,0:T(8,128)S(1)}, f32[3,32,512]{2,1,0:T(8,128)S(1)}, u32[]{:S(2)}, u32[]{:S(2)}) %collective-permute-start.18) | collective-permute-done | bytes 196640 | tf_op jit(solution)/shard_map/ppermute | solution.py:154
  57.8 0.0 collective-permute-start.19
  57.8 0.0 collective-permute-done.23.refs_7_
  57.8 0.0 copy-done.1
  57.8 1.6 %shard_map.61.refs_8_ = f32[256,256]{1,0:T(8,128)S(1)} custom-call(s32[1,3]{1,0:T(1,128)S(1)} %copy-done.3, bf16[1536,256]{1,0:T(8,128)(2,1)S(1)} %get-tuple-element.15.refs_0_.right_high, bf16[1536,256]{1,0:T(8,128)(2,1)S(1)} %get-tuple-element.16.right_low, f32[512,256]{1,0:T(8,128)S(1)} %copy-done.1, f32[3,32,512]{2,1,0:T(8,128)S(1)} %get-tuple-element.24.refs_0_, ...), custom_call_target="tpu_custom_call" | custom-call | flops 603979776 | bytes 3670028 | tf_op jit(solution)/shard_map/pallas_call | solution.py:216
  59.4 0.0 collective-permute-done.13.refs_1_
  59.4 0.0 collective-permute-done.15.refs_3_
  59.4 0.0 collective-permute-done.17.refs_5_
  59.4 0.0 collective-permute-done.19.refs_7_
  59.4 2.4 %shard_map.62 = f32[512,256]{1,0:T(8,128)} custom-call(s32[1,3]{1,0:T(1,128)S(1)} %copy-done.3, bf16[1536,256]{1,0:T(8,128)(2,1)S(1)} %get-tuple-element.15.refs_0_.right_high, bf16[1536,256]{1,0:T(8,128)(2,1)S(1)} %get-tuple-element.16.right_low, f32[512,256]{1,0:T(8,128)S(1)} %copy-done.1, f32[3,32,512]{2,1,0:T(8,128)S(1)} %shard_map.60.refs_0_, ...), custom_call_target="tpu_custom_call" | custom-call | flops 603979776 | bytes 3932172 | tf_op jit(solution)/shard_map/pallas_call | solution.py:216
  (3 shorter events, 0.1 us)
Async XLA Ops:
  0.0 4.3 %copy-start = (f32[1,512,512]{2,1,0:T(8,128)S(1)}, f32[1,512,512]{2,1,0:T(8,128)}, u32[]{:S(2)}) copy-start(f32[1,512,512]{2,1,0:T(8,128)} %param.5) | copy-start | bytes 3145732
  1.2 3.1 %collective-permute-start.1 = (f32[256,512]{1,0:T(8,128)S(1)}, f32[256,512]{1,0:T(8,128)S(1)}, u32[]{:S(2)}, u32[]{:S(2)}) collective-permute-start(f32[256,512]{1,0:T(8,128)S(1)} %bitcast.8), channel_id=1, source_target_pairs={{0,2},{2,0},{4,6},{6,4},{8,10},{10,8},{12,14},{14,12},{16,18},{18,... | collective-permute-start | bytes 1572872 | tf_op jit(solution)/shard_map/ppermute | solution.py:154
  1.7 37.6 %collective-permute-start = (f32[1024,256]{1,0:T(8,128)}, f32[1024,256]{1,0:T(8,128)S(1)}, u32[]{:S(2)}, u32[]{:S(2)}) collective-permute-start(f32[1024,256]{1,0:T(8,128)} %refs_0_.1), channel_id=1, source_target_pairs={{1,0},{0,1},{3,2},{2,3},{5,4},{4,5},{7,6},{6,7},{9,8},{8,9},{11,10... | collective-permute-start | bytes 3145736 | tf_op jit(solution)/shard_map/ppermute | solution.py:158
  4.3 6.8 %collective-permute-start.4 = (f32[2,32,512]{2,1,0:T(8,128)S(1)}, f32[2,32,512]{2,1,0:T(8,128)S(1)}, u32[]{:S(2)}, u32[]{:S(2)}) collective-permute-start(f32[2,32,512]{2,1,0:T(8,128)S(1)} %get-tuple-element.19), channel_id=1, source_target_pairs={{0,12},{2,14},{4,8},{6,10},{8,4},{10,6},{12,0},{14,2},{16,28},{18,... | collective-permute-start | bytes 393224 | tf_op jit(solution)/shard_map/ppermute | solution.py:154
  7.2 6.8 %copy-start.3 = (s32[1,3]{1,0:T(1,128)S(1)}, s32[1,3]{1,0:T(1,128)}, u32[]{:S(2)}) copy-start(s32[1,3]{1,0:T(1,128)} %owners.9) | copy-start | bytes 40
  7.2 6.6 %collective-permute-start.2 = (f32[2,32,512]{2,1,0:T(8,128)S(1)}, f32[2,32,512]{2,1,0:T(8,128)S(1)}, u32[]{:S(2)}, u32[]{:S(2)}) collective-permute-start(f32[2,32,512]{2,1,0:T(8,128)S(1)} %get-tuple-element.17), channel_id=1, source_target_pairs={{0,4},{2,6},{4,0},{6,2},{8,12},{10,14},{12,8},{14,10},{16,20},{18,... | collective-permute-start | bytes 393224 | tf_op jit(solution)/shard_map/ppermute | solution.py:154
  7.7 6.3 %collective-permute-start.3 = (f32[2,32,512]{2,1,0:T(8,128)S(1)}, f32[2,32,512]{2,1,0:T(8,128)S(1)}, u32[]{:S(2)}, u32[]{:S(2)}) collective-permute-start(f32[2,32,512]{2,1,0:T(8,128)S(1)} %get-tuple-element.18), channel_id=1, source_target_pairs={{0,8},{2,10},{4,12},{6,14},{8,0},{10,2},{12,4},{14,6},{16,24},{18,... | collective-permute-start | bytes 393224 | tf_op jit(solution)/shard_map/ppermute | solution.py:154
  14.7 15.9 %collective-permute-start.5 = (f32[3,32,512]{2,1,0:T(8,128)S(1)}, f32[3,32,512]{2,1,0:T(8,128)S(1)}, u32[]{:S(2)}, u32[]{:S(2)}) collective-permute-start(f32[3,32,512]{2,1,0:T(8,128)S(1)} %shard_map.57.mine), channel_id=1, source_target_pairs={{0,16},{2,18},{4,20},{6,22},{8,24},{10,26},{12,28},{14,30},{16,0},... | collective-permute-start | bytes 589832 | tf_op jit(solution)/shard_map/ppermute | solution.py:154
  17.4 5.1 %collective-permute-start.6 = (f32[2,32,512]{2,1,0:T(8,128)S(1)}, f32[2,32,512]{2,1,0:T(8,128)S(1)}, u32[]{:S(2)}, u32[]{:S(2)}) collective-permute-start(f32[2,32,512]{2,1,0:T(8,128)S(1)} %get-tuple-element.20), channel_id=1, source_target_pairs={{0,4},{2,6},{4,0},{6,2},{8,12},{10,14},{12,8},{14,10},{16,20},{18,... | collective-permute-start | bytes 393224 | tf_op jit(solution)/shard_map/ppermute | solution.py:154
  18.9 9.3 %collective-permute-start.7 = (f32[2,32,512]{2,1,0:T(8,128)S(1)}, f32[2,32,512]{2,1,0:T(8,128)S(1)}, u32[]{:S(2)}, u32[]{:S(2)}) collective-permute-start(f32[2,32,512]{2,1,0:T(8,128)S(1)} %get-tuple-element.21), channel_id=1, source_target_pairs={{0,8},{2,10},{4,12},{6,14},{8,0},{10,2},{12,4},{14,6},{16,24},{18,... | collective-permute-start | bytes 393224 | tf_op jit(solution)/shard_map/ppermute | solution.py:154
  19.7 19.6 %copy-start.2 = (f32[1024,256]{1,0:T(8,128)S(1)}, f32[1024,256]{1,0:T(8,128)}, u32[]{:S(2)}) copy-start(f32[1024,256]{1,0:T(8,128)} %refs_0_.1) | copy-start | bytes 3145732
  19.7 10.9 %collective-permute-start.8 = (f32[2,32,512]{2,1,0:T(8,128)S(1)}, f32[2,32,512]{2,1,0:T(8,128)S(1)}, u32[]{:S(2)}, u32[]{:S(2)}) collective-permute-start(f32[2,32,512]{2,1,0:T(8,128)S(1)} %get-tuple-element.22), channel_id=1, source_target_pairs={{0,12},{2,14},{4,8},{6,10},{8,4},{10,6},{12,0},{14,2},{16,28},{18,... | collective-permute-start | bytes 393224 | tf_op jit(solution)/shard_map/ppermute | solution.py:154
  31.4 7.9 %copy-start.4 = (s32[3]{0:T(128)S(1)}, s32[3]{0:T(128)}, u32[]{:S(2)}) copy-start(s32[3]{0:T(128)} %offsets.1) | copy-start | bytes 40
  31.4 7.9 %collective-permute-start.10 = (f32[3,32,512]{2,1,0:T(8,128)S(1)}, f32[3,32,512]{2,1,0:T(8,128)S(1)}, u32[]{:S(2)}, u32[]{:S(2)}) collective-permute-start(f32[3,32,512]{2,1,0:T(8,128)S(1)} %get-tuple-element.24.refs_0_), channel_id=1, source_target_pairs={{0,8},{2,10},{4,12},{6,14},{8,0},{10,2},{12,4},{14,6},{16,24},{18,... | collective-permute-start | bytes 589832 | tf_op jit(solution)/shard_map/ppermute | solution.py:154
  31.6 8.7 %collective-permute-start.11 = (f32[3,32,512]{2,1,0:T(8,128)S(1)}, f32[3,32,512]{2,1,0:T(8,128)S(1)}, u32[]{:S(2)}, u32[]{:S(2)}) collective-permute-start(f32[3,32,512]{2,1,0:T(8,128)S(1)} %get-tuple-element.24.refs_0_), channel_id=1, source_target_pairs={{0,4},{2,6},{4,0},{6,2},{8,12},{10,14},{12,8},{14,10},{16,20},{18,... | collective-permute-start | bytes 589832 | tf_op jit(solution)/shard_map/ppermute | solution.py:154
  32.1 10.6 %collective-permute-start.9 = (f32[3,32,512]{2,1,0:T(8,128)S(1)}, f32[3,32,512]{2,1,0:T(8,128)S(1)}, u32[]{:S(2)}, u32[]{:S(2)}) collective-permute-start(f32[3,32,512]{2,1,0:T(8,128)S(1)} %get-tuple-element.23.mine), channel_id=1, source_target_pairs={{0,16},{2,18},{4,20},{6,22},{8,24},{10,26},{12,28},{14,30},{16,0},... | collective-permute-start | bytes 589832 | tf_op jit(solution)/shard_map/ppermute | solution.py:154
  39.3 5.7 %collective-permute-start.12 = (f32[3,32,512]{2,1,0:T(8,128)S(1)}, f32[3,32,512]{2,1,0:T(8,128)S(1)}, u32[]{:S(2)}, u32[]{:S(2)}) collective-permute-start(f32[3,32,512]{2,1,0:T(8,128)S(1)} %collective-permute-done.10.refs_1_.refs_4_), channel_id=1, source_target_pairs={{0,4},{2,6},{4,0},{6,2},{8,12},{10,14},{12,8},{14,10},{16,20},{18,... | collective-permute-start | bytes 589832 | tf_op jit(solution)/shard_map/ppermute | solution.py:154
  45.0 12.8 %copy-start.1 = (f32[512,256]{1,0:T(8,128)S(1)}, f32[512,256]{1,0:T(8,128)}, u32[]{:S(2)}) copy-start(f32[512,256]{1,0:T(8,128)} %previous.3) | copy-start | bytes 1572868
  45.6 5.7 %collective-permute-start.16 = (f32[3,32,512]{2,1,0:T(8,128)S(1)}, f32[3,32,512]{2,1,0:T(8,128)S(1)}, u32[]{:S(2)}, u32[]{:S(2)}) collective-permute-start(f32[3,32,512]{2,1,0:T(8,128)S(1)} %shard_map.60.refs_0_), channel_id=1, source_target_pairs={{0,8},{2,10},{4,12},{6,14},{8,0},{10,2},{12,4},{14,6},{16,24},{18,... | collective-permute-start | bytes 589832 | tf_op jit(solution)/shard_map/ppermute | solution.py:154
  45.8 5.9 %collective-permute-start.20 = (f32[3,32,512]{2,1,0:T(8,128)S(1)}, f32[3,32,512]{2,1,0:T(8,128)S(1)}, u32[]{:S(2)}, u32[]{:S(2)}) collective-permute-start(f32[3,32,512]{2,1,0:T(8,128)S(1)} %get-tuple-element.24.refs_0_), channel_id=1, source_target_pairs={{0,2},{2,0},{4,6},{6,4},{8,10},{10,8},{12,14},{14,12},{16,18},{18,... | collective-permute-start | bytes 589832 | tf_op jit(solution)/shard_map/ppermute | solution.py:154
  45.8 5.9 %collective-permute-start.21 = (f32[3,32,512]{2,1,0:T(8,128)S(1)}, f32[3,32,512]{2,1,0:T(8,128)S(1)}, u32[]{:S(2)}, u32[]{:S(2)}) collective-permute-start(f32[3,32,512]{2,1,0:T(8,128)S(1)} %collective-permute-done.11.refs_2_), channel_id=1, source_target_pairs={{0,2},{2,0},{4,6},{6,4},{8,10},{10,8},{12,14},{14,12},{16,18},{18,... | collective-permute-start | bytes 589832 | tf_op jit(solution)/shard_map/ppermute | solution.py:154
  46.3 5.9 %collective-permute-start.22 = (f32[3,32,512]{2,1,0:T(8,128)S(1)}, f32[3,32,512]{2,1,0:T(8,128)S(1)}, u32[]{:S(2)}, u32[]{:S(2)}) collective-permute-start(f32[3,32,512]{2,1,0:T(8,128)S(1)} %collective-permute-done.10.refs_1_.refs_4_), channel_id=1, source_target_pairs={{0,2},{2,0},{4,6},{6,4},{8,10},{10,8},{12,14},{14,12},{16,18},{18,... | collective-permute-start | bytes 589832 | tf_op jit(solution)/shard_map/ppermute | solution.py:154
  46.3 7.7 %collective-permute-start.14 = (f32[3,32,512]{2,1,0:T(8,128)S(1)}, f32[3,32,512]{2,1,0:T(8,128)S(1)}, u32[]{:S(2)}, u32[]{:S(2)}) collective-permute-start(f32[3,32,512]{2,1,0:T(8,128)S(1)} %shard_map.60.refs_0_), channel_id=1, source_target_pairs={{0,4},{2,6},{4,0},{6,2},{8,12},{10,14},{12,8},{14,10},{16,20},{18,... | collective-permute-start | bytes 589832 | tf_op jit(solution)/shard_map/ppermute | solution.py:154
  51.3 6.5 %collective-permute-start.18 = (f32[3,32,512]{2,1,0:T(8,128)S(1)}, f32[3,32,512]{2,1,0:T(8,128)S(1)}, u32[]{:S(2)}, u32[]{:S(2)}) collective-permute-start(f32[3,32,512]{2,1,0:T(8,128)S(1)} %collective-permute-done.16.refs_4_), channel_id=1, source_target_pairs={{0,4},{2,6},{4,0},{6,2},{8,12},{10,14},{12,8},{14,10},{16,20},{18,... | collective-permute-start | bytes 589832 | tf_op jit(solution)/shard_map/ppermute | solution.py:154
  51.6 6.2 %collective-permute-start.23 = (f32[3,32,512]{2,1,0:T(8,128)S(1)}, f32[3,32,512]{2,1,0:T(8,128)S(1)}, u32[]{:S(2)}, u32[]{:S(2)}) collective-permute-start(f32[3,32,512]{2,1,0:T(8,128)S(1)} %collective-permute-done.12.refs_3_.refs_6_), channel_id=1, source_target_pairs={{0,2},{2,0},{4,6},{6,4},{8,10},{10,8},{12,14},{14,12},{16,18},{18,... | collective-permute-start | bytes 589832 | tf_op jit(solution)/shard_map/ppermute | solution.py:154
  51.6 7.7 %collective-permute-start.13 = (f32[3,32,512]{2,1,0:T(8,128)S(1)}, f32[3,32,512]{2,1,0:T(8,128)S(1)}, u32[]{:S(2)}, u32[]{:S(2)}) collective-permute-start(f32[3,32,512]{2,1,0:T(8,128)S(1)} %shard_map.60.refs_0_), channel_id=1, source_target_pairs={{0,2},{2,0},{4,6},{6,4},{8,10},{10,8},{12,14},{14,12},{16,18},{18,... | collective-permute-start | bytes 589832 | tf_op jit(solution)/shard_map/ppermute | solution.py:154
  52.2 7.2 %collective-permute-start.17 = (f32[3,32,512]{2,1,0:T(8,128)S(1)}, f32[3,32,512]{2,1,0:T(8,128)S(1)}, u32[]{:S(2)}, u32[]{:S(2)}) collective-permute-start(f32[3,32,512]{2,1,0:T(8,128)S(1)} %collective-permute-done.16.refs_4_), channel_id=1, source_target_pairs={{0,2},{2,0},{4,6},{6,4},{8,10},{10,8},{12,14},{14,12},{16,18},{18,... | collective-permute-start | bytes 589832 | tf_op jit(solution)/shard_map/ppermute | solution.py:154
  54.1 5.3 %collective-permute-start.15 = (f32[3,32,512]{2,1,0:T(8,128)S(1)}, f32[3,32,512]{2,1,0:T(8,128)S(1)}, u32[]{:S(2)}, u32[]{:S(2)}) collective-permute-start(f32[3,32,512]{2,1,0:T(8,128)S(1)} %collective-permute-done.14.refs_2_), channel_id=1, source_target_pairs={{0,2},{2,0},{4,6},{6,4},{8,10},{10,8},{12,14},{14,12},{16,18},{18,... | collective-permute-start | bytes 589832 | tf_op jit(solution)/shard_map/ppermute | solution.py:154
  57.8 1.6 %collective-permute-start.19 = (f32[3,32,512]{2,1,0:T(8,128)S(1)}, f32[3,32,512]{2,1,0:T(8,128)S(1)}, u32[]{:S(2)}, u32[]{:S(2)}) collective-permute-start(f32[3,32,512]{2,1,0:T(8,128)S(1)} %collective-permute-done.18.refs_6_), channel_id=1, source_target_pairs={{0,2},{2,0},{4,6},{6,4},{8,10},{10,8},{12,14},{14,12},{16,18},{18,... | collective-permute-start | bytes 589832 | tf_op jit(solution)/shard_map/ppermute | solution.py:154

commit v2 on v0

v2 whole, which is shorter than its diff:
```python
import functools

import jax
import jax.numpy as jnp
from jax import lax
from jax.experimental import pallas as pl
from jax.experimental.pallas import tpu as pltpu
from jax.sharding import PartitionSpec as P

PARTS = 2
VMEM = pl.BlockSpec(memory_space=pltpu.VMEM)
SMEM = pl.BlockSpec(memory_space=pltpu.SMEM)
ANY = pl.BlockSpec(memory_space=pl.ANY)


def call(kernel, out_shape, in_specs, operands, flops=0, scratch=()):
    outs = out_shape if isinstance(out_shape, tuple) else (out_shape,)
    moved = sum(x.size * x.dtype.itemsize for x in (*operands, *outs))
    return pl.pallas_call(
        kernel,
        out_shape=out_shape,
        in_specs=in_specs,
        out_specs=jax.tree.map(lambda _: VMEM, out_shape),
        scratch_shapes=scratch,
        cost_estimate=pl.CostEstimate(flops=flops, bytes_accessed=moved, transcendentals=0),
        compiler_params=pltpu.CompilerParams(vmem_limit_bytes=32 * 1024 * 1024),
    )(*operands)


def split(value):
    high = value.astype(jnp.bfloat16)
    low = (value - high.astype(jnp.float32)).astype(jnp.bfloat16)
    return high, low


def dot(left, right):
    return jnp.dot(left, right, preferred_element_type=jnp.float32)


def flag_kernel(group, few, owners, out):
    count = owners.shape[1]
    upper = jnp.int32(0)
    for number in range(count):
        upper += owners[0, number] // group
    many = jnp.where(jnp.maximum(upper, count - upper) > few, 1, 0)
    out[...] = jnp.full(out.shape, many, jnp.int32)


def copy_kernel(array, *refs):
    refs[-1][...] = array[...]


def gather_kernel(chips, own, got, *outs):
    parts, _, chunk, _ = outs[0].shape
    for step, out in enumerate(outs, 1):
        for part in range(parts):
            place = part * chips + step
            out[part, 0] = own[2 * place * chunk:(2 * place + 1) * chunk, :]
            out[part, 1] = got[place * chunk:(place + 1) * chunk, :]


def pick(part, chips, owners, own, got, pieces, outs):
    out, packed = outs[0], outs[1:]
    chunk = out.shape[1]
    group = 2 * chips
    index = lax.axis_index("row")
    first = part * chips * chunk
    before = jnp.int32(0)
    for number in range(out.shape[0]):
        owner = owners[0, number]
        mask = (owner % group) ^ (index % group)
        here = owner // group == index // group

        def put(read):
            out[number] = read()
            for ref in packed:
                for slot in range(min(number + 1, ref.shape[0])):

                    @pl.when(here & (before == slot))
                    def _():
                        ref[slot] = read()

        @pl.when(mask == 0)
        def _():
            put(lambda: own[2 * first:2 * first + chunk, :])

        @pl.when(mask == 1)
        def _():
            put(lambda: got[first:first + chunk, :])

        for step, piece in enumerate(pieces, 1):
            for core in range(2):

                @pl.when(mask == 2 * step + core)
                def _():
                    put(lambda: piece[part, core])

        before = jnp.where(here, before + 1, before)


def merge(group, owners, mine, other, out):
    half = lax.axis_index("row") // group
    packed = other.shape[0] < out.shape[0]
    before = jnp.int32(0)
    for number in range(out.shape[0]):
        here = owners[0, number] // group == half

        @pl.when(here)
        def _():
            out[number] = mine[number]

        if packed:
            for slot in range(min(number + 1, other.shape[0])):

                @pl.when(jnp.logical_not(here) & (before == slot))
                def _():
                    out[number] = other[slot]

            before = jnp.where(here, before, before + 1)
        else:

            @pl.when(jnp.logical_not(here))
            def _():
                out[number] = other[number]


def pick_kernel(chips, owners, own, got, *refs):
    pick(0, chips, owners, own, got, refs[:chips - 1], refs[chips - 1:])


def step_kernel(part, chips, owners, mine, other, own, got, *refs):
    pick(part, chips, owners, own, got, refs[:chips - 1], refs[chips:])
    merge(2 * chips, owners, mine, other, refs[chips - 1])


def merge_kernel(group, owners, mine, other, *refs):
    merge(group, owners, mine, other, refs[-1])


def right_kernel(offsets, *refs):
    sources, (right_high, right_low) = refs[:-2], refs[-2:]
    count = offsets.shape[0]
    width = right_high.shape[0] // count
    blocks = [ref.at[place:place + width] for ref in sources for place in range(0, ref.shape[0], width)]
    for number in range(count):
        lanes = slice(number * width, (number + 1) * width)
        for block, ref in enumerate(blocks):

            @pl.when(offsets[number] == block)
            def _():
                high, low = split(ref[...])
                right_high[lanes, :] = high
                right_low[lanes, :] = low


def multiply_kernel(part, group, owners, right_high, right_low, previous, *refs):
    pieces, early = refs[:group], refs[group:-3]
    out, left_high, left_low = refs[-3:]
    count, chunk, width = pieces[0].shape
    member = lax.axis_index("row") % group
    size = group * chunk
    for number in range(count):
        mask = (owners[0, number] % group) ^ member
        lanes = slice(number * width, (number + 1) * width)
        for step in range(group):
            place = pl.multiple_of((mask ^ step) * chunk, chunk)
            high, low = split(pieces[step][number])
            left_high[pl.ds(place, chunk), lanes] = high
            left_low[pl.ds(place, chunk), lanes] = low
    total = 2.0 * previous[part * size:(part + 1) * size, :] - (
        dot(left_high[...], right_low[...])
        + dot(left_low[...], right_high[...])
        + dot(left_high[...], right_high[...])
    )
    if out.shape[0] > size:
        for number, ref in enumerate(early):
            out[number * size:(number + 1) * size, :] = ref[...]
        out[part * size:, :] = total
    else:
        out[...] = total


def shards(left_slots, right, previous, offsets, owners):
    own = left_slots[0]
    rows, width = own.shape
    count = offsets.shape[0]
    devices = lax.axis_size("row")
    columns = lax.axis_size("col")
    group = devices // 2
    chips = group // 2
    size = rows // PARTS
    chunk = size // group
    few = (2 * count + 2) // 3

    def shape(*dims):
        return jax.ShapeDtypeStruct(dims, own.dtype)

    def swap(array, mask):
        return lax.ppermute(array, "row", [(i, i ^ mask) for i in range(devices)])

    def shift(array, distance):
        pairs = [((i + distance) % columns, i) for i in range(columns)]
        return lax.ppermute(array, "col", pairs)

    def copy(array, wait):
        return call(copy_kernel, jax.ShapeDtypeStruct(array.shape, array.dtype), [VMEM, ANY], (array, wait))

    got = swap(own.reshape(PARTS * chips, 2 * chunk, width)[:, chunk:].reshape(rows // 2, width), 1)
    sent = call(
        functools.partial(gather_kernel, chips),
        (shape(PARTS, 2, chunk, width),) * (chips - 1),
        [VMEM, VMEM],
        (own, got),
    )
    arrived = [swap(array, 2 * step) for step, array in enumerate(sent, 1)]

    flags = call(
        functools.partial(flag_kernel, group, few), jax.ShapeDtypeStruct((8, 128), jnp.int32), [SMEM], (owners,)
    )
    distance = 1
    while distance < columns:
        flags = flags | shift(flags, distance)
        distance *= 2

    rest = right.shape[0] - width
    last = right[rest:]
    last_blocks = [shift(last, distance) for distance in range(1, columns)]

    def finish(slots):
        packed = (shape(slots, chunk, width),) if slots < count else ()
        piece = shape(count, chunk, width)
        picked = call(
            functools.partial(pick_kernel, chips),
            (piece, *packed),
            [SMEM] + [VMEM] * (chips + 1),
            (owners, own, got, *arrived),
        )

        sources = [right]
        if rest:
            first_blocks = copy(right[:rest], picked[0])
        for distance, block in enumerate(last_blocks, 1):
            sources += [shift(first_blocks, distance), block] if rest else [block]
        terms = jax.ShapeDtypeStruct((count * width, right.shape[1]), jnp.bfloat16)
        right_terms = call(
            right_kernel, (terms, terms), [SMEM] + [VMEM] * len(sources), (offsets, *sources), flops=4 * terms.size
        )

        def spread(part, merged):
            pieces = {0: merged}
            bits = [1 << b for b in range(1, group.bit_length() - 1)]
            for bit in bits if part % 2 else reversed(bits):
                for s in list(pieces):
                    pieces[s + bit] = swap(pieces[s], bit)
            return pieces

        gathered = []
        for part in range(1, PARTS):
            merged, *following = call(
                functools.partial(step_kernel, part, chips),
                (piece, piece, *packed),
                [SMEM] + [VMEM] * (chips + 3),
                (owners, picked[0], swap(picked[-1], group), own, got, *arrived),
            )
            picked = following
            gathered.append(spread(part - 1, merged))
        wait = [array for pieces in gathered for s, array in pieces.items() if s]
        merged = call(
            functools.partial(merge_kernel, group),
            piece,
            [SMEM, VMEM, VMEM] + [ANY] * len(wait),
            (owners, picked[0], swap(picked[-1], group), *wait),
        )
        gathered.append(spread(PARTS - 1, merged))

        results = []
        for part, pieces in enumerate(gathered):
            for s in list(pieces):
                pieces[s + 1] = swap(pieces[s], 1)
            early = results if part == PARTS - 1 else []
            operands = (owners, *right_terms, previous, *[pieces[s] for s in range(group)], *early)
            results.append(call(
                functools.partial(multiply_kernel, part, group),
                jax.ShapeDtypeStruct((rows if early else size, right.shape[1]), previous.dtype),
                [SMEM] + [VMEM] * (len(operands) - 1),
                operands,
                flops=6 * size * count * width * right.shape[1],
                scratch=[pltpu.VMEM((size, count * width), jnp.bfloat16)] * 2,
            ))
        return results[-1]

    return lax.cond(flags[0, 0] == 0, lambda: finish(few), lambda: finish(count))


def solution(mesh):
    return jax.shard_map(
        shards,
        mesh=mesh,
        in_specs=(P("row", "col", None), P("col", "row"), P("col", "row"), P(), P("col", None)),
        out_specs=P("col", "row"),
        check_vma=False,
    )
```

time: 60.4 us -> 62.5 us (1.035)
  waiting for transfers between devices: 18.6 us -> 29.5 us
  starting transfers between devices: 32.8 us -> 22.6 us
  local copies, waits for them, and re-layouts: 1.19 us -> 2.62 us
  Pallas kernels: 7.42 us -> 6.77 us
    ppermute x23 -> x20, starting transfers between devices: 30.3 us -> 16.6 us  [swap(): return lax.ppermute(array, 'row', [(i, i ^ mask) for i in range(devices)])]
    ppermute x1 -> x3, waiting for transfers between devices: 0.01 us -> 6.63 us  [shift(): return lax.ppermute(array, 'col', pairs)]
    ppermute x23 -> x20, waiting for transfers between devices: 18.6 us -> 22.9 us  [swap(): return lax.ppermute(array, 'row', [(i, i ^ mask) for i in range(devices)])]
    pallas_call x2 -> x0, Pallas kernels: 3.89 us -> none  [shards(): pl.pallas_call(functools.partial(multiply_kernel, part), out_shape=out_sh...]
    ppermute x1 -> x3, starting transfers between devices: 2.56 us -> 5.97 us  [shift(): return lax.ppermute(array, 'col', pairs)]
    pallas_call x7 -> x9, Pallas kernels: 3.53 us -> 6.77 us  [call(): pl.pallas_call(kernel, out_shape=out_shape, in_specs=in_specs, out_specs=...]
    unnamed x10 -> x12, local copies, waits for them, and re-layouts: 0.03 us -> 0.81 us
    slice x1 -> x4, local copies, waits for them, and re-layouts: 1.17 us -> 1.81 us  [the longest x1 1.23 us: shards(): own.reshape(PARTS * chips, 2 * chunk, width)[:, chunk:]]
  transfers between devices with their start and end apart: 24 -> 23, of which waited for: 8 -> 8; matrix products, arithmetic and copies ran while one was open for 0% -> 1% of each run, Pallas kernels for 8% -> 6%
where the time goes in v2:
time: 62.5 us; the launch traced here: 62.4 us
  waiting for transfers between devices  29.5 us (47%)
  starting transfers between devices  22.6 us (36%)
  Pallas kernels  6.77 us (11%)
  local copies, waits for them, and re-layouts  2.62 us (4%)
  between operations  0.73 us (1%)
    ppermute x20, waiting for transfers between devices, swap(): return lax.ppermute(array, 'row', [(i, i ^ mask) for i in range(devices)])  22.9 us
    ppermute x20, starting transfers between devices, swap(): return lax.ppermute(array, 'row', [(i, i ^ mask) for i in range(devices)])  16.6 us
    pallas_call x9, Pallas kernels, call(): pl.pallas_call(kernel, out_shape=out_shape, in_specs=in_specs, out_specs=...  6.77 us
    ppermute x3, waiting for transfers between devices, shift(): return lax.ppermute(array, 'col', pairs)  6.63 us
    ppermute x3, starting transfers between devices, shift(): return lax.ppermute(array, 'col', pairs)  5.97 us
  transfers between devices with their start and end apart: 23, of which 8 were waited for; matrix products, arithmetic and copies ran while one was open for 1% of the time, Pallas kernels for 6%

profile of v2, /device:TPU:0, one launch (start us, length us, event | category | flops | bytes accessed | tf_op | source)
XLA Modules:
  0.0 62.4 jit_solution(3964493527767100847)
XLA Ops:
  0.0 1.2 %slice.18 = f32[8,32,512]{2,1,0:T(8,128)S(1)} slice(f32[8,64,512]{2,1,0:T(8,128)} %bitcast.4), slice={[0:8], [32:64], [0:512]} | slice | bytes 1048576 | tf_op jit(solution)/shard_map/slice | solution.py:208
  1.2 0.5 collective-permute-start.35
  1.8 0.0 copy-done.1
  1.8 2.6 %collective-permute-start.39 = (f32[512,256]{1,0:T(8,128)S(1)}, f32[512,256]{1,0:T(8,128)S(1)}, u32[]{:S(2)}, u32[]{:S(2)}) collective-permute-start(f32[512,256]{1,0:T(8,128)S(1)} %slice.17), channel_id=1, source_target_pairs={{1,0},{0,1},{3,2},{2,3},{5,4},{4,5},{7,6},{6,7},{9,8},{8,9},{11,10... | collective-permute-start | bytes 1572872 | tf_op jit(solution)/shard_map/ppermute | solution.py:203
  4.4 0.0 collective-permute-done.35.got
  4.4 0.0 copy-done
  4.4 0.1 shard_map.62
  4.5 1.8 %collective-permute-start.36 = (f32[2,2,32,512]{3,2,1,0:T(8,128)S(1)}, f32[2,2,32,512]{3,2,1,0:T(8,128)S(1)}, u32[]{:S(2)}, u32[]{:S(2)}) collective-permute-start(f32[2,2,32,512]{3,2,1,0:T(8,128)S(1)} %get-tuple-element.82), channel_id=1, source_target_pairs={{0,4},{2,6},{4,0},{6,2},{8,12},{10,14},{12,8},{14,10},{16,20},{18,... | collective-permute-start | bytes 786440 | tf_op jit(solution)/shard_map/ppermute | solution.py:199
  6.3 1.6 %collective-permute-start.37 = (f32[2,2,32,512]{3,2,1,0:T(8,128)S(1)}, f32[2,2,32,512]{3,2,1,0:T(8,128)S(1)}, u32[]{:S(2)}, u32[]{:S(2)}) collective-permute-start(f32[2,2,32,512]{3,2,1,0:T(8,128)S(1)} %get-tuple-element.83), channel_id=1, source_target_pairs={{0,8},{2,10},{4,12},{6,14},{8,0},{10,2},{12,4},{14,6},{16,24},{18,... | collective-permute-start | bytes 786440 | tf_op jit(solution)/shard_map/ppermute | solution.py:199
  7.9 0.2 collective-permute-start.38
  8.0 0.0 copy-done.4
  8.1 0.6 shard_map.61
  8.6 1.8 %collective-permute-start.34 = (s32[8,128]{1,0:T(8,128)S(1)}, s32[8,128]{1,0:T(8,128)S(1)}, u32[]{:S(2)}, u32[]{:S(2)}) collective-permute-start(s32[8,128]{1,0:T(8,128)S(1)} %shard_map.61), channel_id=1, source_target_pairs={{1,0},{0,1},{3,2},{2,3},{5,4},{4,5},{7,6},{6,7},{9,8},{8,9},{11,10... | collective-permute-start | bytes 12296 | tf_op jit(solution)/shard_map/ppermute | solution.py:203
  10.4 6.6 %collective-permute-done.34 = s32[8,128]{1,0:T(8,128)S(1)} collective-permute-done((s32[8,128]{1,0:T(8,128)S(1)}, s32[8,128]{1,0:T(8,128)S(1)}, u32[]{:S(2)}, u32[]{:S(2)}) %collective-permute-start.34) | collective-permute-done | bytes 4128 | tf_op jit(solution)/shard_map/ppermute | solution.py:203
  17.0 0.5 slice.15
  18.2 0.0 copy-start.5
  18.2 0.0 collective-permute-done.39
  18.2 0.0 collective-permute-done.36
  18.2 0.0 collective-permute-done.37
  18.2 1.5 %collective-permute-done.38 = f32[2,2,32,512]{3,2,1,0:T(8,128)S(1)} collective-permute-done((f32[2,2,32,512]{3,2,1,0:T(8,128)S(1)}, f32[2,2,32,512]{3,2,1,0:T(8,128)S(1)}, u32[]{:S(2)}, u32[]{:S(2)}) %collective-permute-start.38) | collective-permute-done | bytes 262176 | tf_op jit(solution)/shard_map/ppermute | solution.py:199
  19.8 0.0 copy-done.5
  19.8 41.7 %conditional.1 = (f32[512,256]{1,0:T(8,128)S(1)}) conditional(s32[]{:T(128)} %bitcast, (f32[1024,256]{1,0:T(8,128)S(1)}, s32[1,3]{1,0:T(1,128)S(1)}, f32[512,512]{1,0:T(8,128)S(1)}, f32[256,512]{1,0:T(8,128)S(1)}, f32[2,2,32,512]{3,2,1,0:T(8,128)S(1)}, /*index=5*/f32[2,2,32,512]{3,2,1,0:T(8,128)S(1)}, f32[2,2,32,512]{3,2,1,0:T(8,128)S(1)}, ...), branch_computations={%region_0.0_spmd, %region_1.0_spmd} | conditional | flops 1209532416 | bytes 35914488 | solution.py:292
  19.8 0.7 %branch_1_fun.7 = (f32[3,32,512]{2,1,0:T(8,128)S(1)}, f32[2,32,512]{2,1,0:T(8,128)S(1)}) custom-call(s32[1,3]{1,0:T(1,128)S(1)} %get-tuple-element.62.owners, f32[512,512]{1,0:T(8,128)S(1)} %get-tuple-element.65.own, f32[256,512]{1,0:T(8,128)S(1)} %get-tuple-element.66.got, f32[2,2,32,512]{3,2,1,0:T(8,128)S(1)} %get-tuple-element.67.refs_0_, ...), custom_call_target="tpu_custom_call" | custom-call | bytes 2686988 | tf_op jit(solution)/shard_map/cond/branch_1_fun/pallas_call | solution.py:19
  20.5 2.8 %collective-permute-start.18 = (f32[2,32,512]{2,1,0:T(8,128)S(1)}, f32[2,32,512]{2,1,0:T(8,128)S(1)}, u32[]{:S(2)}, u32[]{:S(2)}) collective-permute-start(f32[2,32,512]{2,1,0:T(8,128)S(1)} %get-tuple-element.75), channel_id=1, source_target_pairs={{0,16},{2,18},{4,20},{6,22},{8,24},{10,26},{12,28},{14,30},{16,0},... | collective-permute-start | bytes 393224 | tf_op jit(solution)/shard_map/cond/branch_1_fun/ppermute | solution.py:199
  23.3 5.5 %collective-permute-done.18.other = f32[2,32,512]{2,1,0:T(8,128)S(1)} collective-permute-done((f32[2,32,512]{2,1,0:T(8,128)S(1)}, f32[2,32,512]{2,1,0:T(8,128)S(1)}, u32[]{:S(2)}, u32[]{:S(2)}) %collective-permute-start.18) | collective-permute-done | bytes 131104 | tf_op jit(solution)/shard_map/cond/branch_1_fun/ppermute | solution.py:199
  28.8 0.8 %branch_1_fun.10 = (f32[3,32,512]{2,1,0:T(8,128)S(1)}, f32[3,32,512]{2,1,0:T(8,128)S(1)}, f32[2,32,512]{2,1,0:T(8,128)S(1)}) custom-call(s32[1,3]{1,0:T(1,128)S(1)} %get-tuple-element.62.owners, f32[3,32,512]{2,1,0:T(8,128)S(1)} %get-tuple-element.70.refs_0_.mine, f32[2,32,512]{2,1,0:T(8,128)S(1)} %collective-permute-done.18.other, ...), custom_call_target="tpu_custom_call" | custom-call | bytes 3211276 | tf_op jit(solution)/shard_map/cond/branch_1_fun/pallas_call | solution.py:19
  29.6 0.8 %collective-permute-start.20 = (f32[3,32,512]{2,1,0:T(8,128)S(1)}, f32[3,32,512]{2,1,0:T(8,128)S(1)}, u32[]{:S(2)}, u32[]{:S(2)}) collective-permute-start(f32[3,32,512]{2,1,0:T(8,128)S(1)} %get-tuple-element.78.refs_0_), channel_id=1, source_target_pairs={{0,8},{2,10},{4,12},{6,14},{8,0},{10,2},{12,4},{14,6},{16,24},{18,... | collective-permute-start | bytes 589832 | tf_op jit(solution)/shard_map/cond/branch_1_fun/ppermute | solution.py:199
  30.4 1.5 %collective-permute-start.21 = (f32[3,32,512]{2,1,0:T(8,128)S(1)}, f32[3,32,512]{2,1,0:T(8,128)S(1)}, u32[]{:S(2)}, u32[]{:S(2)}) collective-permute-start(f32[3,32,512]{2,1,0:T(8,128)S(1)} %get-tuple-element.78.refs_0_), channel_id=1, source_target_pairs={{0,4},{2,6},{4,0},{6,2},{8,12},{10,14},{12,8},{14,10},{16,20},{18,... | collective-permute-start | bytes 589832 | tf_op jit(solution)/shard_map/cond/branch_1_fun/ppermute | solution.py:199
  31.9 3.4 %collective-permute-done.20.refs_0_.refs_4_ = f32[3,32,512]{2,1,0:T(8,128)S(1)} collective-permute-done((f32[3,32,512]{2,1,0:T(8,128)S(1)}, f32[3,32,512]{2,1,0:T(8,128)S(1)}, u32[]{:S(2)}, u32[]{:S(2)}) %collective-permute-start.20) | collective-permute-done | bytes 196640 | tf_op jit(solution)/shard_map/cond/branch_1_fun/ppermute | solution.py:199
  35.3 1.6 %collective-permute-start.22 = (f32[3,32,512]{2,1,0:T(8,128)S(1)}, f32[3,32,512]{2,1,0:T(8,128)S(1)}, u32[]{:S(2)}, u32[]{:S(2)}) collective-permute-start(f32[3,32,512]{2,1,0:T(8,128)S(1)} %collective-permute-done.20.refs_0_.refs_4_), channel_id=1, source_target_pairs={{0,4},{2,6},{4,0},{6,2},{8,12},{10,14},{12,8},{14,10},{16,20},{18,... | collective-permute-start | bytes 589832 | tf_op jit(solution)/shard_map/cond/branch_1_fun/ppermute | solution.py:199
  36.9 2.9 %collective-permute-start.19 = (f32[2,32,512]{2,1,0:T(8,128)S(1)}, f32[2,32,512]{2,1,0:T(8,128)S(1)}, u32[]{:S(2)}, u32[]{:S(2)}) collective-permute-start(f32[2,32,512]{2,1,0:T(8,128)S(1)} %get-tuple-element.77), channel_id=1, source_target_pairs={{0,16},{2,18},{4,20},{6,22},{8,24},{10,26},{12,28},{14,30},{16,0},... | collective-permute-start | bytes 393224 | tf_op jit(solution)/shard_map/cond/branch_1_fun/ppermute | solution.py:199
  39.8 1.6 %collective-permute-start.17 = (f32[512,256]{1,0:T(8,128)S(1)}, f32[512,256]{1,0:T(8,128)S(1)}, u32[]{:S(2)}, u32[]{:S(2)}) collective-permute-start(f32[512,256]{1,0:T(8,128)S(1)} %branch_1_fun.8), channel_id=1, source_target_pairs={{1,0},{0,1},{3,2},{2,3},{5,4},{4,5},{7,6},{6,7},{9,8},{8,9},{11,10... | collective-permute-start | bytes 1572872 | tf_op jit(solution)/shard_map/cond/branch_1_fun/ppermute | solution.py:203
  41.4 0.0 collective-permute-start.30
  41.4 3.3 %collective-permute-done.19.other = f32[2,32,512]{2,1,0:T(8,128)S(1)} collective-permute-done((f32[2,32,512]{2,1,0:T(8,128)S(1)}, f32[2,32,512]{2,1,0:T(8,128)S(1)}, u32[]{:S(2)}, u32[]{:S(2)}) %collective-permute-start.19) | collective-permute-done | bytes 131104 | tf_op jit(solution)/shard_map/cond/branch_1_fun/ppermute | solution.py:199
  44.7 0.0 collective-permute-done.21.refs_1_.refs_2_
  44.7 0.0 collective-permute-done.22.refs_2_.refs_6_
  44.8 0.6 branch_1_fun.11.refs_0_
  45.4 0.6 collective-permute-start.24
  45.9 0.0 collective-permute-start.32
  46.0 0.5 collective-permute-start.31
  46.5 0.0 collective-permute-done.30.refs_1_
  46.5 0.7 %collective-permute-start.26 = (f32[3,32,512]{2,1,0:T(8,128)S(1)}, f32[3,32,512]{2,1,0:T(8,128)S(1)}, u32[]{:S(2)}, u32[]{:S(2)}) collective-permute-start(f32[3,32,512]{2,1,0:T(8,128)S(1)} %branch_1_fun.11.refs_0_), channel_id=1, source_target_pairs={{0,8},{2,10},{4,12},{6,14},{8,0},{10,2},{12,4},{14,6},{16,24},{18,... | collective-permute-start | bytes 589832 | tf_op jit(solution)/shard_map/cond/branch_1_fun/ppermute | solution.py:199
  47.2 4.0 %collective-permute-done.24.refs_2_ = f32[3,32,512]{2,1,0:T(8,128)S(1)} collective-permute-done((f32[3,32,512]{2,1,0:T(8,128)S(1)}, f32[3,32,512]{2,1,0:T(8,128)S(1)}, u32[]{:S(2)}, u32[]{:S(2)}) %collective-permute-start.24) | collective-permute-done | bytes 196640 | tf_op jit(solution)/shard_map/cond/branch_1_fun/ppermute | solution.py:199
  51.1 0.7 %collective-permute-start.28 = (f32[3,32,512]{2,1,0:T(8,128)S(1)}, f32[3,32,512]{2,1,0:T(8,128)S(1)}, u32[]{:S(2)}, u32[]{:S(2)}) collective-permute-start(f32[3,32,512]{2,1,0:T(8,128)S(1)} %collective-permute-done.24.refs_2_), channel_id=1, source_target_pairs={{0,8},{2,10},{4,12},{6,14},{8,0},{10,2},{12,4},{14,6},{16,24},{18,... | collective-permute-start | bytes 589832 | tf_op jit(solution)/shard_map/cond/branch_1_fun/ppermute | solution.py:199
  51.8 0.0 collective-permute-done.32.refs_5_
  51.8 0.0 collective-permute-start.33
  51.8 0.0 collective-permute-done.31.refs_3_
  51.8 0.5 collective-permute-start.23
  52.3 0.0 collective-permute-done.17.refs_1_
  52.3 0.1 collective-permute-start.25
  52.4 1.8 %collective-permute-done.26.refs_4_ = f32[3,32,512]{2,1,0:T(8,128)S(1)} collective-permute-done((f32[3,32,512]{2,1,0:T(8,128)S(1)}, f32[3,32,512]{2,1,0:T(8,128)S(1)}, u32[]{:S(2)}, u32[]{:S(2)}) %collective-permute-start.26) | collective-permute-done | bytes 196640 | tf_op jit(solution)/shard_map/cond/branch_1_fun/ppermute | solution.py:199
  54.2 0.0 collective-permute-start.27
  54.2 3.2 %collective-permute-done.28.refs_6_ = f32[3,32,512]{2,1,0:T(8,128)S(1)} collective-permute-done((f32[3,32,512]{2,1,0:T(8,128)S(1)}, f32[3,32,512]{2,1,0:T(8,128)S(1)}, u32[]{:S(2)}, u32[]{:S(2)}) %collective-permute-start.28) | collective-permute-done | bytes 196640 | tf_op jit(solution)/shard_map/cond/branch_1_fun/ppermute | solution.py:199
  57.5 0.0 collective-permute-start.29
  57.5 0.9 %branch_1_fun.9 = (bf16[1536,256]{1,0:T(8,128)(2,1)S(1)}, bf16[1536,256]{1,0:T(8,128)(2,1)S(1)}) custom-call(s32[3]{0:T(128)S(1)} %get-tuple-element.91.offsets, f32[1024,256]{1,0:T(8,128)S(1)} %get-tuple-element.64.refs_0_, f32[512,256]{1,0:T(8,128)S(1)} %collective-permute-done.17.refs_1_, f32[512,256]{1,0:T(8,128)S(1)} %get-tuple-element.71.refs_2_), custom_call_target="tpu_custom_call" | custom-call | flops 1572864 | bytes 3670028 | tf_op jit(solution)/shard_map/cond/branch_1_fun/pallas_call | solution.py:19
  58.4 0.0 collective-permute-done.33.refs_7_
  58.4 1.5 %branch_1_fun.12.refs_8_ = f32[256,256]{1,0:T(8,128)S(1)} custom-call(s32[1,3]{1,0:T(1,128)S(1)} %get-tuple-element.62.owners, bf16[1536,256]{1,0:T(8,128)(2,1)S(1)} %get-tuple-element.72.right_high, bf16[1536,256]{1,0:T(8,128)(2,1)S(1)} %get-tuple-element.73.right_low, f32[512,256]{1,0:T(8,128)S(1)} %get-tuple-element.93.previous, ...), custom_call_target="tpu_custom_call" | custom-call | flops 603979776 | bytes 3932172 | tf_op jit(solution)/shard_map/cond/branch_1_fun/pallas_call | solution.py:19
  60.0 0.0 collective-permute-done.23.refs_1_
  60.0 0.0 collective-permute-done.25.refs_3_
  60.0 0.0 collective-permute-done.27.refs_5_
  60.0 0.0 collective-permute-done.29.refs_7_
  60.0 1.5 %branch_1_fun.13 = f32[512,256]{1,0:T(8,128)S(1)} custom-call(s32[1,3]{1,0:T(1,128)S(1)} %get-tuple-element.62.owners, bf16[1536,256]{1,0:T(8,128)(2,1)S(1)} %get-tuple-element.72.right_high, bf16[1536,256]{1,0:T(8,128)(2,1)S(1)} %get-tuple-element.73.right_low, f32[512,256]{1,0:T(8,128)S(1)} %get-tuple-element.93.previous, ...), custom_call_target="tpu_custom_call" | custom-call | flops 603979776 | bytes 4456460 | tf_op jit(solution)/shard_map/cond/branch_1_fun/pallas_call | solution.py:19
  61.6 0.0 copy-start.3
  61.6 0.8 %copy-done.3 = f32[512,256]{1,0:T(8,128)} copy-done((f32[512,256]{1,0:T(8,128)}, f32[512,256]{1,0:T(8,128)S(1)}, u32[]{:S(2)}) %copy-start.3) | copy-done | bytes 524312
  (9 shorter events, 0.1 us)
Async XLA Ops:
  0.0 1.8 %copy-start.1 = (f32[1024,256]{1,0:T(8,128)S(1)}, f32[1024,256]{1,0:T(8,128)}, u32[]{:S(2)}) copy-start(f32[1024,256]{1,0:T(8,128)} %param.8) | copy-start | bytes 3145732
  0.0 4.4 %copy-start = (f32[1,512,512]{2,1,0:T(8,128)S(1)}, f32[1,512,512]{2,1,0:T(8,128)}, u32[]{:S(2)}) copy-start(f32[1,512,512]{2,1,0:T(8,128)} %param.7) | copy-start | bytes 3145732
  1.2 3.2 %collective-permute-start.35 = (f32[256,512]{1,0:T(8,128)S(1)}, f32[256,512]{1,0:T(8,128)S(1)}, u32[]{:S(2)}, u32[]{:S(2)}) collective-permute-start(f32[256,512]{1,0:T(8,128)S(1)} %bitcast.8), channel_id=1, source_target_pairs={{0,2},{2,0},{4,6},{6,4},{8,10},{10,8},{12,14},{14,12},{16,18},{18,... | collective-permute-start | bytes 1572872 | tf_op jit(solution)/shard_map/ppermute | solution.py:199
  1.8 16.4 %collective-permute-start.39 = (f32[512,256]{1,0:T(8,128)S(1)}, f32[512,256]{1,0:T(8,128)S(1)}, u32[]{:S(2)}, u32[]{:S(2)}) collective-permute-start(f32[512,256]{1,0:T(8,128)S(1)} %slice.17), channel_id=1, source_target_pairs={{1,0},{0,1},{3,2},{2,3},{5,4},{4,5},{7,6},{6,7},{9,8},{8,9},{11,10... | collective-permute-start | bytes 1572872 | tf_op jit(solution)/shard_map/ppermute | solution.py:203
  4.4 15.4 %copy-start.2 = (f32[512,256]{1,0:T(8,128)S(1)}, f32[512,256]{1,0:T(8,128)}, u32[]{:S(2)}) copy-start(f32[512,256]{1,0:T(8,128)} %param.9) | copy-start | bytes 1572868
  4.5 13.7 %collective-permute-start.36 = (f32[2,2,32,512]{3,2,1,0:T(8,128)S(1)}, f32[2,2,32,512]{3,2,1,0:T(8,128)S(1)}, u32[]{:S(2)}, u32[]{:S(2)}) collective-permute-start(f32[2,2,32,512]{3,2,1,0:T(8,128)S(1)} %get-tuple-element.82), channel_id=1, source_target_pairs={{0,4},{2,6},{4,0},{6,2},{8,12},{10,14},{12,8},{14,10},{16,20},{18,... | collective-permute-start | bytes 786440 | tf_op jit(solution)/shard_map/ppermute | solution.py:199
  6.3 1.7 %copy-start.4 = (s32[1,3]{1,0:T(1,128)S(1)}, s32[1,3]{1,0:T(1,128)}, u32[]{:S(2)}) copy-start(s32[1,3]{1,0:T(1,128)} %owners.1) | copy-start | bytes 40
  6.3 11.9 %collective-permute-start.37 = (f32[2,2,32,512]{3,2,1,0:T(8,128)S(1)}, f32[2,2,32,512]{3,2,1,0:T(8,128)S(1)}, u32[]{:S(2)}, u32[]{:S(2)}) collective-permute-start(f32[2,2,32,512]{3,2,1,0:T(8,128)S(1)} %get-tuple-element.83), channel_id=1, source_target_pairs={{0,8},{2,10},{4,12},{6,14},{8,0},{10,2},{12,4},{14,6},{16,24},{18,... | collective-permute-start | bytes 786440 | tf_op jit(solution)/shard_map/ppermute | solution.py:199
  7.9 11.9 %collective-permute-start.38 = (f32[2,2,32,512]{3,2,1,0:T(8,128)S(1)}, f32[2,2,32,512]{3,2,1,0:T(8,128)S(1)}, u32[]{:S(2)}, u32[]{:S(2)}) collective-permute-start(f32[2,2,32,512]{3,2,1,0:T(8,128)S(1)} %get-tuple-element.84), channel_id=1, source_target_pairs={{0,12},{2,14},{4,8},{6,10},{8,4},{10,6},{12,0},{14,2},{16,28},{18,... | collective-permute-start | bytes 786440 | tf_op jit(solution)/shard_map/ppermute | solution.py:199
  8.6 8.4 %collective-permute-start.34 = (s32[8,128]{1,0:T(8,128)S(1)}, s32[8,128]{1,0:T(8,128)S(1)}, u32[]{:S(2)}, u32[]{:S(2)}) collective-permute-start(s32[8,128]{1,0:T(8,128)S(1)} %shard_map.61), channel_id=1, source_target_pairs={{1,0},{0,1},{3,2},{2,3},{5,4},{4,5},{7,6},{6,7},{9,8},{8,9},{11,10... | collective-permute-start | bytes 12296 | tf_op jit(solution)/shard_map/ppermute | solution.py:203
  18.2 1.6 %copy-start.5 = (s32[3]{0:T(128)S(1)}, s32[3]{0:T(128)}, u32[]{:S(2)}) copy-start(s32[3]{0:T(128)} %param.10) | copy-start | bytes 40
  20.5 8.3 %collective-permute-start.18 = (f32[2,32,512]{2,1,0:T(8,128)S(1)}, f32[2,32,512]{2,1,0:T(8,128)S(1)}, u32[]{:S(2)}, u32[]{:S(2)}) collective-permute-start(f32[2,32,512]{2,1,0:T(8,128)S(1)} %get-tuple-element.75), channel_id=1, source_target_pairs={{0,16},{2,18},{4,20},{6,22},{8,24},{10,26},{12,28},{14,30},{16,0},... | collective-permute-start | bytes 393224 | tf_op jit(solution)/shard_map/cond/branch_1_fun/ppermute | solution.py:199
  29.6 5.7 %collective-permute-start.20 = (f32[3,32,512]{2,1,0:T(8,128)S(1)}, f32[3,32,512]{2,1,0:T(8,128)S(1)}, u32[]{:S(2)}, u32[]{:S(2)}) collective-permute-start(f32[3,32,512]{2,1,0:T(8,128)S(1)} %get-tuple-element.78.refs_0_), channel_id=1, source_target_pairs={{0,8},{2,10},{4,12},{6,14},{8,0},{10,2},{12,4},{14,6},{16,24},{18,... | collective-permute-start | bytes 589832 | tf_op jit(solution)/shard_map/cond/branch_1_fun/ppermute | solution.py:199
  30.4 14.4 %collective-permute-start.21 = (f32[3,32,512]{2,1,0:T(8,128)S(1)}, f32[3,32,512]{2,1,0:T(8,128)S(1)}, u32[]{:S(2)}, u32[]{:S(2)}) collective-permute-start(f32[3,32,512]{2,1,0:T(8,128)S(1)} %get-tuple-element.78.refs_0_), channel_id=1, source_target_pairs={{0,4},{2,6},{4,0},{6,2},{8,12},{10,14},{12,8},{14,10},{16,20},{18,... | collective-permute-start | bytes 589832 | tf_op jit(solution)/shard_map/cond/branch_1_fun/ppermute | solution.py:199
  35.3 9.4 %collective-permute-start.22 = (f32[3,32,512]{2,1,0:T(8,128)S(1)}, f32[3,32,512]{2,1,0:T(8,128)S(1)}, u32[]{:S(2)}, u32[]{:S(2)}) collective-permute-start(f32[3,32,512]{2,1,0:T(8,128)S(1)} %collective-permute-done.20.refs_0_.refs_4_), channel_id=1, source_target_pairs={{0,4},{2,6},{4,0},{6,2},{8,12},{10,14},{12,8},{14,10},{16,20},{18,... | collective-permute-start | bytes 589832 | tf_op jit(solution)/shard_map/cond/branch_1_fun/ppermute | solution.py:199
  36.9 7.8 %collective-permute-start.19 = (f32[2,32,512]{2,1,0:T(8,128)S(1)}, f32[2,32,512]{2,1,0:T(8,128)S(1)}, u32[]{:S(2)}, u32[]{:S(2)}) collective-permute-start(f32[2,32,512]{2,1,0:T(8,128)S(1)} %get-tuple-element.77), channel_id=1, source_target_pairs={{0,16},{2,18},{4,20},{6,22},{8,24},{10,26},{12,28},{14,30},{16,0},... | collective-permute-start | bytes 393224 | tf_op jit(solution)/shard_map/cond/branch_1_fun/ppermute | solution.py:199
  39.8 12.5 %collective-permute-start.17 = (f32[512,256]{1,0:T(8,128)S(1)}, f32[512,256]{1,0:T(8,128)S(1)}, u32[]{:S(2)}, u32[]{:S(2)}) collective-permute-start(f32[512,256]{1,0:T(8,128)S(1)} %branch_1_fun.8), channel_id=1, source_target_pairs={{1,0},{0,1},{3,2},{2,3},{5,4},{4,5},{7,6},{6,7},{9,8},{8,9},{11,10... | collective-permute-start | bytes 1572872 | tf_op jit(solution)/shard_map/cond/branch_1_fun/ppermute | solution.py:203
  41.4 5.1 %collective-permute-start.30 = (f32[3,32,512]{2,1,0:T(8,128)S(1)}, f32[3,32,512]{2,1,0:T(8,128)S(1)}, u32[]{:S(2)}, u32[]{:S(2)}) collective-permute-start(f32[3,32,512]{2,1,0:T(8,128)S(1)} %get-tuple-element.78.refs_0_), channel_id=1, source_target_pairs={{0,2},{2,0},{4,6},{6,4},{8,10},{10,8},{12,14},{14,12},{16,18},{18,... | collective-permute-start | bytes 589832 | tf_op jit(solution)/shard_map/cond/branch_1_fun/ppermute | solution.py:199
  45.4 5.7 %collective-permute-start.24 = (f32[3,32,512]{2,1,0:T(8,128)S(1)}, f32[3,32,512]{2,1,0:T(8,128)S(1)}, u32[]{:S(2)}, u32[]{:S(2)}) collective-permute-start(f32[3,32,512]{2,1,0:T(8,128)S(1)} %branch_1_fun.11.refs_0_), channel_id=1, source_target_pairs={{0,4},{2,6},{4,0},{6,2},{8,12},{10,14},{12,8},{14,10},{16,20},{18,... | collective-permute-start | bytes 589832 | tf_op jit(solution)/shard_map/cond/branch_1_fun/ppermute | solution.py:199
  45.9 5.9 %collective-permute-start.32 = (f32[3,32,512]{2,1,0:T(8,128)S(1)}, f32[3,32,512]{2,1,0:T(8,128)S(1)}, u32[]{:S(2)}, u32[]{:S(2)}) collective-permute-start(f32[3,32,512]{2,1,0:T(8,128)S(1)} %collective-permute-done.20.refs_0_.refs_4_), channel_id=1, source_target_pairs={{0,2},{2,0},{4,6},{6,4},{8,10},{10,8},{12,14},{14,12},{16,18},{18,... | collective-permute-start | bytes 589832 | tf_op jit(solution)/shard_map/cond/branch_1_fun/ppermute | solution.py:199
  46.0 5.9 %collective-permute-start.31 = (f32[3,32,512]{2,1,0:T(8,128)S(1)}, f32[3,32,512]{2,1,0:T(8,128)S(1)}, u32[]{:S(2)}, u32[]{:S(2)}) collective-permute-start(f32[3,32,512]{2,1,0:T(8,128)S(1)} %collective-permute-done.21.refs_1_.refs_2_), channel_id=1, source_target_pairs={{0,2},{2,0},{4,6},{6,4},{8,10},{10,8},{12,14},{14,12},{16,18},{18,... | collective-permute-start | bytes 589832 | tf_op jit(solution)/shard_map/cond/branch_1_fun/ppermute | solution.py:199
  46.5 7.8 %collective-permute-start.26 = (f32[3,32,512]{2,1,0:T(8,128)S(1)}, f32[3,32,512]{2,1,0:T(8,128)S(1)}, u32[]{:S(2)}, u32[]{:S(2)}) collective-permute-start(f32[3,32,512]{2,1,0:T(8,128)S(1)} %branch_1_fun.11.refs_0_), channel_id=1, source_target_pairs={{0,8},{2,10},{4,12},{6,14},{8,0},{10,2},{12,4},{14,6},{16,24},{18,... | collective-permute-start | bytes 589832 | tf_op jit(solution)/shard_map/cond/branch_1_fun/ppermute | solution.py:199
  51.1 6.4 %collective-permute-start.28 = (f32[3,32,512]{2,1,0:T(8,128)S(1)}, f32[3,32,512]{2,1,0:T(8,128)S(1)}, u32[]{:S(2)}, u32[]{:S(2)}) collective-permute-start(f32[3,32,512]{2,1,0:T(8,128)S(1)} %collective-permute-done.24.refs_2_), channel_id=1, source_target_pairs={{0,8},{2,10},{4,12},{6,14},{8,0},{10,2},{12,4},{14,6},{16,24},{18,... | collective-permute-start | bytes 589832 | tf_op jit(solution)/shard_map/cond/branch_1_fun/ppermute | solution.py:199
  51.8 6.6 %collective-permute-start.33 = (f32[3,32,512]{2,1,0:T(8,128)S(1)}, f32[3,32,512]{2,1,0:T(8,128)S(1)}, u32[]{:S(2)}, u32[]{:S(2)}) collective-permute-start(f32[3,32,512]{2,1,0:T(8,128)S(1)} %collective-permute-done.22.refs_2_.refs_6_), channel_id=1, source_target_pairs={{0,2},{2,0},{4,6},{6,4},{8,10},{10,8},{12,14},{14,12},{16,18},{18,... | collective-permute-start | bytes 589832 | tf_op jit(solution)/shard_map/cond/branch_1_fun/ppermute | solution.py:199
  51.8 8.1 %collective-permute-start.23 = (f32[3,32,512]{2,1,0:T(8,128)S(1)}, f32[3,32,512]{2,1,0:T(8,128)S(1)}, u32[]{:S(2)}, u32[]{:S(2)}) collective-permute-start(f32[3,32,512]{2,1,0:T(8,128)S(1)} %branch_1_fun.11.refs_0_), channel_id=1, source_target_pairs={{0,2},{2,0},{4,6},{6,4},{8,10},{10,8},{12,14},{14,12},{16,18},{18,... | collective-permute-start | bytes 589832 | tf_op jit(solution)/shard_map/cond/branch_1_fun/ppermute | solution.py:199
  52.3 7.6 %collective-permute-start.25 = (f32[3,32,512]{2,1,0:T(8,128)S(1)}, f32[3,32,512]{2,1,0:T(8,128)S(1)}, u32[]{:S(2)}, u32[]{:S(2)}) collective-permute-start(f32[3,32,512]{2,1,0:T(8,128)S(1)} %collective-permute-done.24.refs_2_), channel_id=1, source_target_pairs={{0,2},{2,0},{4,6},{6,4},{8,10},{10,8},{12,14},{14,12},{16,18},{18,... | collective-permute-start | bytes 589832 | tf_op jit(solution)/shard_map/cond/branch_1_fun/ppermute | solution.py:199
  54.2 5.7 %collective-permute-start.27 = (f32[3,32,512]{2,1,0:T(8,128)S(1)}, f32[3,32,512]{2,1,0:T(8,128)S(1)}, u32[]{:S(2)}, u32[]{:S(2)}) collective-permute-start(f32[3,32,512]{2,1,0:T(8,128)S(1)} %collective-permute-done.26.refs_4_), channel_id=1, source_target_pairs={{0,2},{2,0},{4,6},{6,4},{8,10},{10,8},{12,14},{14,12},{16,18},{18,... | collective-permute-start | bytes 589832 | tf_op jit(solution)/shard_map/cond/branch_1_fun/ppermute | solution.py:199
  57.5 2.5 %collective-permute-start.29 = (f32[3,32,512]{2,1,0:T(8,128)S(1)}, f32[3,32,512]{2,1,0:T(8,128)S(1)}, u32[]{:S(2)}, u32[]{:S(2)}) collective-permute-start(f32[3,32,512]{2,1,0:T(8,128)S(1)} %collective-permute-done.28.refs_6_), channel_id=1, source_target_pairs={{0,2},{2,0},{4,6},{6,4},{8,10},{10,8},{12,14},{14,12},{16,18},{18,... | collective-permute-start | bytes 589832 | tf_op jit(solution)/shard_map/cond/branch_1_fun/ppermute | solution.py:199
  61.6 0.8 %copy-start.3 = (f32[512,256]{1,0:T(8,128)}, f32[512,256]{1,0:T(8,128)S(1)}, u32[]{:S(2)}) copy-start(f32[512,256]{1,0:T(8,128)S(1)} %get-tuple-element.173) | copy-start | bytes 1572868

commit v3 on v0

--- a/solution.py
+++ b/solution.py
@@ -66,7 +66,8 @@
                     out[number] = piece[core]
 
 
-def merge_kernel(group, owners, mine, other, out):
+def merge_kernel(group, owners, mine, other, *refs):
+    out = refs[-1]
     half = lax.axis_index("row") // group
     for number in range(out.shape[0]):
         here = owners[0, number] // group == half
@@ -172,18 +173,18 @@
 
     results = []
     for part in range(PARTS):
+        wait = right_terms[:1] if part == PARTS - 1 else ()
         merged = call(
             functools.partial(merge_kernel, group),
             piece,
-            [SMEM, VMEM, VMEM],
-            (owners, mine[part], swap(mine[part], group)),
+            [SMEM, VMEM, VMEM] + [ANY] * len(wait),
+            (owners, mine[part], swap(mine[part], group), *wait),
         )
         pieces = {0: merged}
-        step = chips
-        while step > 1:
+        bits = [1 << b for b in range(1, group.bit_length() - 1)]
+        for bit in bits if part % 2 else reversed(bits):
             for s in list(pieces):
-                pieces[s + step] = swap(pieces[s], step)
-            step //= 2
+                pieces[s + bit] = swap(pieces[s], bit)
         for s in list(pieces):
             pieces[s + 1] = swap(pieces[s], 1)
         last = part == PARTS - 1

time: 60.4 us -> 59.3 us (0.982)
  starting transfers between devices: 32.8 us -> 30.5 us
  waiting for transfers between devices: 18.6 us -> 19.9 us
    ppermute x23, starting transfers between devices: 30.3 us -> 27.6 us  [swap(): return lax.ppermute(array, 'row', [(i, i ^ mask) for i in range(devices)])]
    ppermute x23, waiting for transfers between devices: 18.6 us -> 19.9 us  [swap(): return lax.ppermute(array, 'row', [(i, i ^ mask) for i in range(devices)])]
  transfers between devices with their start and end apart: 24 -> 24, of which waited for: 8 -> 8; matrix products, arithmetic and copies ran while one was open for 0% -> 2% of each run, Pallas kernels for 8% -> 9%
where the time goes in v3:
time: 59.3 us; the launch traced here: 59.1 us
  starting transfers between devices  30.5 us (51%)
  waiting for transfers between devices  19.9 us (34%)
  Pallas kernels  7.44 us (13%)
  local copies, waits for them, and re-layouts  1.1 us (2%)
    ppermute x23, starting transfers between devices, swap(): return lax.ppermute(array, 'row', [(i, i ^ mask) for i in range(devices)])  27.6 us
    ppermute x23, waiting for transfers between devices, swap(): return lax.ppermute(array, 'row', [(i, i ^ mask) for i in range(devices)])  19.9 us
    pallas_call x2, Pallas kernels, shards(): pl.pallas_call(functools.partial(multiply_kernel, part), out_shape=out_sh...  3.91 us
    pallas_call x7, Pallas kernels, call(): pl.pallas_call(kernel, out_shape=out_shape, in_specs=in_specs, out_specs=...  3.54 us
    ppermute x1, starting transfers between devices, shift(): return lax.ppermute(array, 'col', pairs)  2.94 us
  transfers between devices with their start and end apart: 24, of which 8 were waited for; matrix products, arithmetic and copies ran while one was open for 2% of the time, Pallas kernels for 9%

profile of v3, /device:TPU:0, one launch (start us, length us, event | category | flops | bytes accessed | tf_op | source)
XLA Modules:
  0.0 59.1 jit_solution(4255330769758156599)
XLA Ops:
  0.0 2.9 %collective-permute-start = (f32[1024,256]{1,0:T(8,128)}, f32[1024,256]{1,0:T(8,128)S(1)}, u32[]{:S(2)}, u32[]{:S(2)}) collective-permute-start(f32[1024,256]{1,0:T(8,128)} %refs_0_.1), channel_id=1, source_target_pairs={{1,0},{0,1},{3,2},{2,3},{5,4},{4,5},{7,6},{6,7},{9,8},{8,9},{11,10... | collective-permute-start | bytes 3145736 | tf_op jit(solution)/shard_map/ppermute | solution.py:147
  2.9 1.1 %slice.4 = f32[8,32,512]{2,1,0:T(8,128)S(1)} slice(f32[8,64,512]{2,1,0:T(8,128)} %bitcast.3), slice={[0:8], [32:64], [0:512]} | slice | bytes 1048576 | tf_op jit(solution)/shard_map/slice | solution.py:149
  4.0 0.1 collective-permute-start.1
  4.1 1.9 %collective-permute-done.1.got = f32[256,512]{1,0:T(8,128)S(1)} collective-permute-done((f32[256,512]{1,0:T(8,128)S(1)}, f32[256,512]{1,0:T(8,128)S(1)}, u32[]{:S(2)}, u32[]{:S(2)}) %collective-permute-start.1) | collective-permute-done | bytes 524320 | tf_op jit(solution)/shard_map/ppermute | solution.py:143
  6.0 0.0 copy-done
  6.0 2.6 %collective-permute-start.2 = (f32[2,32,512]{2,1,0:T(8,128)S(1)}, f32[2,32,512]{2,1,0:T(8,128)S(1)}, u32[]{:S(2)}, u32[]{:S(2)}) collective-permute-start(f32[2,32,512]{2,1,0:T(8,128)S(1)} %get-tuple-element.15), channel_id=1, source_target_pairs={{0,12},{2,14},{4,8},{6,10},{8,4},{10,6},{12,0},{14,2},{16,28},{18,... | collective-permute-start | bytes 393224 | tf_op jit(solution)/shard_map/ppermute | solution.py:143
  8.6 0.5 collective-permute-start.14
  9.1 0.4 collective-permute-start.15
  9.6 3.2 %collective-permute-done.2.refs_0_.refs_2_ = f32[2,32,512]{2,1,0:T(8,128)S(1)} collective-permute-done((f32[2,32,512]{2,1,0:T(8,128)S(1)}, f32[2,32,512]{2,1,0:T(8,128)S(1)}, u32[]{:S(2)}, u32[]{:S(2)}) %collective-permute-start.2) | collective-permute-done | bytes 131104 | tf_op jit(solution)/shard_map/ppermute | solution.py:143
  12.8 2.2 %collective-permute-start.3 = (f32[2,32,512]{2,1,0:T(8,128)S(1)}, f32[2,32,512]{2,1,0:T(8,128)S(1)}, u32[]{:S(2)}, u32[]{:S(2)}) collective-permute-start(f32[2,32,512]{2,1,0:T(8,128)S(1)} %get-tuple-element.16), channel_id=1, source_target_pairs={{0,4},{2,6},{4,0},{6,2},{8,12},{10,14},{12,8},{14,10},{16,20},{18,... | collective-permute-start | bytes 393224 | tf_op jit(solution)/shard_map/ppermute | solution.py:143
  15.0 1.6 %collective-permute-start.4 = (f32[2,32,512]{2,1,0:T(8,128)S(1)}, f32[2,32,512]{2,1,0:T(8,128)S(1)}, u32[]{:S(2)}, u32[]{:S(2)}) collective-permute-start(f32[2,32,512]{2,1,0:T(8,128)S(1)} %get-tuple-element.17), channel_id=1, source_target_pairs={{0,8},{2,10},{4,12},{6,14},{8,0},{10,2},{12,4},{14,6},{16,24},{18,... | collective-permute-start | bytes 393224 | tf_op jit(solution)/shard_map/ppermute | solution.py:143
  16.6 0.0 collective-permute-done.14.refs_0_
  16.6 0.5 collective-permute-start.5
  17.1 0.0 collective-permute-done.15.refs_1_
  17.1 0.0 copy-done.3
  17.1 0.7 %shard_map.60.mine = f32[3,32,512]{2,1,0:T(8,128)S(1)} custom-call(s32[1,3]{1,0:T(1,128)S(1)} %copy-done.3, f32[512,512]{1,0:T(8,128)S(1)} %bitcast.6, f32[256,512]{1,0:T(8,128)S(1)} %collective-permute-done.1.got, f32[2,32,512]{2,1,0:T(8,128)S(1)} %collective-permute-done.14.refs_0_, f32[2,32,512]{2,1,0:T(8,128)S(1)} %collective-permute-done.15.refs_1_, ...), custom_call_target="tpu_custom_call" | custom-call | bytes 2162700 | tf_op jit(solution)/shard_map/pallas_call | solution.py:19
  17.8 0.0 copy-start.2
  17.8 2.7 %collective-permute-start.16 = (f32[3,32,512]{2,1,0:T(8,128)S(1)}, f32[3,32,512]{2,1,0:T(8,128)S(1)}, u32[]{:S(2)}, u32[]{:S(2)}) collective-permute-start(f32[3,32,512]{2,1,0:T(8,128)S(1)} %shard_map.60.mine), channel_id=1, source_target_pairs={{0,16},{2,18},{4,20},{6,22},{8,24},{10,26},{12,28},{14,30},{16,0},... | collective-permute-start | bytes 589832 | tf_op jit(solution)/shard_map/ppermute | solution.py:143
  20.5 0.0 collective-permute-done.3.refs_0_
  20.5 4.6 %collective-permute-done.4.refs_1_ = f32[2,32,512]{2,1,0:T(8,128)S(1)} collective-permute-done((f32[2,32,512]{2,1,0:T(8,128)S(1)}, f32[2,32,512]{2,1,0:T(8,128)S(1)}, u32[]{:S(2)}, u32[]{:S(2)}) %collective-permute-start.4) | collective-permute-done | bytes 131104 | tf_op jit(solution)/shard_map/ppermute | solution.py:143
  25.1 0.0 collective-permute-done.5.refs_2_
  25.1 0.7 %shard_map.58.mine = f32[3,32,512]{2,1,0:T(8,128)S(1)} custom-call(s32[1,3]{1,0:T(1,128)S(1)} %copy-done.3, f32[512,512]{1,0:T(8,128)S(1)} %bitcast.7, f32[256,512]{1,0:T(8,128)S(1)} %collective-permute-done.1.got, f32[2,32,512]{2,1,0:T(8,128)S(1)} %collective-permute-done.3.refs_0_, f32[2,32,512]{2,1,0:T(8,128)S(1)} %collective-permute-done.4.refs_1_, ...), custom_call_target="tpu_custom_call" | custom-call | bytes 2162700 | tf_op jit(solution)/shard_map/pallas_call | solution.py:19
  25.8 0.0 copy-start.4
  25.8 1.5 %collective-permute-start.6 = (f32[3,32,512]{2,1,0:T(8,128)S(1)}, f32[3,32,512]{2,1,0:T(8,128)S(1)}, u32[]{:S(2)}, u32[]{:S(2)}) collective-permute-start(f32[3,32,512]{2,1,0:T(8,128)S(1)} %shard_map.58.mine), channel_id=1, source_target_pairs={{0,16},{2,18},{4,20},{6,22},{8,24},{10,26},{12,28},{14,30},{16,0},... | collective-permute-start | bytes 589832 | tf_op jit(solution)/shard_map/ppermute | solution.py:143
  27.3 0.0 collective-permute-done.16.other
  27.3 0.6 %shard_map.61.refs_0_ = f32[3,32,512]{2,1,0:T(8,128)S(1)} custom-call(s32[1,3]{1,0:T(1,128)S(1)} %copy-done.3, f32[3,32,512]{2,1,0:T(8,128)S(1)} %shard_map.60.mine, f32[3,32,512]{2,1,0:T(8,128)S(1)} %collective-permute-done.16.other), custom_call_target="tpu_custom_call" | custom-call | bytes 589836 | tf_op jit(solution)/shard_map/pallas_call | solution.py:19
  27.9 7.5 %collective-permute-start.20 = (f32[3,32,512]{2,1,0:T(8,128)S(1)}, f32[3,32,512]{2,1,0:T(8,128)S(1)}, u32[]{:S(2)}, u32[]{:S(2)}) collective-permute-start(f32[3,32,512]{2,1,0:T(8,128)S(1)} %shard_map.61.refs_0_), channel_id=1, source_target_pairs={{0,8},{2,10},{4,12},{6,14},{8,0},{10,2},{12,4},{14,6},{16,24},{18,... | collective-permute-start | bytes 589832 | tf_op jit(solution)/shard_map/ppermute | solution.py:143
  35.4 1.9 %collective-permute-start.18 = (f32[3,32,512]{2,1,0:T(8,128)S(1)}, f32[3,32,512]{2,1,0:T(8,128)S(1)}, u32[]{:S(2)}, u32[]{:S(2)}) collective-permute-start(f32[3,32,512]{2,1,0:T(8,128)S(1)} %shard_map.61.refs_0_), channel_id=1, source_target_pairs={{0,4},{2,6},{4,0},{6,2},{8,12},{10,14},{12,8},{14,10},{16,20},{18,... | collective-permute-start | bytes 589832 | tf_op jit(solution)/shard_map/ppermute | solution.py:143
  37.2 0.0 collective-permute-start.17
  37.3 0.0 collective-permute-done.refs_1_
  37.3 0.0 copy-done.2
  37.3 0.0 copy-done.4
  37.3 0.9 %shard_map.55 = (bf16[1536,256]{1,0:T(8,128)(2,1)S(1)}, bf16[1536,256]{1,0:T(8,128)(2,1)S(1)}) custom-call(s32[3]{0:T(128)S(1)} %copy-done.4, f32[1024,256]{1,0:T(8,128)S(1)} %copy-done.2, f32[1024,256]{1,0:T(8,128)S(1)} %collective-permute-done.refs_1_), custom_call_target="tpu_custom_call" | custom-call | flops 1572864 | bytes 3670028 | tf_op jit(solution)/shard_map/pallas_call | solution.py:19
  38.2 0.0 collective-permute-done.6.other
  38.2 0.0 copy-start.1
  38.2 0.6 %shard_map.59.refs_0_ = f32[3,32,512]{2,1,0:T(8,128)S(1)} custom-call(s32[1,3]{1,0:T(1,128)S(1)} %copy-done.3, f32[3,32,512]{2,1,0:T(8,128)S(1)} %shard_map.58.mine, f32[3,32,512]{2,1,0:T(8,128)S(1)} %collective-permute-done.6.other, bf16[1536,256]{1,0:T(8,128)(2,1)S(1)} %get-tuple-element.13.refs_0_.right_high), custom_call_target="tpu_custom_call" | custom-call | bytes 1376268 | tf_op jit(solution)/shard_map/pallas_call | solution.py:19
  38.8 1.3 %collective-permute-start.8 = (f32[3,32,512]{2,1,0:T(8,128)S(1)}, f32[3,32,512]{2,1,0:T(8,128)S(1)}, u32[]{:S(2)}, u32[]{:S(2)}) collective-permute-start(f32[3,32,512]{2,1,0:T(8,128)S(1)} %shard_map.59.refs_0_), channel_id=1, source_target_pairs={{0,4},{2,6},{4,0},{6,2},{8,12},{10,14},{12,8},{14,10},{16,20},{18,... | collective-permute-start | bytes 589832 | tf_op jit(solution)/shard_map/ppermute | solution.py:143
  40.1 1.3 %collective-permute-done.20.refs_4_ = f32[3,32,512]{2,1,0:T(8,128)S(1)} collective-permute-done((f32[3,32,512]{2,1,0:T(8,128)S(1)}, f32[3,32,512]{2,1,0:T(8,128)S(1)}, u32[]{:S(2)}, u32[]{:S(2)}) %collective-permute-start.20) | collective-permute-done | bytes 196640 | tf_op jit(solution)/shard_map/ppermute | solution.py:143
  41.4 2.1 %collective-permute-start.22 = (f32[3,32,512]{2,1,0:T(8,128)S(1)}, f32[3,32,512]{2,1,0:T(8,128)S(1)}, u32[]{:S(2)}, u32[]{:S(2)}) collective-permute-start(f32[3,32,512]{2,1,0:T(8,128)S(1)} %collective-permute-done.20.refs_4_), channel_id=1, source_target_pairs={{0,4},{2,6},{4,0},{6,2},{8,12},{10,14},{12,8},{14,10},{16,20},{18,... | collective-permute-start | bytes 589832 | tf_op jit(solution)/shard_map/ppermute | solution.py:143
  43.5 0.0 collective-permute-start.21
  43.5 0.0 collective-permute-done.18.refs_2_
  43.5 0.5 collective-permute-start.19
  44.0 0.0 collective-permute-done.17.refs_1_
  44.0 0.0 collective-permute-start.10
  44.0 2.6 %collective-permute-done.8.refs_2_ = f32[3,32,512]{2,1,0:T(8,128)S(1)} collective-permute-done((f32[3,32,512]{2,1,0:T(8,128)S(1)}, f32[3,32,512]{2,1,0:T(8,128)S(1)}, u32[]{:S(2)}, u32[]{:S(2)}) %collective-permute-start.8) | collective-permute-done | bytes 196640 | tf_op jit(solution)/shard_map/ppermute | solution.py:143
  46.6 1.7 %collective-permute-start.12 = (f32[3,32,512]{2,1,0:T(8,128)S(1)}, f32[3,32,512]{2,1,0:T(8,128)S(1)}, u32[]{:S(2)}, u32[]{:S(2)}) collective-permute-start(f32[3,32,512]{2,1,0:T(8,128)S(1)} %collective-permute-done.8.refs_2_), channel_id=1, source_target_pairs={{0,8},{2,10},{4,12},{6,14},{8,0},{10,2},{12,4},{14,6},{16,24},{18,... | collective-permute-start | bytes 589832 | tf_op jit(solution)/shard_map/ppermute | solution.py:143
  48.3 2.1 %collective-permute-done.22.refs_6_ = f32[3,32,512]{2,1,0:T(8,128)S(1)} collective-permute-done((f32[3,32,512]{2,1,0:T(8,128)S(1)}, f32[3,32,512]{2,1,0:T(8,128)S(1)}, u32[]{:S(2)}, u32[]{:S(2)}) %collective-permute-start.22) | collective-permute-done | bytes 196640 | tf_op jit(solution)/shard_map/ppermute | solution.py:143
  50.4 0.0 collective-permute-start.23
  50.4 0.0 collective-permute-done.21.refs_5_
  50.4 0.5 collective-permute-start.7
  50.9 0.0 collective-permute-done.19.refs_3_
  50.9 0.1 collective-permute-start.9
  51.0 0.8 %collective-permute-done.10.refs_4_ = f32[3,32,512]{2,1,0:T(8,128)S(1)} collective-permute-done((f32[3,32,512]{2,1,0:T(8,128)S(1)}, f32[3,32,512]{2,1,0:T(8,128)S(1)}, u32[]{:S(2)}, u32[]{:S(2)}) %collective-permute-start.10) | collective-permute-done | bytes 196640 | tf_op jit(solution)/shard_map/ppermute | solution.py:143
  51.8 0.0 collective-permute-start.11
  51.8 3.3 %collective-permute-done.12.refs_6_ = f32[3,32,512]{2,1,0:T(8,128)S(1)} collective-permute-done((f32[3,32,512]{2,1,0:T(8,128)S(1)}, f32[3,32,512]{2,1,0:T(8,128)S(1)}, u32[]{:S(2)}, u32[]{:S(2)}) %collective-permute-start.12) | collective-permute-done | bytes 196640 | tf_op jit(solution)/shard_map/ppermute | solution.py:143
  55.1 0.0 collective-permute-start.13
  55.1 0.0 collective-permute-done.23.refs_7_
  55.1 0.0 copy-done.1
  55.1 1.6 %shard_map.62.refs_8_ = f32[256,256]{1,0:T(8,128)S(1)} custom-call(s32[1,3]{1,0:T(1,128)S(1)} %copy-done.3, bf16[1536,256]{1,0:T(8,128)(2,1)S(1)} %get-tuple-element.13.refs_0_.right_high, bf16[1536,256]{1,0:T(8,128)(2,1)S(1)} %get-tuple-element.14.right_low, f32[512,256]{1,0:T(8,128)S(1)} %copy-done.1, f32[3,32,512]{2,1,0:T(8,128)S(1)} %shard_map.61.refs_0_, ...), custom_call_target="tpu_custom_call" | custom-call | flops 603979776 | bytes 3670028 | tf_op jit(solution)/shard_map/pallas_call | solution.py:194
  56.7 0.0 collective-permute-done.7.refs_1_
  56.7 0.0 collective-permute-done.11.refs_5_
  56.7 0.0 collective-permute-done.9.refs_3_
  56.7 0.0 collective-permute-done.13.refs_7_
  56.7 2.4 %shard_map.63 = f32[512,256]{1,0:T(8,128)} custom-call(s32[1,3]{1,0:T(1,128)S(1)} %copy-done.3, bf16[1536,256]{1,0:T(8,128)(2,1)S(1)} %get-tuple-element.13.refs_0_.right_high, bf16[1536,256]{1,0:T(8,128)(2,1)S(1)} %get-tuple-element.14.right_low, f32[512,256]{1,0:T(8,128)S(1)} %copy-done.1, f32[3,32,512]{2,1,0:T(8,128)S(1)} %shard_map.59.refs_0_, ...), custom_call_target="tpu_custom_call" | custom-call | flops 603979776 | bytes 3932172 | tf_op jit(solution)/shard_map/pallas_call | solution.py:194
  (4 shorter events, 0.1 us)
Async XLA Ops:
  0.0 6.0 %copy-start = (f32[1,512,512]{2,1,0:T(8,128)S(1)}, f32[1,512,512]{2,1,0:T(8,128)}, u32[]{:S(2)}) copy-start(f32[1,512,512]{2,1,0:T(8,128)} %param.5) | copy-start | bytes 3145732
  0.0 37.3 %collective-permute-start = (f32[1024,256]{1,0:T(8,128)}, f32[1024,256]{1,0:T(8,128)S(1)}, u32[]{:S(2)}, u32[]{:S(2)}) collective-permute-start(f32[1024,256]{1,0:T(8,128)} %refs_0_.1), channel_id=1, source_target_pairs={{1,0},{0,1},{3,2},{2,3},{5,4},{4,5},{7,6},{6,7},{9,8},{8,9},{11,10... | collective-permute-start | bytes 3145736 | tf_op jit(solution)/shard_map/ppermute | solution.py:147
  4.0 2.0 %collective-permute-start.1 = (f32[256,512]{1,0:T(8,128)S(1)}, f32[256,512]{1,0:T(8,128)S(1)}, u32[]{:S(2)}, u32[]{:S(2)}) collective-permute-start(f32[256,512]{1,0:T(8,128)S(1)} %bitcast.8), channel_id=1, source_target_pairs={{0,2},{2,0},{4,6},{6,4},{8,10},{10,8},{12,14},{14,12},{16,18},{18,... | collective-permute-start | bytes 1572872 | tf_op jit(solution)/shard_map/ppermute | solution.py:143
  6.0 6.7 %collective-permute-start.2 = (f32[2,32,512]{2,1,0:T(8,128)S(1)}, f32[2,32,512]{2,1,0:T(8,128)S(1)}, u32[]{:S(2)}, u32[]{:S(2)}) collective-permute-start(f32[2,32,512]{2,1,0:T(8,128)S(1)} %get-tuple-element.15), channel_id=1, source_target_pairs={{0,12},{2,14},{4,8},{6,10},{8,4},{10,6},{12,0},{14,2},{16,28},{18,... | collective-permute-start | bytes 393224 | tf_op jit(solution)/shard_map/ppermute | solution.py:143
  8.6 8.0 %collective-permute-start.14 = (f32[2,32,512]{2,1,0:T(8,128)S(1)}, f32[2,32,512]{2,1,0:T(8,128)S(1)}, u32[]{:S(2)}, u32[]{:S(2)}) collective-permute-start(f32[2,32,512]{2,1,0:T(8,128)S(1)} %get-tuple-element.19), channel_id=1, source_target_pairs={{0,4},{2,6},{4,0},{6,2},{8,12},{10,14},{12,8},{14,10},{16,20},{18,... | collective-permute-start | bytes 393224 | tf_op jit(solution)/shard_map/ppermute | solution.py:143
  9.1 8.0 %collective-permute-start.15 = (f32[2,32,512]{2,1,0:T(8,128)S(1)}, f32[2,32,512]{2,1,0:T(8,128)S(1)}, u32[]{:S(2)}, u32[]{:S(2)}) collective-permute-start(f32[2,32,512]{2,1,0:T(8,128)S(1)} %get-tuple-element.20), channel_id=1, source_target_pairs={{0,8},{2,10},{4,12},{6,14},{8,0},{10,2},{12,4},{14,6},{16,24},{18,... | collective-permute-start | bytes 393224 | tf_op jit(solution)/shard_map/ppermute | solution.py:143
  12.8 7.7 %collective-permute-start.3 = (f32[2,32,512]{2,1,0:T(8,128)S(1)}, f32[2,32,512]{2,1,0:T(8,128)S(1)}, u32[]{:S(2)}, u32[]{:S(2)}) collective-permute-start(f32[2,32,512]{2,1,0:T(8,128)S(1)} %get-tuple-element.16), channel_id=1, source_target_pairs={{0,4},{2,6},{4,0},{6,2},{8,12},{10,14},{12,8},{14,10},{16,20},{18,... | collective-permute-start | bytes 393224 | tf_op jit(solution)/shard_map/ppermute | solution.py:143
  15.0 2.1 %copy-start.3 = (s32[1,3]{1,0:T(1,128)S(1)}, s32[1,3]{1,0:T(1,128)}, u32[]{:S(2)}) copy-start(s32[1,3]{1,0:T(1,128)} %owners.11) | copy-start | bytes 40
  15.0 10.1 %collective-permute-start.4 = (f32[2,32,512]{2,1,0:T(8,128)S(1)}, f32[2,32,512]{2,1,0:T(8,128)S(1)}, u32[]{:S(2)}, u32[]{:S(2)}) collective-permute-start(f32[2,32,512]{2,1,0:T(8,128)S(1)} %get-tuple-element.17), channel_id=1, source_target_pairs={{0,8},{2,10},{4,12},{6,14},{8,0},{10,2},{12,4},{14,6},{16,24},{18,... | collective-permute-start | bytes 393224 | tf_op jit(solution)/shard_map/ppermute | solution.py:143
  16.6 8.5 %collective-permute-start.5 = (f32[2,32,512]{2,1,0:T(8,128)S(1)}, f32[2,32,512]{2,1,0:T(8,128)S(1)}, u32[]{:S(2)}, u32[]{:S(2)}) collective-permute-start(f32[2,32,512]{2,1,0:T(8,128)S(1)} %get-tuple-element.18), channel_id=1, source_target_pairs={{0,12},{2,14},{4,8},{6,10},{8,4},{10,6},{12,0},{14,2},{16,28},{18,... | collective-permute-start | bytes 393224 | tf_op jit(solution)/shard_map/ppermute | solution.py:143
  17.8 19.5 %copy-start.2 = (f32[1024,256]{1,0:T(8,128)S(1)}, f32[1024,256]{1,0:T(8,128)}, u32[]{:S(2)}) copy-start(f32[1024,256]{1,0:T(8,128)} %refs_0_.1) | copy-start | bytes 3145732
  17.8 9.5 %collective-permute-start.16 = (f32[3,32,512]{2,1,0:T(8,128)S(1)}, f32[3,32,512]{2,1,0:T(8,128)S(1)}, u32[]{:S(2)}, u32[]{:S(2)}) collective-permute-start(f32[3,32,512]{2,1,0:T(8,128)S(1)} %shard_map.60.mine), channel_id=1, source_target_pairs={{0,16},{2,18},{4,20},{6,22},{8,24},{10,26},{12,28},{14,30},{16,0},... | collective-permute-start | bytes 589832 | tf_op jit(solution)/shard_map/ppermute | solution.py:143
  25.8 11.5 %copy-start.4 = (s32[3]{0:T(128)S(1)}, s32[3]{0:T(128)}, u32[]{:S(2)}) copy-start(s32[3]{0:T(128)} %offsets.1) | copy-start | bytes 40
  25.8 12.4 %collective-permute-start.6 = (f32[3,32,512]{2,1,0:T(8,128)S(1)}, f32[3,32,512]{2,1,0:T(8,128)S(1)}, u32[]{:S(2)}, u32[]{:S(2)}) collective-permute-start(f32[3,32,512]{2,1,0:T(8,128)S(1)} %shard_map.58.mine), channel_id=1, source_target_pairs={{0,16},{2,18},{4,20},{6,22},{8,24},{10,26},{12,28},{14,30},{16,0},... | collective-permute-start | bytes 589832 | tf_op jit(solution)/shard_map/ppermute | solution.py:143
  27.9 13.5 %collective-permute-start.20 = (f32[3,32,512]{2,1,0:T(8,128)S(1)}, f32[3,32,512]{2,1,0:T(8,128)S(1)}, u32[]{:S(2)}, u32[]{:S(2)}) collective-permute-start(f32[3,32,512]{2,1,0:T(8,128)S(1)} %shard_map.61.refs_0_), channel_id=1, source_target_pairs={{0,8},{2,10},{4,12},{6,14},{8,0},{10,2},{12,4},{14,6},{16,24},{18,... | collective-permute-start | bytes 589832 | tf_op jit(solution)/shard_map/ppermute | solution.py:143
  35.4 8.1 %collective-permute-start.18 = (f32[3,32,512]{2,1,0:T(8,128)S(1)}, f32[3,32,512]{2,1,0:T(8,128)S(1)}, u32[]{:S(2)}, u32[]{:S(2)}) collective-permute-start(f32[3,32,512]{2,1,0:T(8,128)S(1)} %shard_map.61.refs_0_), channel_id=1, source_target_pairs={{0,4},{2,6},{4,0},{6,2},{8,12},{10,14},{12,8},{14,10},{16,20},{18,... | collective-permute-start | bytes 589832 | tf_op jit(solution)/shard_map/ppermute | solution.py:143
  37.2 6.8 %collective-permute-start.17 = (f32[3,32,512]{2,1,0:T(8,128)S(1)}, f32[3,32,512]{2,1,0:T(8,128)S(1)}, u32[]{:S(2)}, u32[]{:S(2)}) collective-permute-start(f32[3,32,512]{2,1,0:T(8,128)S(1)} %shard_map.61.refs_0_), channel_id=1, source_target_pairs={{0,2},{2,0},{4,6},{6,4},{8,10},{10,8},{12,14},{14,12},{16,18},{18,... | collective-permute-start | bytes 589832 | tf_op jit(solution)/shard_map/ppermute | solution.py:143
  38.2 16.9 %copy-start.1 = (f32[512,256]{1,0:T(8,128)S(1)}, f32[512,256]{1,0:T(8,128)}, u32[]{:S(2)}) copy-start(f32[512,256]{1,0:T(8,128)} %previous.3) | copy-start | bytes 1572868
  38.8 7.8 %collective-permute-start.8 = (f32[3,32,512]{2,1,0:T(8,128)S(1)}, f32[3,32,512]{2,1,0:T(8,128)S(1)}, u32[]{:S(2)}, u32[]{:S(2)}) collective-permute-start(f32[3,32,512]{2,1,0:T(8,128)S(1)} %shard_map.59.refs_0_), channel_id=1, source_target_pairs={{0,4},{2,6},{4,0},{6,2},{8,12},{10,14},{12,8},{14,10},{16,20},{18,... | collective-permute-start | bytes 589832 | tf_op jit(solution)/shard_map/ppermute | solution.py:143
  41.4 9.0 %collective-permute-start.22 = (f32[3,32,512]{2,1,0:T(8,128)S(1)}, f32[3,32,512]{2,1,0:T(8,128)S(1)}, u32[]{:S(2)}, u32[]{:S(2)}) collective-permute-start(f32[3,32,512]{2,1,0:T(8,128)S(1)} %collective-permute-done.20.refs_4_), channel_id=1, source_target_pairs={{0,4},{2,6},{4,0},{6,2},{8,12},{10,14},{12,8},{14,10},{16,20},{18,... | collective-permute-start | bytes 589832 | tf_op jit(solution)/shard_map/ppermute | solution.py:143
  43.5 6.9 %collective-permute-start.21 = (f32[3,32,512]{2,1,0:T(8,128)S(1)}, f32[3,32,512]{2,1,0:T(8,128)S(1)}, u32[]{:S(2)}, u32[]{:S(2)}) collective-permute-start(f32[3,32,512]{2,1,0:T(8,128)S(1)} %collective-permute-done.20.refs_4_), channel_id=1, source_target_pairs={{0,2},{2,0},{4,6},{6,4},{8,10},{10,8},{12,14},{14,12},{16,18},{18,... | collective-permute-start | bytes 589832 | tf_op jit(solution)/shard_map/ppermute | solution.py:143
  43.5 7.4 %collective-permute-start.19 = (f32[3,32,512]{2,1,0:T(8,128)S(1)}, f32[3,32,512]{2,1,0:T(8,128)S(1)}, u32[]{:S(2)}, u32[]{:S(2)}) collective-permute-start(f32[3,32,512]{2,1,0:T(8,128)S(1)} %collective-permute-done.18.refs_2_), channel_id=1, source_target_pairs={{0,2},{2,0},{4,6},{6,4},{8,10},{10,8},{12,14},{14,12},{16,18},{18,... | collective-permute-start | bytes 589832 | tf_op jit(solution)/shard_map/ppermute | solution.py:143
  44.0 7.8 %collective-permute-start.10 = (f32[3,32,512]{2,1,0:T(8,128)S(1)}, f32[3,32,512]{2,1,0:T(8,128)S(1)}, u32[]{:S(2)}, u32[]{:S(2)}) collective-permute-start(f32[3,32,512]{2,1,0:T(8,128)S(1)} %shard_map.59.refs_0_), channel_id=1, source_target_pairs={{0,8},{2,10},{4,12},{6,14},{8,0},{10,2},{12,4},{14,6},{16,24},{18,... | collective-permute-start | bytes 589832 | tf_op jit(solution)/shard_map/ppermute | solution.py:143
  46.6 8.5 %collective-permute-start.12 = (f32[3,32,512]{2,1,0:T(8,128)S(1)}, f32[3,32,512]{2,1,0:T(8,128)S(1)}, u32[]{:S(2)}, u32[]{:S(2)}) collective-permute-start(f32[3,32,512]{2,1,0:T(8,128)S(1)} %collective-permute-done.8.refs_2_), channel_id=1, source_target_pairs={{0,8},{2,10},{4,12},{6,14},{8,0},{10,2},{12,4},{14,6},{16,24},{18,... | collective-permute-start | bytes 589832 | tf_op jit(solution)/shard_map/ppermute | solution.py:143
  50.4 4.7 %collective-permute-start.23 = (f32[3,32,512]{2,1,0:T(8,128)S(1)}, f32[3,32,512]{2,1,0:T(8,128)S(1)}, u32[]{:S(2)}, u32[]{:S(2)}) collective-permute-start(f32[3,32,512]{2,1,0:T(8,128)S(1)} %collective-permute-done.22.refs_6_), channel_id=1, source_target_pairs={{0,2},{2,0},{4,6},{6,4},{8,10},{10,8},{12,14},{14,12},{16,18},{18,... | collective-permute-start | bytes 589832 | tf_op jit(solution)/shard_map/ppermute | solution.py:143
  50.4 6.3 %collective-permute-start.7 = (f32[3,32,512]{2,1,0:T(8,128)S(1)}, f32[3,32,512]{2,1,0:T(8,128)S(1)}, u32[]{:S(2)}, u32[]{:S(2)}) collective-permute-start(f32[3,32,512]{2,1,0:T(8,128)S(1)} %shard_map.59.refs_0_), channel_id=1, source_target_pairs={{0,2},{2,0},{4,6},{6,4},{8,10},{10,8},{12,14},{14,12},{16,18},{18,... | collective-permute-start | bytes 589832 | tf_op jit(solution)/shard_map/ppermute | solution.py:143
  50.9 5.8 %collective-permute-start.9 = (f32[3,32,512]{2,1,0:T(8,128)S(1)}, f32[3,32,512]{2,1,0:T(8,128)S(1)}, u32[]{:S(2)}, u32[]{:S(2)}) collective-permute-start(f32[3,32,512]{2,1,0:T(8,128)S(1)} %collective-permute-done.8.refs_2_), channel_id=1, source_target_pairs={{0,2},{2,0},{4,6},{6,4},{8,10},{10,8},{12,14},{14,12},{16,18},{18,... | collective-permute-start | bytes 589832 | tf_op jit(solution)/shard_map/ppermute | solution.py:143
  51.8 4.9 %collective-permute-start.11 = (f32[3,32,512]{2,1,0:T(8,128)S(1)}, f32[3,32,512]{2,1,0:T(8,128)S(1)}, u32[]{:S(2)}, u32[]{:S(2)}) collective-permute-start(f32[3,32,512]{2,1,0:T(8,128)S(1)} %collective-permute-done.10.refs_4_), channel_id=1, source_target_pairs={{0,2},{2,0},{4,6},{6,4},{8,10},{10,8},{12,14},{14,12},{16,18},{18,... | collective-permute-start | bytes 589832 | tf_op jit(solution)/shard_map/ppermute | solution.py:143
  55.1 1.6 %collective-permute-start.13 = (f32[3,32,512]{2,1,0:T(8,128)S(1)}, f32[3,32,512]{2,1,0:T(8,128)S(1)}, u32[]{:S(2)}, u32[]{:S(2)}) collective-permute-start(f32[3,32,512]{2,1,0:T(8,128)S(1)} %collective-permute-done.12.refs_6_), channel_id=1, source_target_pairs={{0,2},{2,0},{4,6},{6,4},{8,10},{10,8},{12,14},{14,12},{16,18},{18,... | collective-permute-start | bytes 589832 | tf_op jit(solution)/shard_map/ppermute | solution.py:143

commit v4 on v3

--- a/solution.py
+++ b/solution.py
@@ -36,34 +36,10 @@
     return jnp.dot(left, right, preferred_element_type=jnp.float32)
 
 
-def gather_kernel(part, chips, own, got, *refs):
-    outs = refs[-(chips - 1):]
-    chunk = outs[0].shape[1]
-    for step, out in enumerate(outs, 1):
-        place = part * chips + step
-        out[0] = own[2 * place * chunk:(2 * place + 1) * chunk, :]
-        out[1] = got[place * chunk:(place + 1) * chunk, :]
-
-
-def pick_kernel(part, chips, owners, own, got, *refs):
-    pieces, out = refs[:-1], refs[-1]
+def pick_kernel(group, part, owners, arrived, out):
     chunk = out.shape[1]
-    member = lax.axis_index("row") % (2 * chips)
-    first = part * chips
-    near = [own[2 * first * chunk:(2 * first + 1) * chunk, :], got[first * chunk:(first + 1) * chunk, :]]
     for number in range(out.shape[0]):
-        mask = (owners[0, number] % (2 * chips)) ^ member
-        for core in range(2):
-
-            @pl.when(mask == core)
-            def _():
-                out[number] = near[core]
-
-            for step, piece in enumerate(pieces, 1):
-
-                @pl.when(mask == 2 * step + core)
-                def _():
-                    out[number] = piece[core]
+        out[number] = arrived[owners[0, number] % group, part * chunk:(part + 1) * chunk, :]
 
 
 def merge_kernel(group, owners, mine, other, *refs):
@@ -98,32 +74,32 @@
                     right_low[lanes, :] = low
 
 
-def multiply_kernel(part, owners, right_high, right_low, previous, *refs):
+def multiply_kernel(part, right_high, right_low, previous, *refs):
     group = len(refs) - part - 3
     pieces, early = refs[:group], refs[group:group + part]
     out, left_high, left_low = refs[group + part:]
     count, chunk, width = pieces[0].shape
     member = lax.axis_index("row") % group
-    size = group * chunk
     for number in range(count):
-        mask = (owners[0, number] % group) ^ member
         lanes = slice(number * width, (number + 1) * width)
         for step in range(group):
-            place = pl.multiple_of((mask ^ step) * chunk, chunk)
+            place = pl.multiple_of((member ^ step) * chunk, chunk)
             high, low = split(pieces[step][number])
             left_high[pl.ds(place, chunk), lanes] = high
             left_low[pl.ds(place, chunk), lanes] = low
-    total = 2.0 * previous[part * size:(part + 1) * size, :] - (
+    product = (
         dot(left_high[...], right_low[...])
         + dot(left_low[...], right_high[...])
         + dot(left_high[...], right_high[...])
     )
-    if out.shape[0] > size:
-        for number, ref in enumerate(early):
-            out[number * size:(number + 1) * size, :] = ref[...]
-        out[part * size:, :] = total
+    if part < PARTS - 1:
+        out[...] = product
     else:
-        out[...] = total
+        for number, ref in enumerate((*early, product)):
+            for place in range(group):
+                first = (place * PARTS + number) * chunk
+                rows = slice(first, first + chunk)
+                out[rows, :] = 2.0 * previous[rows, :] - ref[place * chunk:(place + 1) * chunk, :]
 
 
 def shards(left_slots, right, previous, offsets, owners):
@@ -133,11 +109,9 @@
     devices = lax.axis_size("row")
     columns = lax.axis_size("col")
     group = devices // 2
-    chips = group // 2
     size = rows // PARTS
     chunk = size // group
     piece = jax.ShapeDtypeStruct((count, chunk, width), own.dtype)
-    pair = jax.ShapeDtypeStruct((2, chunk, width), own.dtype)
 
     def swap(array, mask):
         return lax.ppermute(array, "row", [(i, i ^ mask) for i in range(devices)])
@@ -146,24 +120,14 @@
         pairs = [((i + distance) % columns, i) for i in range(columns)]
         return lax.ppermute(array, "col", pairs)
 
-    got = swap(own.reshape(rows // (2 * chunk), 2 * chunk, width)[:, chunk:].reshape(rows // 2, width), 1)
-    mine = []
-    wait = []
-    for part in range(PARTS):
-        sent = call(
-            functools.partial(gather_kernel, part, chips),
-            (pair,) * (chips - 1),
-            [VMEM, VMEM] + [ANY] * len(wait),
-            (own, got, *wait),
-        )
-        pieces = [swap(array, 2 * step) for step, array in enumerate(sent, 1)]
-        wait = pieces[-1:]
-        mine.append(call(
-            functools.partial(pick_kernel, part, chips),
-            piece,
-            [SMEM] + [VMEM] * (2 + len(pieces)),
-            (owners, own, got, *pieces),
-        ))
+    groups = [list(range(first, first + group)) for first in range(0, devices, group)]
+    arrived = lax.all_to_all(
+        own.reshape(group, PARTS * chunk, width), "row", 0, 0, axis_index_groups=groups, tiled=True
+    )
+    mine = [
+        call(functools.partial(pick_kernel, group, part), piece, [SMEM, VMEM], (owners, arrived))
+        for part in range(PARTS)
+    ]
 
     rights = [right] + [shift(right, distance) for distance in range(1, columns)]
     terms = jax.ShapeDtypeStruct((count * width, right.shape[1]), jnp.bfloat16)
@@ -188,13 +152,13 @@
         for s in list(pieces):
             pieces[s + 1] = swap(pieces[s], 1)
         last = part == PARTS - 1
-        operands = (owners, *right_terms, previous, *[pieces[s] for s in range(group)], *results)
+        operands = (*right_terms, previous, *[pieces[s] for s in range(group)], *results)
         out_shape = jax.ShapeDtypeStruct((rows if last else size, right.shape[1]), previous.dtype)
         moved = sum(x.size * x.dtype.itemsize for x in operands)
         results.append(pl.pallas_call(
             functools.partial(multiply_kernel, part),
             out_shape=out_shape,
-            in_specs=[SMEM] + [VMEM] * (len(operands) - 1),
+            in_specs=[VMEM] * len(operands),
             out_specs=VMEM,
             scratch_shapes=[pltpu.VMEM((size, count * width), jnp.bfloat16)] * 2,
             cost_estimate=pl.CostEstimate(

time: 59.3 us -> 60.3 us (1.017)
  waiting for transfers between devices: 19.9 us -> 35.6 us
  starting transfers between devices: 30.5 us -> 18.4 us
  Pallas kernels: 7.44 us -> 6.03 us
  local copies, waits for them, and re-layouts: 1.1 us -> 0.02 us
    ppermute x23 -> x16, starting transfers between devices: 27.6 us -> 11.4 us  [swap(): return lax.ppermute(array, 'row', [(i, i ^ mask) for i in range(devices)])]
    all_to_all x0 -> x1, waiting for transfers between devices: none -> 12.9 us  [shards(): lax.all_to_all(own.reshape(group, PARTS * chunk, width), 'row', 0, 0, axi...]
    all_to_all x0 -> x1, starting transfers between devices: none -> 5.39 us  [shards(): lax.all_to_all(own.reshape(group, PARTS * chunk, width), 'row', 0, 0, axi...]
    ppermute x23 -> x16, waiting for transfers between devices: 19.9 us -> 22.7 us  [swap(): return lax.ppermute(array, 'row', [(i, i ^ mask) for i in range(devices)])]
    ppermute x1, starting transfers between devices: 2.94 us -> 1.56 us  [shift(): return lax.ppermute(array, 'col', pairs)]
    pallas_call x2, Pallas kernels: 3.91 us -> 2.8 us  [shards(): pl.pallas_call(functools.partial(multiply_kernel, part), out_shape=out_sh...]
    slice x1 -> x0, local copies, waits for them, and re-layouts: 1.08 us -> none  [shards(): own.reshape(rows // (2 * chunk), 2 * chunk, width)[:, chunk:]]
    pallas_call x7 -> x5, Pallas kernels: 3.54 us -> 3.23 us  [call(): pl.pallas_call(kernel, out_shape=out_shape, in_specs=in_specs, out_specs=...]
  transfers between devices with their start and end apart: 24 -> 18, of which waited for: 8 -> 9; matrix products, arithmetic and copies ran while one was open for 2% -> 0% of each run, Pallas kernels for 9% -> 7%
where the time goes in v4:
time: 60.3 us; the launch traced here: 60.1 us
  waiting for transfers between devices  35.6 us (59%)
  starting transfers between devices  18.4 us (31%)
  Pallas kernels  6.03 us (10%)
    ppermute x16, waiting for transfers between devices, swap(): return lax.ppermute(array, 'row', [(i, i ^ mask) for i in range(devices)])  22.7 us
    all_to_all x1, waiting for transfers between devices, shards(): lax.all_to_all(own.reshape(group, PARTS * chunk, width), 'row', 0, 0, axi...  12.9 us
    ppermute x16, starting transfers between devices, swap(): return lax.ppermute(array, 'row', [(i, i ^ mask) for i in range(devices)])  11.4 us
    all_to_all x1, starting transfers between devices, shards(): lax.all_to_all(own.reshape(group, PARTS * chunk, width), 'row', 0, 0, axi...  5.39 us
    pallas_call x5, Pallas kernels, call(): pl.pallas_call(kernel, out_shape=out_shape, in_specs=in_specs, out_specs=...  3.23 us
    pallas_call x2, Pallas kernels, shards(): pl.pallas_call(functools.partial(multiply_kernel, part), out_shape=out_sh...  2.8 us
    ppermute x1, starting transfers between devices, shift(): return lax.ppermute(array, 'col', pairs)  1.56 us
  transfers between devices with their start and end apart: 18, of which 9 were waited for; matrix products, arithmetic and copies ran while one was open for 0% of the time, Pallas kernels for 7%

profile of v4, /device:TPU:0, one launch (start us, length us, event | category | flops | bytes accessed | tf_op | source)
XLA Modules:
  0.0 60.1 jit_solution(13290408633405490830)
XLA Ops:
  0.0 0.0 copy-start.1
  0.0 0.0 copy-start.2
  0.0 5.4 %all-to-all-start = ((f32[8,64,512]{2,1,0:T(8,128)}), f32[8,64,512]{2,1,0:T(8,128)S(1)}, u32[]{:S(2)}, u32[]{:S(2)}) async-start(f32[8,64,512]{2,1,0:T(8,128)} %bitcast.1), calls=%async_computation | async-start | bytes 2097152 | tf_op jit(solution)/shard_map/all_to_all | solution.py:124
  5.4 0.0 copy-done.1
  5.4 1.6 %collective-permute-start = (f32[1024,256]{1,0:T(8,128)S(1)}, f32[1024,256]{1,0:T(8,128)S(1)}, u32[]{:S(2)}, u32[]{:S(2)}) collective-permute-start(f32[1024,256]{1,0:T(8,128)S(1)} %copy-done.1), channel_id=1, source_target_pairs={{1,0},{0,1},{3,2},{2,3},{5,4},{4,5},{7,6},{6,7},{9,8},{8,9},{11,10... | collective-permute-start | bytes 3145736 | tf_op jit(solution)/shard_map/ppermute | solution.py:121
  7.0 12.9 %all-to-all-done.arrived = f32[8,64,512]{2,1,0:T(8,128)S(1)} async-done(((f32[8,64,512]{2,1,0:T(8,128)}), f32[8,64,512]{2,1,0:T(8,128)S(1)}, u32[]{:S(2)}, u32[]{:S(2)}) %all-to-all-start) | async-done | bytes 1048608 | tf_op jit(solution)/shard_map/all_to_all | solution.py:124
  19.9 0.0 copy-done.2
  19.9 0.6 shard_map.58.mine
  20.4 2.7 %collective-permute-start.9 = (f32[3,32,512]{2,1,0:T(8,128)S(1)}, f32[3,32,512]{2,1,0:T(8,128)S(1)}, u32[]{:S(2)}, u32[]{:S(2)}) collective-permute-start(f32[3,32,512]{2,1,0:T(8,128)S(1)} %shard_map.58.mine), channel_id=1, source_target_pairs={{0,16},{2,18},{4,20},{6,22},{8,24},{10,26},{12,28},{14,30},{16,0},... | collective-permute-start | bytes 589832 | tf_op jit(solution)/shard_map/ppermute | solution.py:117
  23.1 0.6 shard_map.56.mine
  23.7 0.0 copy-start.3
  23.7 0.4 collective-permute-start.1
  24.1 12.4 %collective-permute-done.9.other = f32[3,32,512]{2,1,0:T(8,128)S(1)} collective-permute-done((f32[3,32,512]{2,1,0:T(8,128)S(1)}, f32[3,32,512]{2,1,0:T(8,128)S(1)}, u32[]{:S(2)}, u32[]{:S(2)}) %collective-permute-start.9) | collective-permute-done | bytes 196640 | tf_op jit(solution)/shard_map/ppermute | solution.py:117
  36.5 0.6 %shard_map.59.refs_0_ = f32[3,32,512]{2,1,0:T(8,128)S(1)} custom-call(s32[1,3]{1,0:T(1,128)S(1)} %copy-done.2, f32[3,32,512]{2,1,0:T(8,128)S(1)} %shard_map.58.mine, f32[3,32,512]{2,1,0:T(8,128)S(1)} %collective-permute-done.9.other), custom_call_target="tpu_custom_call" | custom-call | bytes 589836 | tf_op jit(solution)/shard_map/pallas_call | solution.py:19
  37.1 0.7 %collective-permute-start.13 = (f32[3,32,512]{2,1,0:T(8,128)S(1)}, f32[3,32,512]{2,1,0:T(8,128)S(1)}, u32[]{:S(2)}, u32[]{:S(2)}) collective-permute-start(f32[3,32,512]{2,1,0:T(8,128)S(1)} %shard_map.59.refs_0_), channel_id=1, source_target_pairs={{0,8},{2,10},{4,12},{6,14},{8,0},{10,2},{12,4},{14,6},{16,24},{18,... | collective-permute-start | bytes 589832 | tf_op jit(solution)/shard_map/ppermute | solution.py:117
  37.8 0.0 collective-permute-done.refs_1_
  37.8 0.0 copy-done.3
  37.8 0.9 %shard_map.55 = (bf16[1536,256]{1,0:T(8,128)(2,1)S(1)}, bf16[1536,256]{1,0:T(8,128)(2,1)S(1)}) custom-call(s32[3]{0:T(128)S(1)} %copy-done.3, f32[1024,256]{1,0:T(8,128)S(1)} %copy-done.1, f32[1024,256]{1,0:T(8,128)S(1)} %collective-permute-done.refs_1_), custom_call_target="tpu_custom_call" | custom-call | flops 1572864 | bytes 3670028 | tf_op jit(solution)/shard_map/pallas_call | solution.py:19
  38.7 1.5 %collective-permute-start.11 = (f32[3,32,512]{2,1,0:T(8,128)S(1)}, f32[3,32,512]{2,1,0:T(8,128)S(1)}, u32[]{:S(2)}, u32[]{:S(2)}) collective-permute-start(f32[3,32,512]{2,1,0:T(8,128)S(1)} %shard_map.59.refs_0_), channel_id=1, source_target_pairs={{0,4},{2,6},{4,0},{6,2},{8,12},{10,14},{12,8},{14,10},{16,20},{18,... | collective-permute-start | bytes 589832 | tf_op jit(solution)/shard_map/ppermute | solution.py:117
  40.2 0.0 collective-permute-start.10
  40.2 0.4 collective-permute-done.1.other
  40.6 0.0 copy-start
  40.6 0.6 %shard_map.57.refs_0_ = f32[3,32,512]{2,1,0:T(8,128)S(1)} custom-call(s32[1,3]{1,0:T(1,128)S(1)} %copy-done.2, f32[3,32,512]{2,1,0:T(8,128)S(1)} %shard_map.56.mine, f32[3,32,512]{2,1,0:T(8,128)S(1)} %collective-permute-done.1.other, bf16[1536,256]{1,0:T(8,128)(2,1)S(1)} %get-tuple-element.7.refs_0_.right_high), custom_call_target="tpu_custom_call" | custom-call | bytes 1376268 | tf_op jit(solution)/shard_map/pallas_call | solution.py:19
  41.2 1.5 %collective-permute-start.3 = (f32[3,32,512]{2,1,0:T(8,128)S(1)}, f32[3,32,512]{2,1,0:T(8,128)S(1)}, u32[]{:S(2)}, u32[]{:S(2)}) collective-permute-start(f32[3,32,512]{2,1,0:T(8,128)S(1)} %shard_map.57.refs_0_), channel_id=1, source_target_pairs={{0,4},{2,6},{4,0},{6,2},{8,12},{10,14},{12,8},{14,10},{16,20},{18,... | collective-permute-start | bytes 589832 | tf_op jit(solution)/shard_map/ppermute | solution.py:117
  42.7 2.0 %collective-permute-done.13.refs_4_ = f32[3,32,512]{2,1,0:T(8,128)S(1)} collective-permute-done((f32[3,32,512]{2,1,0:T(8,128)S(1)}, f32[3,32,512]{2,1,0:T(8,128)S(1)}, u32[]{:S(2)}, u32[]{:S(2)}) %collective-permute-start.13) | collective-permute-done | bytes 196640 | tf_op jit(solution)/shard_map/ppermute | solution.py:117
  44.7 1.5 %collective-permute-start.15 = (f32[3,32,512]{2,1,0:T(8,128)S(1)}, f32[3,32,512]{2,1,0:T(8,128)S(1)}, u32[]{:S(2)}, u32[]{:S(2)}) collective-permute-start(f32[3,32,512]{2,1,0:T(8,128)S(1)} %collective-permute-done.13.refs_4_), channel_id=1, source_target_pairs={{0,4},{2,6},{4,0},{6,2},{8,12},{10,14},{12,8},{14,10},{16,20},{18,... | collective-permute-start | bytes 589832 | tf_op jit(solution)/shard_map/ppermute | solution.py:117
  46.2 0.0 collective-permute-start.5
  46.2 0.0 collective-permute-done.11.refs_2_
  46.2 0.0 collective-permute-start.14
  46.2 0.0 collective-permute-done.10.refs_1_
  46.2 0.5 collective-permute-start.12
  46.7 2.8 %collective-permute-done.3.refs_2_ = f32[3,32,512]{2,1,0:T(8,128)S(1)} collective-permute-done((f32[3,32,512]{2,1,0:T(8,128)S(1)}, f32[3,32,512]{2,1,0:T(8,128)S(1)}, u32[]{:S(2)}, u32[]{:S(2)}) %collective-permute-start.3) | collective-permute-done | bytes 196640 | tf_op jit(solution)/shard_map/ppermute | solution.py:117
  49.4 2.1 %collective-permute-start.7 = (f32[3,32,512]{2,1,0:T(8,128)S(1)}, f32[3,32,512]{2,1,0:T(8,128)S(1)}, u32[]{:S(2)}, u32[]{:S(2)}) collective-permute-start(f32[3,32,512]{2,1,0:T(8,128)S(1)} %collective-permute-done.3.refs_2_), channel_id=1, source_target_pairs={{0,8},{2,10},{4,12},{6,14},{8,0},{10,2},{12,4},{14,6},{16,24},{18,... | collective-permute-start | bytes 589832 | tf_op jit(solution)/shard_map/ppermute | solution.py:117
  51.6 1.5 %collective-permute-done.15.refs_6_ = f32[3,32,512]{2,1,0:T(8,128)S(1)} collective-permute-done((f32[3,32,512]{2,1,0:T(8,128)S(1)}, f32[3,32,512]{2,1,0:T(8,128)S(1)}, u32[]{:S(2)}, u32[]{:S(2)}) %collective-permute-start.15) | collective-permute-done | bytes 196640 | tf_op jit(solution)/shard_map/ppermute | solution.py:117
  53.1 0.0 collective-permute-start.16
  53.1 0.9 %collective-permute-done.5.refs_4_ = f32[3,32,512]{2,1,0:T(8,128)S(1)} collective-permute-done((f32[3,32,512]{2,1,0:T(8,128)S(1)}, f32[3,32,512]{2,1,0:T(8,128)S(1)}, u32[]{:S(2)}, u32[]{:S(2)}) %collective-permute-start.5) | collective-permute-done | bytes 196640 | tf_op jit(solution)/shard_map/ppermute | solution.py:117
  54.0 0.0 collective-permute-start.2
  54.0 0.0 collective-permute-done.14.refs_5_
  54.0 0.5 collective-permute-start.4
  54.5 0.0 collective-permute-done.12.refs_3_
  54.5 0.1 collective-permute-start.6
  54.5 2.3 %collective-permute-done.7.refs_6_ = f32[3,32,512]{2,1,0:T(8,128)S(1)} collective-permute-done((f32[3,32,512]{2,1,0:T(8,128)S(1)}, f32[3,32,512]{2,1,0:T(8,128)S(1)}, u32[]{:S(2)}, u32[]{:S(2)}) %collective-permute-start.7) | collective-permute-done | bytes 196640 | tf_op jit(solution)/shard_map/ppermute | solution.py:117
  56.9 0.0 collective-permute-start.8
  56.9 0.0 collective-permute-done.16.refs_7_
  56.9 0.0 copy-done
  56.9 1.0 %shard_map.60.refs_8_ = f32[256,256]{1,0:T(8,128)S(1)} custom-call(bf16[1536,256]{1,0:T(8,128)(2,1)S(1)} %get-tuple-element.7.refs_0_.right_high, bf16[1536,256]{1,0:T(8,128)(2,1)S(1)} %get-tuple-element.8.right_low, f32[512,256]{1,0:T(8,128)S(1)} %copy-done, f32[3,32,512]{2,1,0:T(8,128)S(1)} %shard_map.59.refs_0_, ...), custom_call_target="tpu_custom_call" | custom-call | flops 603979776 | bytes 3670016 | tf_op jit(solution)/shard_map/pallas_call | solution.py:158
  57.9 0.0 collective-permute-done.2.refs_1_
  57.9 0.0 collective-permute-done.6.refs_5_
  57.9 0.0 collective-permute-done.4.refs_3_
  57.9 0.4 collective-permute-done.8.refs_7_
  58.3 1.8 %shard_map.61 = f32[512,256]{1,0:T(8,128)} custom-call(bf16[1536,256]{1,0:T(8,128)(2,1)S(1)} %get-tuple-element.7.refs_0_.right_high, bf16[1536,256]{1,0:T(8,128)(2,1)S(1)} %get-tuple-element.8.right_low, f32[512,256]{1,0:T(8,128)S(1)} %copy-done, f32[3,32,512]{2,1,0:T(8,128)S(1)} %shard_map.57.refs_0_, f32[3,32,512]{2,1,0:T(8,128)S(1)} %collective-permute-done.2.refs_1_, ...), custom_call_target="tpu_custom_call" | custom-call | flops 603979776 | bytes 3932160 | tf_op jit(solution)/shard_map/pallas_call | solution.py:158
Async XLA Ops:
  0.0 5.4 %copy-start.1 = (f32[1024,256]{1,0:T(8,128)S(1)}, f32[1024,256]{1,0:T(8,128)}, u32[]{:S(2)}) copy-start(f32[1024,256]{1,0:T(8,128)} %refs_0_.1) | copy-start | bytes 3145732
  0.0 19.9 %copy-start.2 = (s32[1,3]{1,0:T(1,128)S(1)}, s32[1,3]{1,0:T(1,128)}, u32[]{:S(2)}) copy-start(s32[1,3]{1,0:T(1,128)} %owners.7) | copy-start | bytes 40
  0.0 19.9 %all-to-all-start = ((f32[8,64,512]{2,1,0:T(8,128)}), f32[8,64,512]{2,1,0:T(8,128)S(1)}, u32[]{:S(2)}, u32[]{:S(2)}) async-start(f32[8,64,512]{2,1,0:T(8,128)} %bitcast.1), calls=%async_computation | async-start | bytes 2097152 | tf_op jit(solution)/shard_map/all_to_all | solution.py:124
  5.4 32.4 %collective-permute-start = (f32[1024,256]{1,0:T(8,128)S(1)}, f32[1024,256]{1,0:T(8,128)S(1)}, u32[]{:S(2)}, u32[]{:S(2)}) collective-permute-start(f32[1024,256]{1,0:T(8,128)S(1)} %copy-done.1), channel_id=1, source_target_pairs={{1,0},{0,1},{3,2},{2,3},{5,4},{4,5},{7,6},{6,7},{9,8},{8,9},{11,10... | collective-permute-start | bytes 3145736 | tf_op jit(solution)/shard_map/ppermute | solution.py:121
  20.4 16.1 %collective-permute-start.9 = (f32[3,32,512]{2,1,0:T(8,128)S(1)}, f32[3,32,512]{2,1,0:T(8,128)S(1)}, u32[]{:S(2)}, u32[]{:S(2)}) collective-permute-start(f32[3,32,512]{2,1,0:T(8,128)S(1)} %shard_map.58.mine), channel_id=1, source_target_pairs={{0,16},{2,18},{4,20},{6,22},{8,24},{10,26},{12,28},{14,30},{16,0},... | collective-permute-start | bytes 589832 | tf_op jit(solution)/shard_map/ppermute | solution.py:117
  23.7 14.1 %copy-start.3 = (s32[3]{0:T(128)S(1)}, s32[3]{0:T(128)}, u32[]{:S(2)}) copy-start(s32[3]{0:T(128)} %offsets.1) | copy-start | bytes 40
  23.7 16.9 %collective-permute-start.1 = (f32[3,32,512]{2,1,0:T(8,128)S(1)}, f32[3,32,512]{2,1,0:T(8,128)S(1)}, u32[]{:S(2)}, u32[]{:S(2)}) collective-permute-start(f32[3,32,512]{2,1,0:T(8,128)S(1)} %shard_map.56.mine), channel_id=1, source_target_pairs={{0,16},{2,18},{4,20},{6,22},{8,24},{10,26},{12,28},{14,30},{16,0},... | collective-permute-start | bytes 589832 | tf_op jit(solution)/shard_map/ppermute | solution.py:117
  37.1 7.6 %collective-permute-start.13 = (f32[3,32,512]{2,1,0:T(8,128)S(1)}, f32[3,32,512]{2,1,0:T(8,128)S(1)}, u32[]{:S(2)}, u32[]{:S(2)}) collective-permute-start(f32[3,32,512]{2,1,0:T(8,128)S(1)} %shard_map.59.refs_0_), channel_id=1, source_target_pairs={{0,8},{2,10},{4,12},{6,14},{8,0},{10,2},{12,4},{14,6},{16,24},{18,... | collective-permute-start | bytes 589832 | tf_op jit(solution)/shard_map/ppermute | solution.py:117
  38.7 7.5 %collective-permute-start.11 = (f32[3,32,512]{2,1,0:T(8,128)S(1)}, f32[3,32,512]{2,1,0:T(8,128)S(1)}, u32[]{:S(2)}, u32[]{:S(2)}) collective-permute-start(f32[3,32,512]{2,1,0:T(8,128)S(1)} %shard_map.59.refs_0_), channel_id=1, source_target_pairs={{0,4},{2,6},{4,0},{6,2},{8,12},{10,14},{12,8},{14,10},{16,20},{18,... | collective-permute-start | bytes 589832 | tf_op jit(solution)/shard_map/ppermute | solution.py:117
  40.2 6.0 %collective-permute-start.10 = (f32[3,32,512]{2,1,0:T(8,128)S(1)}, f32[3,32,512]{2,1,0:T(8,128)S(1)}, u32[]{:S(2)}, u32[]{:S(2)}) collective-permute-start(f32[3,32,512]{2,1,0:T(8,128)S(1)} %shard_map.59.refs_0_), channel_id=1, source_target_pairs={{0,2},{2,0},{4,6},{6,4},{8,10},{10,8},{12,14},{14,12},{16,18},{18,... | collective-permute-start | bytes 589832 | tf_op jit(solution)/shard_map/ppermute | solution.py:117
  40.6 16.3 %copy-start = (f32[512,256]{1,0:T(8,128)S(1)}, f32[512,256]{1,0:T(8,128)}, u32[]{:S(2)}) copy-start(f32[512,256]{1,0:T(8,128)} %previous.3) | copy-start | bytes 1572868
  41.2 8.2 %collective-permute-start.3 = (f32[3,32,512]{2,1,0:T(8,128)S(1)}, f32[3,32,512]{2,1,0:T(8,128)S(1)}, u32[]{:S(2)}, u32[]{:S(2)}) collective-permute-start(f32[3,32,512]{2,1,0:T(8,128)S(1)} %shard_map.57.refs_0_), channel_id=1, source_target_pairs={{0,4},{2,6},{4,0},{6,2},{8,12},{10,14},{12,8},{14,10},{16,20},{18,... | collective-permute-start | bytes 589832 | tf_op jit(solution)/shard_map/ppermute | solution.py:117
  44.7 8.4 %collective-permute-start.15 = (f32[3,32,512]{2,1,0:T(8,128)S(1)}, f32[3,32,512]{2,1,0:T(8,128)S(1)}, u32[]{:S(2)}, u32[]{:S(2)}) collective-permute-start(f32[3,32,512]{2,1,0:T(8,128)S(1)} %collective-permute-done.13.refs_4_), channel_id=1, source_target_pairs={{0,4},{2,6},{4,0},{6,2},{8,12},{10,14},{12,8},{14,10},{16,20},{18,... | collective-permute-start | bytes 589832 | tf_op jit(solution)/shard_map/ppermute | solution.py:117
  46.2 7.8 %collective-permute-start.5 = (f32[3,32,512]{2,1,0:T(8,128)S(1)}, f32[3,32,512]{2,1,0:T(8,128)S(1)}, u32[]{:S(2)}, u32[]{:S(2)}) collective-permute-start(f32[3,32,512]{2,1,0:T(8,128)S(1)} %shard_map.57.refs_0_), channel_id=1, source_target_pairs={{0,8},{2,10},{4,12},{6,14},{8,0},{10,2},{12,4},{14,6},{16,24},{18,... | collective-permute-start | bytes 589832 | tf_op jit(solution)/shard_map/ppermute | solution.py:117
  46.2 7.8 %collective-permute-start.14 = (f32[3,32,512]{2,1,0:T(8,128)S(1)}, f32[3,32,512]{2,1,0:T(8,128)S(1)}, u32[]{:S(2)}, u32[]{:S(2)}) collective-permute-start(f32[3,32,512]{2,1,0:T(8,128)S(1)} %collective-permute-done.13.refs_4_), channel_id=1, source_target_pairs={{0,2},{2,0},{4,6},{6,4},{8,10},{10,8},{12,14},{14,12},{16,18},{18,... | collective-permute-start | bytes 589832 | tf_op jit(solution)/shard_map/ppermute | solution.py:117
  46.2 8.3 %collective-permute-start.12 = (f32[3,32,512]{2,1,0:T(8,128)S(1)}, f32[3,32,512]{2,1,0:T(8,128)S(1)}, u32[]{:S(2)}, u32[]{:S(2)}) collective-permute-start(f32[3,32,512]{2,1,0:T(8,128)S(1)} %collective-permute-done.11.refs_2_), channel_id=1, source_target_pairs={{0,2},{2,0},{4,6},{6,4},{8,10},{10,8},{12,14},{14,12},{16,18},{18,... | collective-permute-start | bytes 589832 | tf_op jit(solution)/shard_map/ppermute | solution.py:117
  49.4 7.4 %collective-permute-start.7 = (f32[3,32,512]{2,1,0:T(8,128)S(1)}, f32[3,32,512]{2,1,0:T(8,128)S(1)}, u32[]{:S(2)}, u32[]{:S(2)}) collective-permute-start(f32[3,32,512]{2,1,0:T(8,128)S(1)} %collective-permute-done.3.refs_2_), channel_id=1, source_target_pairs={{0,8},{2,10},{4,12},{6,14},{8,0},{10,2},{12,4},{14,6},{16,24},{18,... | collective-permute-start | bytes 589832 | tf_op jit(solution)/shard_map/ppermute | solution.py:117
  53.1 3.8 %collective-permute-start.16 = (f32[3,32,512]{2,1,0:T(8,128)S(1)}, f32[3,32,512]{2,1,0:T(8,128)S(1)}, u32[]{:S(2)}, u32[]{:S(2)}) collective-permute-start(f32[3,32,512]{2,1,0:T(8,128)S(1)} %collective-permute-done.15.refs_6_), channel_id=1, source_target_pairs={{0,2},{2,0},{4,6},{6,4},{8,10},{10,8},{12,14},{14,12},{16,18},{18,... | collective-permute-start | bytes 589832 | tf_op jit(solution)/shard_map/ppermute | solution.py:117
  54.0 3.9 %collective-permute-start.2 = (f32[3,32,512]{2,1,0:T(8,128)S(1)}, f32[3,32,512]{2,1,0:T(8,128)S(1)}, u32[]{:S(2)}, u32[]{:S(2)}) collective-permute-start(f32[3,32,512]{2,1,0:T(8,128)S(1)} %shard_map.57.refs_0_), channel_id=1, source_target_pairs={{0,2},{2,0},{4,6},{6,4},{8,10},{10,8},{12,14},{14,12},{16,18},{18,... | collective-permute-start | bytes 589832 | tf_op jit(solution)/shard_map/ppermute | solution.py:117
  54.0 4.0 %collective-permute-start.4 = (f32[3,32,512]{2,1,0:T(8,128)S(1)}, f32[3,32,512]{2,1,0:T(8,128)S(1)}, u32[]{:S(2)}, u32[]{:S(2)}) collective-permute-start(f32[3,32,512]{2,1,0:T(8,128)S(1)} %collective-permute-done.3.refs_2_), channel_id=1, source_target_pairs={{0,2},{2,0},{4,6},{6,4},{8,10},{10,8},{12,14},{14,12},{16,18},{18,... | collective-permute-start | bytes 589832 | tf_op jit(solution)/shard_map/ppermute | solution.py:117
  54.5 3.4 %collective-permute-start.6 = (f32[3,32,512]{2,1,0:T(8,128)S(1)}, f32[3,32,512]{2,1,0:T(8,128)S(1)}, u32[]{:S(2)}, u32[]{:S(2)}) collective-permute-start(f32[3,32,512]{2,1,0:T(8,128)S(1)} %collective-permute-done.5.refs_4_), channel_id=1, source_target_pairs={{0,2},{2,0},{4,6},{6,4},{8,10},{10,8},{12,14},{14,12},{16,18},{18,... | collective-permute-start | bytes 589832 | tf_op jit(solution)/shard_map/ppermute | solution.py:117
  56.9 1.4 %collective-permute-start.8 = (f32[3,32,512]{2,1,0:T(8,128)S(1)}, f32[3,32,512]{2,1,0:T(8,128)S(1)}, u32[]{:S(2)}, u32[]{:S(2)}) collective-permute-start(f32[3,32,512]{2,1,0:T(8,128)S(1)} %collective-permute-done.7.refs_6_), channel_id=1, source_target_pairs={{0,2},{2,0},{4,6},{6,4},{8,10},{10,8},{12,14},{14,12},{16,18},{18,... | collective-permute-start | bytes 589832 | tf_op jit(solution)/shard_map/ppermute | solution.py:117

commit v5 on v4

--- a/solution.py
+++ b/solution.py
@@ -36,15 +36,49 @@
     return jnp.dot(left, right, preferred_element_type=jnp.float32)
 
 
-def pick_kernel(group, part, owners, arrived, out):
-    chunk = out.shape[1]
-    for number in range(out.shape[0]):
-        out[number] = arrived[owners[0, number] % group, part * chunk:(part + 1) * chunk, :]
-
-
-def merge_kernel(group, owners, mine, other, *refs):
+def flag_kernel(group, few, owners, out):
+    count = owners.shape[1]
+    upper = jnp.int32(0)
+    for number in range(count):
+        upper += owners[0, number] // group
+    many = jnp.where(jnp.maximum(upper, count - upper) > few, 1, 0)
+    out[...] = jnp.full(out.shape, many, jnp.int32)
+
+
+def copy_kernel(array, wait, out):
+    out[...] = array[...]
+
+
+def pick_kernel(group, owners, arrived, *outs):
+    mine, packed, rest = outs[:PARTS], outs[PARTS:-1], outs[-1]
+    count, chunk, _ = mine[0].shape
+    few = packed[0].shape[0]
+    half = lax.axis_index("row") // group
+    before = jnp.int32(0)
+    for number in range(count):
+        owner = owners[0, number]
+        member = owner % group
+        here = owner // group == half
+        for part in range(PARTS):
+            rows = slice(part * chunk, (part + 1) * chunk)
+            mine[part][number] = arrived[member, rows, :]
+            for slot in range(number + 1):
+
+                @pl.when(here & (before == slot))
+                def _():
+                    if slot < few:
+                        packed[part][slot] = arrived[member, rows, :]
+                    else:
+                        rest[part, slot - few] = arrived[member, rows, :]
+
+        before = jnp.where(here, before + 1, before)
+
+
+def merge_kernel(group, part, owners, mine, other, rest, *refs):
     out = refs[-1]
+    few = other.shape[0]
     half = lax.axis_index("row") // group
+    before = jnp.int32(0)
     for number in range(out.shape[0]):
         here = owners[0, number] // group == half
 
@@ -52,26 +86,29 @@
         def _():
             out[number] = mine[number]
 
-        @pl.when(jnp.logical_not(here))
-        def _():
-            out[number] = other[number]
+        for slot in range(number + 1):
+
+            @pl.when(jnp.logical_not(here) & (before == slot))
+            def _():
+                out[number] = other[slot] if slot < few else rest[part, slot - few]
+
+        before = jnp.where(here, before, before + 1)
 
 
 def right_kernel(offsets, *refs):
-    rights, (right_high, right_low) = refs[:-2], refs[-2:]
+    sources, (right_high, right_low) = refs[:-2], refs[-2:]
     count = offsets.shape[0]
     width = right_high.shape[0] // count
-    blocks = rights[0].shape[0] // width
+    blocks = [ref.at[place:place + width] for ref in sources for place in range(0, ref.shape[0], width)]
     for number in range(count):
         lanes = slice(number * width, (number + 1) * width)
-        for step, ref in enumerate(rights):
-            for block in range(blocks):
-
-                @pl.when(offsets[number] == step * blocks + block)
-                def _():
-                    high, low = split(ref[block * width:(block + 1) * width, :])
-                    right_high[lanes, :] = high
-                    right_low[lanes, :] = low
+        for block, ref in enumerate(blocks):
+
+            @pl.when(offsets[number] == block)
+            def _():
+                high, low = split(ref[...])
+                right_high[lanes, :] = high
+                right_low[lanes, :] = low
 
 
 def multiply_kernel(part, right_high, right_low, previous, *refs):
@@ -124,25 +161,45 @@
     arrived = lax.all_to_all(
         own.reshape(group, PARTS * chunk, width), "row", 0, 0, axis_index_groups=groups, tiled=True
     )
-    mine = [
-        call(functools.partial(pick_kernel, group, part), piece, [SMEM, VMEM], (owners, arrived))
-        for part in range(PARTS)
-    ]
-
-    rights = [right] + [shift(right, distance) for distance in range(1, columns)]
+    few = (2 * count + 2) // 3
+    packed = jax.ShapeDtypeStruct((few, chunk, width), own.dtype)
+    extra = jax.ShapeDtypeStruct((PARTS, count - few, chunk, width), own.dtype)
+    picked = call(
+        functools.partial(pick_kernel, group),
+        (piece,) * PARTS + (packed,) * PARTS + (extra,),
+        [SMEM, VMEM],
+        (owners, arrived),
+    )
+    mine, sent = picked[:PARTS], picked[PARTS:-1]
+    others = [swap(array, group) for array in sent]
+
+    flags = call(
+        functools.partial(flag_kernel, group, few),
+        jax.ShapeDtypeStruct((8, 128), jnp.int32),
+        [SMEM],
+        (owners,),
+    )
+    distance = 1
+    while distance < columns:
+        flags = flags | shift(flags, distance)
+        distance *= 2
+    rest = lax.cond(flags[0, 0] == 0, lambda array: array, lambda array: swap(array, group), picked[-1])
+
+    given = call(copy_kernel, jax.ShapeDtypeStruct(right.shape, right.dtype), [VMEM, ANY], (right, flags))
+    sources = [right] + [shift(given, distance) for distance in range(1, columns)]
     terms = jax.ShapeDtypeStruct((count * width, right.shape[1]), jnp.bfloat16)
     right_terms = call(
-        right_kernel, (terms, terms), [SMEM] + [VMEM] * columns, (offsets, *rights), flops=4 * terms.size
+        right_kernel, (terms, terms), [SMEM] + [VMEM] * len(sources), (offsets, *sources), flops=4 * terms.size
     )
 
     results = []
     for part in range(PARTS):
         wait = right_terms[:1] if part == PARTS - 1 else ()
         merged = call(
-            functools.partial(merge_kernel, group),
+            functools.partial(merge_kernel, group, part),
             piece,
-            [SMEM, VMEM, VMEM] + [ANY] * len(wait),
-            (owners, mine[part], swap(mine[part], group), *wait),
+            [SMEM, VMEM, VMEM, VMEM] + [ANY] * len(wait),
+            (owners, mine[part], others[part], rest, *wait),
         )
         pieces = {0: merged}
         bits = [1 << b for b in range(1, group.bit_length() - 1)]

time: 60.3 us -> 56.6 us (0.939)
  waiting for transfers between devices: 35.6 us -> 28.1 us
  Pallas kernels: 6.03 us -> 7.92 us
  starting transfers between devices: 18.4 us -> 19.2 us
    ppermute x16, waiting for transfers between devices: 22.7 us -> 17.3 us  [swap(): return lax.ppermute(array, 'row', [(i, i ^ mask) for i in range(devices)])]
    all_to_all x1, waiting for transfers between devices: 12.9 us -> 7.63 us  [shards(): lax.all_to_all(own.reshape(group, PARTS * chunk, width), 'row', 0, 0, axi...]
    ppermute x1 -> x2, waiting for transfers between devices: 0.01 us -> 3.18 us  [shift(): return lax.ppermute(array, 'col', pairs)]
    pallas_call x5 -> x6, Pallas kernels: 3.23 us -> 5.12 us  [call(): pl.pallas_call(kernel, out_shape=out_shape, in_specs=in_specs, out_specs=...]
    ppermute x1 -> x2, starting transfers between devices: 1.56 us -> 3.05 us  [shift(): return lax.ppermute(array, 'col', pairs)]
    ppermute x16, starting transfers between devices: 11.4 us -> 10.8 us  [swap(): return lax.ppermute(array, 'row', [(i, i ^ mask) for i in range(devices)])]
  transfers between devices with their start and end apart: 18 -> 19, of which waited for: 9 -> 10; matrix products, arithmetic and copies ran while one was open for 0% -> 1% of each run, Pallas kernels for 7% -> 11%
where the time goes in v5:
time: 56.6 us; the launch traced here: 56.4 us
  waiting for transfers between devices  28.1 us (50%)
  starting transfers between devices  19.2 us (34%)
  Pallas kernels  7.92 us (14%)
  between operations  0.66 us (1%)
    ppermute x16, waiting for transfers between devices, swap(): return lax.ppermute(array, 'row', [(i, i ^ mask) for i in range(devices)])  17.3 us
    ppermute x16, starting transfers between devices, swap(): return lax.ppermute(array, 'row', [(i, i ^ mask) for i in range(devices)])  10.8 us
    all_to_all x1, waiting for transfers between devices, shards(): lax.all_to_all(own.reshape(group, PARTS * chunk, width), 'row', 0, 0, axi...  7.63 us
    all_to_all x1, starting transfers between devices, shards(): lax.all_to_all(own.reshape(group, PARTS * chunk, width), 'row', 0, 0, axi...  5.39 us
    pallas_call x6, Pallas kernels, call(): pl.pallas_call(kernel, out_shape=out_shape, in_specs=in_specs, out_specs=...  5.12 us
    ppermute x2, waiting for transfers between devices, shift(): return lax.ppermute(array, 'col', pairs)  3.18 us
    ppermute x2, starting transfers between devices, shift(): return lax.ppermute(array, 'col', pairs)  3.05 us
    pallas_call x2, Pallas kernels, shards(): pl.pallas_call(functools.partial(multiply_kernel, part), out_shape=out_sh...  2.8 us
  transfers between devices with their start and end apart: 19, of which 10 were waited for; matrix products, arithmetic and copies ran while one was open for 1% of the time, Pallas kernels for 11%

profile of v5, /device:TPU:0, one launch (start us, length us, event | category | flops | bytes accessed | tf_op | source)
XLA Modules:
  0.0 56.4 jit_solution(952168164045793724)
XLA Ops:
  0.0 0.0 copy-start.2
  0.0 0.0 copy-start
  0.0 5.4 %all-to-all-start = ((f32[8,64,512]{2,1,0:T(8,128)}), f32[8,64,512]{2,1,0:T(8,128)S(1)}, u32[]{:S(2)}, u32[]{:S(2)}) async-start(f32[8,64,512]{2,1,0:T(8,128)} %bitcast.2), calls=%async_computation | async-start | bytes 2097152 | tf_op jit(solution)/shard_map/all_to_all | solution.py:161
  5.4 0.0 copy-done.2
  5.4 0.6 shard_map.55
  6.0 1.6 %collective-permute-start.1 = (s32[8,128]{1,0:T(8,128)S(1)}, s32[8,128]{1,0:T(8,128)S(1)}, u32[]{:S(2)}, u32[]{:S(2)}) collective-permute-start(s32[8,128]{1,0:T(8,128)S(1)} %shard_map.55), channel_id=1, source_target_pairs={{1,0},{0,1},{3,2},{2,3},{5,4},{4,5},{7,6},{6,7},{9,8},{8,9},{11,10... | collective-permute-start | bytes 12296 | tf_op jit(solution)/shard_map/ppermute | solution.py:158
  7.5 2.1 %collective-permute-done.1 = s32[8,128]{1,0:T(8,128)S(1)} collective-permute-done((s32[8,128]{1,0:T(8,128)S(1)}, s32[8,128]{1,0:T(8,128)S(1)}, u32[]{:S(2)}, u32[]{:S(2)}) %collective-permute-start.1) | collective-permute-done | bytes 4128 | tf_op jit(solution)/shard_map/ppermute | solution.py:158
  9.6 0.0 copy-done
  9.6 1.1 %shard_map.56 = f32[1024,256]{1,0:T(8,128)} custom-call(f32[1024,256]{1,0:T(8,128)S(1)} %copy-done, s32[8,128]{1,0:T(8,128)S(1)} %or.3.wait), custom_call_target="tpu_custom_call" | custom-call | bytes 2101248 | tf_op jit(solution)/shard_map/pallas_call | solution.py:19
  10.7 1.5 %collective-permute-start.2 = (f32[1024,256]{1,0:T(8,128)}, f32[1024,256]{1,0:T(8,128)S(1)}, u32[]{:S(2)}, u32[]{:S(2)}) collective-permute-start(f32[1024,256]{1,0:T(8,128)} %shard_map.56), channel_id=1, source_target_pairs={{1,0},{0,1},{3,2},{2,3},{5,4},{4,5},{7,6},{6,7},{9,8},{8,9},{11,10... | collective-permute-start | bytes 3145736 | tf_op jit(solution)/shard_map/ppermute | solution.py:158
  12.2 7.6 %all-to-all-done.arrived = f32[8,64,512]{2,1,0:T(8,128)S(1)} async-done(((f32[8,64,512]{2,1,0:T(8,128)}), f32[8,64,512]{2,1,0:T(8,128)S(1)}, u32[]{:S(2)}, u32[]{:S(2)}) %all-to-all-start) | async-done | bytes 1048608 | tf_op jit(solution)/shard_map/all_to_all | solution.py:161
  19.9 1.3 %shard_map.58 = (f32[3,32,512]{2,1,0:T(8,128)S(1)}, f32[3,32,512]{2,1,0:T(8,128)S(1)}, f32[2,32,512]{2,1,0:T(8,128)}, f32[2,32,512]{2,1,0:T(8,128)}, f32[2,1,32,512]{3,2,1,0:T(8,128)S(1)}) custom-call(s32[1,3]{1,0:T(1,128)S(1)} %copy-done.2, f32[8,64,512]{2,1,0:T(8,128)S(1)} %all-to-all-done.arrived), custom_call_target="tpu_custom_call" | custom-call | bytes 1835020 | tf_op jit(solution)/shard_map/pallas_call | solution.py:19
  21.2 2.6 %collective-permute-start.11 = (f32[2,32,512]{2,1,0:T(8,128)}, f32[2,32,512]{2,1,0:T(8,128)S(1)}, u32[]{:S(2)}, u32[]{:S(2)}) collective-permute-start(f32[2,32,512]{2,1,0:T(8,128)} %get-tuple-element.23), channel_id=1, source_target_pairs={{0,16},{2,18},{4,20},{6,22},{8,24},{10,26},{12,28},{14,30},{16,0},... | collective-permute-start | bytes 393224 | tf_op jit(solution)/shard_map/ppermute | solution.py:154
  23.8 0.3 collective-permute-start.3
  24.1 0.5 slice.3
  25.2 8.0 %collective-permute-done.11.other = f32[2,32,512]{2,1,0:T(8,128)S(1)} collective-permute-done((f32[2,32,512]{2,1,0:T(8,128)}, f32[2,32,512]{2,1,0:T(8,128)S(1)}, u32[]{:S(2)}, u32[]{:S(2)}) %collective-permute-start.11) | collective-permute-done | bytes 131104 | tf_op jit(solution)/shard_map/ppermute | solution.py:154
  33.2 0.0 copy-start.3
  33.2 0.6 %shard_map.60.refs_0_ = f32[3,32,512]{2,1,0:T(8,128)S(1)} custom-call(s32[1,3]{1,0:T(1,128)S(1)} %copy-done.2, f32[3,32,512]{2,1,0:T(8,128)S(1)} %get-tuple-element.22.mine, f32[2,32,512]{2,1,0:T(8,128)S(1)} %collective-permute-done.11.other, f32[2,1,32,512]{3,2,1,0:T(8,128)S(1)} %get-tuple-element.24.rest), custom_call_target="tpu_custom_call" | custom-call | bytes 655372 | tf_op jit(solution)/shard_map/pallas_call | solution.py:19
  33.8 0.8 %collective-permute-start.15 = (f32[3,32,512]{2,1,0:T(8,128)S(1)}, f32[3,32,512]{2,1,0:T(8,128)S(1)}, u32[]{:S(2)}, u32[]{:S(2)}) collective-permute-start(f32[3,32,512]{2,1,0:T(8,128)S(1)} %shard_map.60.refs_0_), channel_id=1, source_target_pairs={{0,8},{2,10},{4,12},{6,14},{8,0},{10,2},{12,4},{14,6},{16,24},{18,... | collective-permute-start | bytes 589832 | tf_op jit(solution)/shard_map/ppermute | solution.py:154
  34.6 1.1 %collective-permute-done.2.refs_1_ = f32[1024,256]{1,0:T(8,128)S(1)} collective-permute-done((f32[1024,256]{1,0:T(8,128)}, f32[1024,256]{1,0:T(8,128)S(1)}, u32[]{:S(2)}, u32[]{:S(2)}) %collective-permute-start.2) | collective-permute-done | bytes 1048608 | tf_op jit(solution)/shard_map/ppermute | solution.py:158
  35.7 0.0 copy-done.3
  35.7 0.9 %shard_map.57 = (bf16[1536,256]{1,0:T(8,128)(2,1)S(1)}, bf16[1536,256]{1,0:T(8,128)(2,1)S(1)}) custom-call(s32[3]{0:T(128)S(1)} %copy-done.3, f32[1024,256]{1,0:T(8,128)S(1)} %copy-done, f32[1024,256]{1,0:T(8,128)S(1)} %collective-permute-done.2.refs_1_), custom_call_target="tpu_custom_call" | custom-call | flops 1572864 | bytes 3670028 | tf_op jit(solution)/shard_map/pallas_call | solution.py:19
  36.6 1.7 %collective-permute-start.13 = (f32[3,32,512]{2,1,0:T(8,128)S(1)}, f32[3,32,512]{2,1,0:T(8,128)S(1)}, u32[]{:S(2)}, u32[]{:S(2)}) collective-permute-start(f32[3,32,512]{2,1,0:T(8,128)S(1)} %shard_map.60.refs_0_), channel_id=1, source_target_pairs={{0,4},{2,6},{4,0},{6,2},{8,12},{10,14},{12,8},{14,10},{16,20},{18,... | collective-permute-start | bytes 589832 | tf_op jit(solution)/shard_map/ppermute | solution.py:154
  38.3 0.0 collective-permute-start.12
  38.3 0.0 collective-permute-done.3.other
  38.3 0.0 copy-start.1
  38.3 0.6 %shard_map.59.refs_0_ = f32[3,32,512]{2,1,0:T(8,128)S(1)} custom-call(s32[1,3]{1,0:T(1,128)S(1)} %copy-done.2, f32[3,32,512]{2,1,0:T(8,128)S(1)} %get-tuple-element.19.mine, f32[2,32,512]{2,1,0:T(8,128)S(1)} %collective-permute-done.3.other, f32[2,1,32,512]{3,2,1,0:T(8,128)S(1)} %get-tuple-element.24.rest, ...), custom_call_target="tpu_custom_call" | custom-call | bytes 1441804 | tf_op jit(solution)/shard_map/pallas_call | solution.py:19
  38.9 0.4 collective-permute-start.5
  39.4 1.0 %collective-permute-done.15.refs_4_ = f32[3,32,512]{2,1,0:T(8,128)S(1)} collective-permute-done((f32[3,32,512]{2,1,0:T(8,128)S(1)}, f32[3,32,512]{2,1,0:T(8,128)S(1)}, u32[]{:S(2)}, u32[]{:S(2)}) %collective-permute-start.15) | collective-permute-done | bytes 196640 | tf_op jit(solution)/shard_map/ppermute | solution.py:154
  40.3 1.6 %collective-permute-start.17 = (f32[3,32,512]{2,1,0:T(8,128)S(1)}, f32[3,32,512]{2,1,0:T(8,128)S(1)}, u32[]{:S(2)}, u32[]{:S(2)}) collective-permute-start(f32[3,32,512]{2,1,0:T(8,128)S(1)} %collective-permute-done.15.refs_4_), channel_id=1, source_target_pairs={{0,4},{2,6},{4,0},{6,2},{8,12},{10,14},{12,8},{14,10},{16,20},{18,... | collective-permute-start | bytes 589832 | tf_op jit(solution)/shard_map/ppermute | solution.py:154
  41.9 0.6 collective-permute-start.7
  42.5 0.5 collective-permute-done.13.refs_2_
  43.0 0.0 collective-permute-start.16
  43.0 0.0 collective-permute-done.12.refs_1_
  43.0 0.5 collective-permute-start.14
  43.6 3.7 %collective-permute-done.5.refs_2_ = f32[3,32,512]{2,1,0:T(8,128)S(1)} collective-permute-done((f32[3,32,512]{2,1,0:T(8,128)S(1)}, f32[3,32,512]{2,1,0:T(8,128)S(1)}, u32[]{:S(2)}, u32[]{:S(2)}) %collective-permute-start.5) | collective-permute-done | bytes 196640 | tf_op jit(solution)/shard_map/ppermute | solution.py:154
  47.3 1.3 %collective-permute-start.9 = (f32[3,32,512]{2,1,0:T(8,128)S(1)}, f32[3,32,512]{2,1,0:T(8,128)S(1)}, u32[]{:S(2)}, u32[]{:S(2)}) collective-permute-start(f32[3,32,512]{2,1,0:T(8,128)S(1)} %collective-permute-done.5.refs_2_), channel_id=1, source_target_pairs={{0,8},{2,10},{4,12},{6,14},{8,0},{10,2},{12,4},{14,6},{16,24},{18,... | collective-permute-start | bytes 589832 | tf_op jit(solution)/shard_map/ppermute | solution.py:154
  48.5 2.2 %collective-permute-done.17.refs_6_ = f32[3,32,512]{2,1,0:T(8,128)S(1)} collective-permute-done((f32[3,32,512]{2,1,0:T(8,128)S(1)}, f32[3,32,512]{2,1,0:T(8,128)S(1)}, u32[]{:S(2)}, u32[]{:S(2)}) %collective-permute-start.17) | collective-permute-done | bytes 196640 | tf_op jit(solution)/shard_map/ppermute | solution.py:154
  50.7 0.0 collective-permute-start.18
  50.7 0.0 collective-permute-done.7.refs_4_
  50.7 0.5 collective-permute-start.4
  51.2 0.0 collective-permute-done.16.refs_5_
  51.2 0.1 collective-permute-start.6
  51.3 0.0 collective-permute-done.14.refs_3_
  51.3 0.4 collective-permute-start.8
  51.8 1.4 %collective-permute-done.9.refs_6_ = f32[3,32,512]{2,1,0:T(8,128)S(1)} collective-permute-done((f32[3,32,512]{2,1,0:T(8,128)S(1)}, f32[3,32,512]{2,1,0:T(8,128)S(1)}, u32[]{:S(2)}, u32[]{:S(2)}) %collective-permute-start.9) | collective-permute-done | bytes 196640 | tf_op jit(solution)/shard_map/ppermute | solution.py:154
  53.2 0.0 collective-permute-start.10
  53.2 0.0 collective-permute-done.18.refs_7_
  53.2 0.0 copy-done.1
  53.2 1.0 %shard_map.61.refs_8_ = f32[256,256]{1,0:T(8,128)S(1)} custom-call(bf16[1536,256]{1,0:T(8,128)(2,1)S(1)} %get-tuple-element.17.refs_0_.right_high, bf16[1536,256]{1,0:T(8,128)(2,1)S(1)} %get-tuple-element.18.right_low, f32[512,256]{1,0:T(8,128)S(1)} %copy-done.1, f32[3,32,512]{2,1,0:T(8,128)S(1)} %shard_map.60.refs_0_, ...), custom_call_target="tpu_custom_call" | custom-call | flops 603979776 | bytes 3670016 | tf_op jit(solution)/shard_map/pallas_call | solution.py:215
  54.2 0.0 collective-permute-done.4.refs_1_
  54.2 0.0 collective-permute-done.8.refs_5_
  54.2 0.0 collective-permute-done.6.refs_3_
  54.2 0.4 collective-permute-done.10.refs_7_
  54.6 1.8 %shard_map.62 = f32[512,256]{1,0:T(8,128)} custom-call(bf16[1536,256]{1,0:T(8,128)(2,1)S(1)} %get-tuple-element.17.refs_0_.right_high, bf16[1536,256]{1,0:T(8,128)(2,1)S(1)} %get-tuple-element.18.right_low, f32[512,256]{1,0:T(8,128)S(1)} %copy-done.1, f32[3,32,512]{2,1,0:T(8,128)S(1)} %shard_map.59.refs_0_, ...), custom_call_target="tpu_custom_call" | custom-call | flops 603979776 | bytes 3932160 | tf_op jit(solution)/shard_map/pallas_call | solution.py:215
  (3 shorter events, 0.0 us)
Async XLA Ops:
  0.0 5.4 %copy-start.2 = (s32[1,3]{1,0:T(1,128)S(1)}, s32[1,3]{1,0:T(1,128)}, u32[]{:S(2)}) copy-start(s32[1,3]{1,0:T(1,128)} %owners.7) | copy-start | bytes 40
  0.0 9.6 %copy-start = (f32[1024,256]{1,0:T(8,128)S(1)}, f32[1024,256]{1,0:T(8,128)}, u32[]{:S(2)}) copy-start(f32[1024,256]{1,0:T(8,128)} %refs_0_.1) | copy-start | bytes 3145732
  0.0 19.9 %all-to-all-start = ((f32[8,64,512]{2,1,0:T(8,128)}), f32[8,64,512]{2,1,0:T(8,128)S(1)}, u32[]{:S(2)}, u32[]{:S(2)}) async-start(f32[8,64,512]{2,1,0:T(8,128)} %bitcast.2), calls=%async_computation | async-start | bytes 2097152 | tf_op jit(solution)/shard_map/all_to_all | solution.py:161
  6.0 3.7 %collective-permute-start.1 = (s32[8,128]{1,0:T(8,128)S(1)}, s32[8,128]{1,0:T(8,128)S(1)}, u32[]{:S(2)}, u32[]{:S(2)}) collective-permute-start(s32[8,128]{1,0:T(8,128)S(1)} %shard_map.55), channel_id=1, source_target_pairs={{1,0},{0,1},{3,2},{2,3},{5,4},{4,5},{7,6},{6,7},{9,8},{8,9},{11,10... | collective-permute-start | bytes 12296 | tf_op jit(solution)/shard_map/ppermute | solution.py:158
  10.7 24.9 %collective-permute-start.2 = (f32[1024,256]{1,0:T(8,128)}, f32[1024,256]{1,0:T(8,128)S(1)}, u32[]{:S(2)}, u32[]{:S(2)}) collective-permute-start(f32[1024,256]{1,0:T(8,128)} %shard_map.56), channel_id=1, source_target_pairs={{1,0},{0,1},{3,2},{2,3},{5,4},{4,5},{7,6},{6,7},{9,8},{8,9},{11,10... | collective-permute-start | bytes 3145736 | tf_op jit(solution)/shard_map/ppermute | solution.py:158
  21.2 12.0 %collective-permute-start.11 = (f32[2,32,512]{2,1,0:T(8,128)}, f32[2,32,512]{2,1,0:T(8,128)S(1)}, u32[]{:S(2)}, u32[]{:S(2)}) collective-permute-start(f32[2,32,512]{2,1,0:T(8,128)} %get-tuple-element.23), channel_id=1, source_target_pairs={{0,16},{2,18},{4,20},{6,22},{8,24},{10,26},{12,28},{14,30},{16,0},... | collective-permute-start | bytes 393224 | tf_op jit(solution)/shard_map/ppermute | solution.py:154
  23.8 14.5 %collective-permute-start.3 = (f32[2,32,512]{2,1,0:T(8,128)}, f32[2,32,512]{2,1,0:T(8,128)S(1)}, u32[]{:S(2)}, u32[]{:S(2)}) collective-permute-start(f32[2,32,512]{2,1,0:T(8,128)} %get-tuple-element.20), channel_id=1, source_target_pairs={{0,16},{2,18},{4,20},{6,22},{8,24},{10,26},{12,28},{14,30},{16,0},... | collective-permute-start | bytes 393224 | tf_op jit(solution)/shard_map/ppermute | solution.py:154
  33.2 2.5 %copy-start.3 = (s32[3]{0:T(128)S(1)}, s32[3]{0:T(128)}, u32[]{:S(2)}) copy-start(s32[3]{0:T(128)} %offsets.1) | copy-start | bytes 40
  33.8 6.5 %collective-permute-start.15 = (f32[3,32,512]{2,1,0:T(8,128)S(1)}, f32[3,32,512]{2,1,0:T(8,128)S(1)}, u32[]{:S(2)}, u32[]{:S(2)}) collective-permute-start(f32[3,32,512]{2,1,0:T(8,128)S(1)} %shard_map.60.refs_0_), channel_id=1, source_target_pairs={{0,8},{2,10},{4,12},{6,14},{8,0},{10,2},{12,4},{14,6},{16,24},{18,... | collective-permute-start | bytes 589832 | tf_op jit(solution)/shard_map/ppermute | solution.py:154
  36.6 6.5 %collective-permute-start.13 = (f32[3,32,512]{2,1,0:T(8,128)S(1)}, f32[3,32,512]{2,1,0:T(8,128)S(1)}, u32[]{:S(2)}, u32[]{:S(2)}) collective-permute-start(f32[3,32,512]{2,1,0:T(8,128)S(1)} %shard_map.60.refs_0_), channel_id=1, source_target_pairs={{0,4},{2,6},{4,0},{6,2},{8,12},{10,14},{12,8},{14,10},{16,20},{18,... | collective-permute-start | bytes 589832 | tf_op jit(solution)/shard_map/ppermute | solution.py:154
  38.3 4.8 %collective-permute-start.12 = (f32[3,32,512]{2,1,0:T(8,128)S(1)}, f32[3,32,512]{2,1,0:T(8,128)S(1)}, u32[]{:S(2)}, u32[]{:S(2)}) collective-permute-start(f32[3,32,512]{2,1,0:T(8,128)S(1)} %shard_map.60.refs_0_), channel_id=1, source_target_pairs={{0,2},{2,0},{4,6},{6,4},{8,10},{10,8},{12,14},{14,12},{16,18},{18,... | collective-permute-start | bytes 589832 | tf_op jit(solution)/shard_map/ppermute | solution.py:154
  38.3 14.9 %copy-start.1 = (f32[512,256]{1,0:T(8,128)S(1)}, f32[512,256]{1,0:T(8,128)}, u32[]{:S(2)}) copy-start(f32[512,256]{1,0:T(8,128)} %previous.3) | copy-start | bytes 1572868
  38.9 8.3 %collective-permute-start.5 = (f32[3,32,512]{2,1,0:T(8,128)S(1)}, f32[3,32,512]{2,1,0:T(8,128)S(1)}, u32[]{:S(2)}, u32[]{:S(2)}) collective-permute-start(f32[3,32,512]{2,1,0:T(8,128)S(1)} %shard_map.59.refs_0_), channel_id=1, source_target_pairs={{0,4},{2,6},{4,0},{6,2},{8,12},{10,14},{12,8},{14,10},{16,20},{18,... | collective-permute-start | bytes 589832 | tf_op jit(solution)/shard_map/ppermute | solution.py:154
  40.3 10.4 %collective-permute-start.17 = (f32[3,32,512]{2,1,0:T(8,128)S(1)}, f32[3,32,512]{2,1,0:T(8,128)S(1)}, u32[]{:S(2)}, u32[]{:S(2)}) collective-permute-start(f32[3,32,512]{2,1,0:T(8,128)S(1)} %collective-permute-done.15.refs_4_), channel_id=1, source_target_pairs={{0,4},{2,6},{4,0},{6,2},{8,12},{10,14},{12,8},{14,10},{16,20},{18,... | collective-permute-start | bytes 589832 | tf_op jit(solution)/shard_map/ppermute | solution.py:154
  41.9 8.8 %collective-permute-start.7 = (f32[3,32,512]{2,1,0:T(8,128)S(1)}, f32[3,32,512]{2,1,0:T(8,128)S(1)}, u32[]{:S(2)}, u32[]{:S(2)}) collective-permute-start(f32[3,32,512]{2,1,0:T(8,128)S(1)} %shard_map.59.refs_0_), channel_id=1, source_target_pairs={{0,8},{2,10},{4,12},{6,14},{8,0},{10,2},{12,4},{14,6},{16,24},{18,... | collective-permute-start | bytes 589832 | tf_op jit(solution)/shard_map/ppermute | solution.py:154
  43.0 8.2 %collective-permute-start.16 = (f32[3,32,512]{2,1,0:T(8,128)S(1)}, f32[3,32,512]{2,1,0:T(8,128)S(1)}, u32[]{:S(2)}, u32[]{:S(2)}) collective-permute-start(f32[3,32,512]{2,1,0:T(8,128)S(1)} %collective-permute-done.15.refs_4_), channel_id=1, source_target_pairs={{0,2},{2,0},{4,6},{6,4},{8,10},{10,8},{12,14},{14,12},{16,18},{18,... | collective-permute-start | bytes 589832 | tf_op jit(solution)/shard_map/ppermute | solution.py:154
  43.0 8.3 %collective-permute-start.14 = (f32[3,32,512]{2,1,0:T(8,128)S(1)}, f32[3,32,512]{2,1,0:T(8,128)S(1)}, u32[]{:S(2)}, u32[]{:S(2)}) collective-permute-start(f32[3,32,512]{2,1,0:T(8,128)S(1)} %collective-permute-done.13.refs_2_), channel_id=1, source_target_pairs={{0,2},{2,0},{4,6},{6,4},{8,10},{10,8},{12,14},{14,12},{16,18},{18,... | collective-permute-start | bytes 589832 | tf_op jit(solution)/shard_map/ppermute | solution.py:154
  47.3 5.9 %collective-permute-start.9 = (f32[3,32,512]{2,1,0:T(8,128)S(1)}, f32[3,32,512]{2,1,0:T(8,128)S(1)}, u32[]{:S(2)}, u32[]{:S(2)}) collective-permute-start(f32[3,32,512]{2,1,0:T(8,128)S(1)} %collective-permute-done.5.refs_2_), channel_id=1, source_target_pairs={{0,8},{2,10},{4,12},{6,14},{8,0},{10,2},{12,4},{14,6},{16,24},{18,... | collective-permute-start | bytes 589832 | tf_op jit(solution)/shard_map/ppermute | solution.py:154
  50.7 2.4 %collective-permute-start.18 = (f32[3,32,512]{2,1,0:T(8,128)S(1)}, f32[3,32,512]{2,1,0:T(8,128)S(1)}, u32[]{:S(2)}, u32[]{:S(2)}) collective-permute-start(f32[3,32,512]{2,1,0:T(8,128)S(1)} %collective-permute-done.17.refs_6_), channel_id=1, source_target_pairs={{0,2},{2,0},{4,6},{6,4},{8,10},{10,8},{12,14},{14,12},{16,18},{18,... | collective-permute-start | bytes 589832 | tf_op jit(solution)/shard_map/ppermute | solution.py:154
  50.7 3.5 %collective-permute-start.4 = (f32[3,32,512]{2,1,0:T(8,128)S(1)}, f32[3,32,512]{2,1,0:T(8,128)S(1)}, u32[]{:S(2)}, u32[]{:S(2)}) collective-permute-start(f32[3,32,512]{2,1,0:T(8,128)S(1)} %shard_map.59.refs_0_), channel_id=1, source_target_pairs={{0,2},{2,0},{4,6},{6,4},{8,10},{10,8},{12,14},{14,12},{16,18},{18,... | collective-permute-start | bytes 589832 | tf_op jit(solution)/shard_map/ppermute | solution.py:154
  51.2 3.0 %collective-permute-start.6 = (f32[3,32,512]{2,1,0:T(8,128)S(1)}, f32[3,32,512]{2,1,0:T(8,128)S(1)}, u32[]{:S(2)}, u32[]{:S(2)}) collective-permute-start(f32[3,32,512]{2,1,0:T(8,128)S(1)} %collective-permute-done.5.refs_2_), channel_id=1, source_target_pairs={{0,2},{2,0},{4,6},{6,4},{8,10},{10,8},{12,14},{14,12},{16,18},{18,... | collective-permute-start | bytes 589832 | tf_op jit(solution)/shard_map/ppermute | solution.py:154
  51.3 2.9 %collective-permute-start.8 = (f32[3,32,512]{2,1,0:T(8,128)S(1)}, f32[3,32,512]{2,1,0:T(8,128)S(1)}, u32[]{:S(2)}, u32[]{:S(2)}) collective-permute-start(f32[3,32,512]{2,1,0:T(8,128)S(1)} %collective-permute-done.7.refs_4_), channel_id=1, source_target_pairs={{0,2},{2,0},{4,6},{6,4},{8,10},{10,8},{12,14},{14,12},{16,18},{18,... | collective-permute-start | bytes 589832 | tf_op jit(solution)/shard_map/ppermute | solution.py:154
  53.2 1.4 %collective-permute-start.10 = (f32[3,32,512]{2,1,0:T(8,128)S(1)}, f32[3,32,512]{2,1,0:T(8,128)S(1)}, u32[]{:S(2)}, u32[]{:S(2)}) collective-permute-start(f32[3,32,512]{2,1,0:T(8,128)S(1)} %collective-permute-done.9.refs_6_), channel_id=1, source_target_pairs={{0,2},{2,0},{4,6},{6,4},{8,10},{10,8},{12,14},{14,12},{16,18},{18,... | collective-permute-start | bytes 589832 | tf_op jit(solution)/shard_map/ppermute | solution.py:154
